TPU v7x, 1024 devices: a whole 8x8x8 slice. The times are simulated.
1024 devices in a mesh: dp: 16 (over z, core), expert: 64 (over x, y).
Axes of the slice: x: 8, y: 8, z: 8, core: 2. Of those that a mesh axis runs over, the one named last changes fastest.
Arguments:
- expert_ids: int32 [16384, 8], P(('dp', 'expert')), may hold values from 0 to 63, all different within a row; in each aligned block of 16 rows (0 to 15, 16 to 31, ...) at most 3 rows name the same one
- grad_hidden: bfloat16 [16384, 8, 768], P(('dp', 'expert')), may hold values from -1.796875 to 1.796875
- stored_inputs: bfloat16 [16, 64, 64, 3, 2048], P('dp', 'expert'), may hold values from -6 to 6
- gate_weight: bfloat16 [64, 2048, 768], P('expert'), may hold values from -0.125 to 0.125
- up_weight: bfloat16 [64, 2048, 768], P('expert'), may hold values from -0.125 to 0.125
Outputs:
- grad_tokens: bfloat16 [16384, 2048], P(('dp', 'expert'))
- grad_gate: float32 [64, 2048, 768], P('expert', 'dp')
Inputs may be any that keep to these rules, and one draw needn't show every extreme that they name: `expert_ids`: among the 16 tokens of one device no expert is named more than 3 times, and in every draw some device names some expert exactly 3 times; a token names 8 different experts.
All inputs are finite; a program needn't handle non-finite values.
Results may differ from a plain program's by a relative error of at most 0.02.
Values may be sent and summed in bfloat16 or wider, within the bound.
No kernel may reach another device: no remote copies, remote signals or barrier semaphores. Data moves between devices by JAX's collectives and lax.ppermute only.
A program may use at most 64 MiB of HBM per device.

v0:
```python
import jax
import jax.numpy as jnp
from jax import lax
from jax.sharding import PartitionSpec as P


def on_device(expert_ids, grad_hidden, stored_inputs, gate_weight, up_weight):
    peers = lax.axis_size("expert")
    capacity = stored_inputs.shape[3]
    width = stored_inputs.shape[4]
    hidden = gate_weight.shape[2]
    tok_rows = expert_ids.shape[0]
    picks = expert_ids.shape[1]
    routed = tok_rows * picks
    slot_rows = peers * capacity
    flat_ids = expert_ids.reshape(routed)
    onehot = (flat_ids[:, None] == jnp.arange(peers, dtype=jnp.int32)[None, :]).astype(jnp.int32)
    rank = jnp.cumsum(onehot, axis=0) - onehot
    slot = jnp.sum(rank * onehot, axis=1)
    outgoing = jnp.zeros((peers, capacity, hidden), jnp.bfloat16)
    outgoing = outgoing.at[flat_ids, slot].set(grad_hidden.reshape(routed, hidden))
    arrived = lax.all_to_all(outgoing, "expert", split_axis=0, concat_axis=0, tiled=True)
    inputs = stored_inputs.reshape(slot_rows, width)
    dh_rows = arrived.reshape(slot_rows, hidden)
    w_gate = gate_weight[0]
    w_up = up_weight[0]
    gate = jnp.dot(inputs, w_gate, preferred_element_type=jnp.float32)
    upper = jnp.dot(inputs, w_up, preferred_element_type=jnp.float32)
    sig = jax.nn.sigmoid(gate)
    dh_wide = dh_rows.astype(jnp.float32)
    dgate = (dh_wide * upper * sig * (1.0 + gate * (1.0 - sig))).astype(jnp.bfloat16)
    dupper = (dh_wide * gate * sig).astype(jnp.bfloat16)
    dims = (((1,), (1,)), ((), ()))
    back = lax.dot_general(dgate, w_gate, dims, preferred_element_type=jnp.float32)
    back = back + lax.dot_general(dupper, w_up, dims, preferred_element_type=jnp.float32)
    back = back.astype(jnp.bfloat16).reshape(peers, capacity, width)
    returned = lax.all_to_all(back, "expert", split_axis=0, concat_axis=0, tiled=True)
    picked = returned[flat_ids, slot]
    grad_tokens = jnp.sum(picked.astype(jnp.float32).reshape(tok_rows, picks, width), axis=1)
    grad_tokens = grad_tokens.astype(jnp.bfloat16)
    row_dims = (((0,), (0,)), ((), ()))
    full = lax.dot_general(inputs, dgate, row_dims, preferred_element_type=jnp.float32)
    mine = lax.psum_scatter(
        full.astype(jnp.bfloat16), "dp", scatter_dimension=0, tiled=True
    ).astype(jnp.float32)
    grad_gate = mine[None]
    return (grad_tokens, grad_gate)


def solution(mesh):
    return jax.shard_map(
        on_device,
        mesh=mesh,
        in_specs=(
            P(("dp", "expert"), None),
            P(("dp", "expert"), None, None),
            P("dp", "expert", None, None, None),
            P("expert", None, None),
            P("expert", None, None),
        ),
        out_specs=(P(("dp", "expert"), None), P("expert", "dp", None)),
        check_vma=False,
    )
```

profile of v0, /device:TPU:6, one launch (start us, length us, event | category | flops | bytes accessed | tf_op | source)
XLA Modules:
  0.0 146.7 jit_solution(5909313949865819036)
XLA Ops:
  7.2 0.0 copy-start
  7.2 0.9 copy.18
  8.1 0.1 eq.15
  8.2 0.1 reshape.63
  8.3 0.1 fusion.28
  8.4 0.2 reduce_window_sum.11
  8.5 0.2 select_reduce_fusion
  8.8 12.4 %scatter_fusion = bf16[64,3,768]{2,0,1:T(8,128)(2,1)S(1)} fusion(bf16[64,3,768]{2,0,1:T(8,128)(2,1)S(1)} %broadcast_in_dim.14, s32[128]{0:T(128)S(1)} %get-tuple-element.8, bf16[128,768]{1,0:T(8,128)(2,1)} %bitcast.48), kind=kCustom, calls=%fused_computation.1 | custom fusion | bytes 590848 | tf_op jit(solution)/shard_map/scatter | solution.py:21
  21.2 1.0 copy.20
  22.2 17.3 %all-to-all-start = ((bf16[64,3,768]{2,1,0:T(4,128)(2,1)}), bf16[64,3,768]{2,1,0:T(4,128)(2,1)S(1)}, u32[]{:S(2)}, u32[]{:S(2)}) async-start(bf16[64,3,768]{2,1,0:T(4,128)(2,1)} %copy.20), calls=%async_computation | async-start | bytes 786432 | tf_op jit(solution)/shard_map/all_to_all | solution.py:22
  39.5 0.0 reduce-scatter.4.cloned.1.call-start
  39.6 2.8 %copy.21 = bf16[1,1,64,3,2048]{4,3,2,1,0:T(4,128)(2,1)} copy(bf16[1,1,64,3,2048]{4,2,3,1,0:T(8,128)(2,1)} %param.7) | data formatting | bytes 1572864 | tf_op args[2]
  42.4 3.2 %reshape.65 = bf16[192,2048]{1,0:T(8,128)(2,1)} reshape(bf16[1,1,64,3,2048]{4,3,2,1,0:T(4,128)(2,1)} %copy.21) | data formatting | bytes 1572864 | tf_op jit(solution)/shard_map/reshape | solution.py:23
  45.6 0.0 copy-done
  45.6 2.7 %fusion.2 = f32[192,768]{1,0:T(8,128)} fusion(bf16[192,2048]{1,0:T(8,128)(2,1)} %reshape.65, bf16[1,2048,768]{2,1,0:T(8,128)(2,1)S(1)} %copy-done), kind=kOutput, calls=%fused_computation.5 | convolution fusion | flops 603979776 | bytes 4521984 | tf_op jit(solution)/shard_map/dot_general | solution.py:27
  48.3 4.1 %all-to-all-done = bf16[64,3,768]{2,1,0:T(4,128)(2,1)S(1)} async-done(((bf16[64,3,768]{2,1,0:T(4,128)(2,1)}), bf16[64,3,768]{2,1,0:T(4,128)(2,1)S(1)}, u32[]{:S(2)}, u32[]{:S(2)}) %all-to-all-start) | async-done | bytes 294944 | tf_op jit(solution)/shard_map/all_to_all | solution.py:22
  52.4 1.0 reshape.67
  53.5 0.0 copy-start.1
  53.5 3.3 %fusion.24 = bf16[192,768]{1,0:T(8,128)(2,1)S(1)} fusion(f32[192,768]{1,0:T(8,128)} %reshape.67, bf16[192,2048]{1,0:T(8,128)(2,1)} %reshape.65, bf16[1,2048,768]{2,1,0:T(8,128)(2,1)} %param.9, f32[192,768]{1,0:T(8,128)} %fusion.2), kind=kOutput, calls=%fused_computation.17 | convolution fusion | flops 605454336 | bytes 5406720 | tf_op jit(solution)/shard_map/dot_general | solution.py:28
  56.8 0.0 copy-done.1
  56.8 2.7 %fusion.8 = bf16[2048,768]{0,1:T(8,128)(2,1)} fusion(bf16[192,768]{1,0:T(8,128)(2,1)S(1)} %fusion.24, bf16[192,2048]{1,0:T(8,128)(2,1)S(1)} %copy-done.1), kind=kOutput, calls=%fused_computation.11 | convolution fusion | flops 605552640 | bytes 4227072 | tf_op jit(solution)/shard_map/dot_general | solution.py:42
  59.6 4.6 %copy.24 = bf16[2048,768]{1,0:T(8,128)(2,1)} copy(bf16[2048,768]{0,1:T(8,128)(2,1)} %fusion.8) | data formatting | bytes 6291456
  64.2 0.0 reduce-scatter.4.cloned.1.call-update
  64.2 0.0 copy-start.2
  64.2 0.0 copy-start.3
  64.2 0.0 copy-start.4
  64.3 1.2 fusion
  65.4 0.7 copy-done.2
  66.1 0.1 copy-done.3
  66.2 0.2 copy-done.4
  66.4 2.1 %fusion.12 = bf16[192,2048]{1,0:T(8,128)(2,1)} fusion(f32[192,2048]{1,0:T(8,128)S(1)} %fusion, bf16[1,2048,768]{2,1,0:T(8,128)(2,1)S(1)} %copy-done.2, f32[192,768]{1,0:T(8,128)S(1)} %copy-done.4, f32[192,768]{1,0:T(8,128)S(1)} %copy-done.3), kind=kOutput, calls=%fused_computation.13 | convolution fusion | flops 605650944 | bytes 6684672 | tf_op jit(solution)/shard_map/dot_general | solution.py:35
  68.5 3.3 %reshape.66 = bf16[64,3,2048]{2,1,0:T(4,128)(2,1)} reshape(bf16[192,2048]{1,0:T(8,128)(2,1)} %fusion.12) | data formatting | bytes 1572864 | tf_op jit(solution)/shard_map/reshape | solution.py:36
  71.8 33.9 %all_to_all.10 = bf16[64,3,2048]{2,1,0:T(4,128)(2,1)S(1)} all-to-all(bf16[64,3,2048]{2,1,0:T(4,128)(2,1)} %reshape.66), channel_id=1, replica_groups=mesh['dp'=16,'expert'=64] {'expert'}, dimensions={0} | all-to-all | bytes 1572864 | tf_op jit(solution)/shard_map/all_to_all | solution.py:37
  105.7 1.5 copy.22
  107.1 3.5 %gather_fusion = bf16[128,2048]{1,0:T(8,128)(2,1)} fusion(bf16[64,3,2048]{2,0,1:T(8,128)(2,1)} %copy.22, s32[128]{0:T(128)S(1)} %bitcast.47), kind=kCustom, calls=%fused_computation | custom fusion | bytes 1049600 | tf_op jit(solution)/shard_map/gather | solution.py:38
  110.7 2.0 %bitcast_reduce_fusion = bf16[16,2048]{1,0:T(8,128)(2,1)} fusion(bf16[128,2048]{1,0:T(8,128)(2,1)} %gather_fusion), kind=kLoop, calls=%fused_computation.20 | loop fusion | flops 229376 | bytes 589824 | tf_op jit(solution)/shard_map/reduce_sum | solution.py:39
  112.7 23.6 %reduce-scatter.4.cloned.1.call-done = bf16[128,768]{1,0:T(8,128)(2,1)} async-done(((bf16[2048,768]{1,0:T(8,128)(2,1)}), bf16[128,768]{1,0:T(8,128)(2,1)}) %reduce-scatter.4.cloned.1.call-update) | async-done | bytes 196624
  136.2 1.7 %copy.25 = bf16[128,768]{0,1:T(8,128)(2,1)} copy(bf16[128,768]{1,0:T(8,128)(2,1)} %reduce-scatter.4.cloned.1.call-done) | data formatting | bytes 393216
  138.0 1.0 bitcast_convert_fusion
  138.9 0.9 copy.23
  (2 shorter events, 0.0 us)
Async XLA Ops:
  7.2 38.4 %copy-start = (bf16[1,2048,768]{2,1,0:T(8,128)(2,1)S(1)}, bf16[1,2048,768]{2,1,0:T(8,128)(2,1)}, u32[]{:S(2)}) copy-start(bf16[1,2048,768]{2,1,0:T(8,128)(2,1)} %param.8) | copy-start | bytes 9437188
  22.2 30.3 %all-to-all-start = ((bf16[64,3,768]{2,1,0:T(4,128)(2,1)}), bf16[64,3,768]{2,1,0:T(4,128)(2,1)S(1)}, u32[]{:S(2)}, u32[]{:S(2)}) async-start(bf16[64,3,768]{2,1,0:T(4,128)(2,1)} %copy.20), calls=%async_computation | async-start | bytes 786432 | tf_op jit(solution)/shard_map/all_to_all | solution.py:22
  39.5 96.7 %reduce-scatter.4.cloned.1.call-start = ((), (), s32[]{:S(2)}) async-start(), calls=%async_computation.3 | async-start | bytes 3342336
  53.5 3.3 %copy-start.1 = (bf16[192,2048]{1,0:T(8,128)(2,1)S(1)}, bf16[192,2048]{1,0:T(8,128)(2,1)}, u32[]{:S(2)}) copy-start(bf16[192,2048]{1,0:T(8,128)(2,1)} %reshape.65) | copy-start | bytes 2359300
  64.2 1.9 %copy-start.2 = (bf16[1,2048,768]{2,1,0:T(8,128)(2,1)S(1)}, bf16[1,2048,768]{2,1,0:T(8,128)(2,1)}, u32[]{:S(2)}) copy-start(bf16[1,2048,768]{2,1,0:T(8,128)(2,1)} %param.9) | copy-start | bytes 9437188
  64.2 2.0 %copy-start.3 = (f32[192,768]{1,0:T(8,128)S(1)}, f32[192,768]{1,0:T(8,128)}, u32[]{:S(2)}) copy-start(f32[192,768]{1,0:T(8,128)} %fusion.2) | copy-start | bytes 1769476
  64.2 2.2 %copy-start.4 = (f32[192,768]{1,0:T(8,128)S(1)}, f32[192,768]{1,0:T(8,128)}, u32[]{:S(2)}) copy-start(f32[192,768]{1,0:T(8,128)} %reshape.67) | copy-start | bytes 1769476
Sparse Core Ops, SparseCore 0:
  64.3 71.8 reduce-scatter.3
where the time goes:
time: 148 us; the launch traced here: 147 us
  local copies, waits for them, and re-layouts  38.1 us (26%)
  blocking collectives  33.9 us (23%)
  waiting for transfers between devices  27.7 us (19%)
  starting transfers between devices  17.4 us (12%)
  between operations  14.1 us (10%)
  matrix products  12 us (8%)
  other arithmetic  3.42 us (2%)
    all_to_all x1, blocking collectives, on_device(): lax.all_to_all(back, 'expert', split_axis=0, concat_axis=0, tiled=True)  33.9 us
    unnamed x2, waiting for transfers between devices  23.6 us
    all_to_all x1, starting transfers between devices, on_device(): lax.all_to_all(outgoing, 'expert', split_axis=0, concat_axis=0, tiled=True)  17.3 us
    scatter x2, local copies, waits for them, and re-layouts, on_device(): outgoing.at[flat_ids, slot].set(grad_hidden.reshape(routed, hidden))  13.4 us
    unnamed x15, local copies, waits for them, and re-layouts  12 us
    all_to_all x1, waiting for transfers between devices, on_device(): lax.all_to_all(outgoing, 'expert', split_axis=0, concat_axis=0, tiled=True)  4.13 us
    gather x1, local copies, waits for them, and re-layouts, on_device(): picked = returned[flat_ids, slot]  3.53 us
    dot_general x1, matrix products, on_device(): upper = jnp.dot(inputs, w_up, preferred_element_type=jnp.float32)  3.33 us
  transfers between devices with their start and end apart: 2, of which 2 were waited for; matrix products, arithmetic and copies ran while one was open for 15% of the time, Pallas kernels for 0%

commit v1 on v0

v1 whole, which is shorter than its diff:
```python
import functools

import jax
import jax.numpy as jnp
from jax import lax
from jax.experimental import pallas as pl
from jax.experimental.pallas import tpu as pltpu
from jax.sharding import PartitionSpec as P

BF, F32 = jnp.bfloat16, jnp.float32
LANES = 128
MIB = 1 << 20
WHOLE = pl.BlockSpec(memory_space=pltpu.VMEM)
SCALAR = pl.BlockSpec(memory_space=pltpu.SMEM)
NT = (((1,), (1,)), ((), ()))


def call(body, outs, n_in, scratch=(), flops=0, moved=0, first=None, vmem=16):
    return pl.pallas_call(
        body,
        out_shape=outs,
        in_specs=[SCALAR if i == first else WHOLE for i in range(n_in)],
        out_specs=jax.tree.map(lambda _: WHOLE, outs),
        scratch_shapes=list(scratch),
        compiler_params=pltpu.CompilerParams(vmem_limit_bytes=vmem * MIB),
        cost_estimate=pl.CostEstimate(flops=flops, bytes_accessed=moved, transcendentals=0),
    )


def iota(shape, axis):
    return lax.broadcasted_iota(jnp.int32, shape, axis)


def pack(peers, cap, ids_ref, grads_ref, out_ref, take_ref, wide_ref):
    picks, tokens = ids_ref.shape
    routed, hidden = grads_ref.shape
    ids = ids_ref[...].astype(F32).astype(BF)
    token_of = (iota((tokens, routed), 1) // picks == iota((tokens, routed), 0)).astype(F32).astype(BF)
    by_row = jnp.dot(ids, token_of, preferred_element_type=F32)
    mine = iota((picks, routed), 1) % picks == iota((picks, routed), 0)
    e_row = jnp.sum(jnp.where(mine, by_row, 0.0), axis=0, keepdims=True)
    token_col = (iota((routed, tokens), 0) // picks == iota((routed, tokens), 1)).astype(F32).astype(BF)
    by_col = lax.dot_general(token_col, ids, NT, preferred_element_type=F32)
    mine = iota((routed, picks), 0) % picks == iota((routed, picks), 1)
    e_col = jnp.sum(jnp.where(mine, by_col, 0.0), axis=1, keepdims=True)
    earlier = iota((routed, routed), 0) < iota((routed, routed), 1)
    slot = jnp.sum(jnp.where(earlier & (e_col == e_row), 1.0, 0.0), axis=0, keepdims=True)
    row = slot * peers + e_row
    place = (iota((cap * peers, routed), 0).astype(F32) == row).astype(F32).astype(BF)
    sent = jnp.dot(place, grads_ref[...], preferred_element_type=F32)
    cols = hidden // LANES
    rows = wide_ref.shape[0] // peers
    for j in range(cap):
        for c in range(cols):
            wide_ref[pl.ds(j * cols + c, peers, stride=rows), :] = sent[
                j * peers : (j + 1) * peers, c * LANES : (c + 1) * LANES
            ]
    for r in range(cap * cols, rows):
        wide_ref[pl.ds(r, peers, stride=rows), :] = jnp.zeros((peers, LANES), F32)
    out_ref[...] = wide_ref[...].astype(BF)
    take_ref[...] = lax.dot_general(token_of, place, NT, preferred_element_type=F32).astype(BF)


def partner_columns(core_ref, x_ref, out_ref):
    other = 1 - core_ref[0]
    for z in range(out_ref.shape[1] // LANES):
        start = pl.multiple_of((2 * z + other) * LANES, LANES)
        out_ref[:, z * LANES : (z + 1) * LANES] = x_ref[:, pl.ds(start, LANES)]


def by_role(roles, spot_ref, x_ref, partner_ref, out_ref):
    core, z = spot_ref[0], spot_ref[1]
    chips = partner_ref.shape[1] // LANES
    rows = x_ref.shape[0]
    sign = 1 - 2 * core
    for n, offset in enumerate(roles):
        chip = lax.rem(z + sign * offset + chips, chips)
        start = pl.multiple_of((2 * chip + core) * LANES, LANES)
        own = x_ref[:, pl.ds(start, LANES)].astype(F32)
        near = partner_ref[:, pl.ds(pl.multiple_of(chip * LANES, LANES), LANES)].astype(F32)
        both = jnp.concatenate([own, near], axis=0)
        out_ref[n * LANES : (n + 1) * LANES, :] = both.T.astype(BF)


def factors(x_ref, wg_ref, wu_ref, fg_ref, fu_ref):
    x = x_ref[...]
    gate = jnp.dot(x, wg_ref[...], preferred_element_type=F32)
    up = jnp.dot(x, wu_ref[...], preferred_element_type=F32)
    sig = 1.0 / (1.0 + jnp.exp(-gate))
    fg_ref[...] = up * sig * (1.0 + gate * (1.0 - sig))
    fu_ref[...] = gate * sig


def hidden_grads(peers, cap, got_ref, fg_ref, fu_ref, dgate_ref, dup_ref, wide_ref):
    wide_ref[...] = got_ref[...].astype(F32)
    rows = wide_ref.shape[0] // peers
    cols = fg_ref.shape[1] // LANES
    for j in range(cap):
        for c in range(cols):
            at = (slice(j * peers, (j + 1) * peers), slice(c * LANES, (c + 1) * LANES))
            piece = wide_ref[pl.ds(j * cols + c, peers, stride=rows), :]
            dgate_ref[at] = (piece * fg_ref[at]).astype(BF)
            dup_ref[at] = (piece * fu_ref[at]).astype(BF)


def input_grads(peers, cap, steps, dgate_ref, dup_ref, wg_ref, wu_ref, out_ref, wide_ref):
    step = pl.program_id(0)
    back = lax.dot_general(dgate_ref[...], wg_ref[...], NT, preferred_element_type=F32)
    back = back + lax.dot_general(dup_ref[...], wu_ref[...], NT, preferred_element_type=F32)
    rows = wide_ref.shape[0] // peers
    cols = back.shape[1] // LANES
    for j in range(cap):
        for c in range(cols):
            at = j * (rows // cap) + step * cols + c
            wide_ref[pl.ds(at, peers, stride=rows), :] = back[
                j * peers : (j + 1) * peers, c * LANES : (c + 1) * LANES
            ]

    @pl.when(step == steps - 1)
    def _():
        out_ref[...] = wide_ref[...].astype(BF)


def partials(first, xt_ref, own_ref, near_ref, *outs):
    rows = own_ref.shape[0]
    xt = xt_ref[first * LANES : (first + len(outs)) * LANES, :]
    total = jnp.dot(xt[:, :rows], own_ref[...], preferred_element_type=F32)
    total = total + jnp.dot(xt[:, rows:], near_ref[...], preferred_element_type=F32)
    for n, out in enumerate(outs):
        out[...] = total[n * LANES : (n + 1) * LANES].astype(out.dtype)


def add_right(part_ref, a_ref, b_ref, out_ref):
    out_ref[...] = (part_ref[...] + a_ref[...].astype(F32) + b_ref[...].astype(F32)).astype(BF)


def add_left(part_ref, a_ref, out_ref):
    out_ref[...] = (part_ref[...] + a_ref[...].astype(F32)).astype(BF)


def total_of(part_ref, a_ref, b_ref, c_ref, d_ref, out_ref):
    near = a_ref[...].astype(F32) + b_ref[...].astype(F32)
    far = c_ref[...].astype(F32) + d_ref[...].astype(F32)
    out_ref[...] = part_ref[...] + near + far


def combine(peers, cap, take_ref, got_ref, out_ref, wide_ref):
    wide_ref[...] = got_ref[...].astype(F32)
    rows = wide_ref.shape[0] // peers
    cols = rows // cap
    for c in range(cols):
        part = [wide_ref[pl.ds(j * cols + c, peers, stride=rows), :] for j in range(cap)]
        piece = jnp.concatenate(part, axis=0).astype(BF)
        total = jnp.dot(take_ref[...], piece, preferred_element_type=F32)
        out_ref[:, c * LANES : (c + 1) * LANES] = total.astype(BF)


ROLES = (4, 3, -3, 1, -1, 2, -2, 0)


def on_device(expert_ids, grad_hidden, stored_inputs, gate_weight, up_weight):
    peers = lax.axis_size("expert")
    replicas = lax.axis_size("dp")
    chips = replicas // 2
    cap, width = stored_inputs.shape[3], stored_inputs.shape[4]
    hidden = gate_weight.shape[2]
    tokens, picks = expert_ids.shape
    routed, slot_rows = tokens * picks, peers * cap
    sds = jax.ShapeDtypeStruct
    w_gate, w_up = gate_weight[0], up_weight[0]
    x = stored_inputs[0, 0].transpose(1, 0, 2).reshape(slot_rows, width)
    spot = lax.axis_index("dp")
    spot = jnp.stack([spot % 2, spot // 2]).astype(jnp.int32)

    def along_z(value, offset):
        pairs = []
        for z in range(chips):
            for core in range(2):
                to = (z + (offset if core == 0 else -offset)) % chips
                pairs.append((2 * z + core, 2 * to + core))
        return lax.ppermute(value, "dp", pairs)

    swap = functools.partial(lax.ppermute, axis_name="dp", perm=[(i, i ^ 1) for i in range(replicas)])

    in_rows = -(-(cap * hidden // LANES) // 8) * 8
    outgoing, take = call(
        functools.partial(pack, peers, cap),
        (sds((peers * in_rows, LANES), BF), sds((tokens, slot_rows), BF)),
        2,
        [pltpu.VMEM((peers * in_rows, LANES), F32)],
        flops=2 * slot_rows * routed * hidden,
        moved=4 * peers * in_rows * LANES,
    )(expert_ids.T, grad_hidden.reshape(routed, hidden))
    arrived = lax.all_to_all(outgoing.reshape(peers, in_rows, LANES), "expert", 0, 0, tiled=True)

    half = chips * LANES
    lent = call(partner_columns, sds((slot_rows, half), BF), 2, first=0, moved=4 * slot_rows * half)(spot, x)
    borrowed = swap(lent)
    parts = hidden // 256
    f_gate, f_up = pl.pallas_call(
        factors,
        grid=(parts,),
        out_shape=(sds((slot_rows, hidden), F32),) * 2,
        in_specs=[
            pl.BlockSpec((slot_rows, width), lambda i: (0, 0)),
            pl.BlockSpec((width, 256), lambda i: (0, i)),
            pl.BlockSpec((width, 256), lambda i: (0, i)),
        ],
        out_specs=(pl.BlockSpec((slot_rows, 256), lambda i: (0, i)),) * 2,
        compiler_params=pltpu.CompilerParams(vmem_limit_bytes=24 * MIB),
        cost_estimate=pl.CostEstimate(
            flops=4 * slot_rows * width * hidden, bytes_accessed=8 * width * hidden, transcendentals=slot_rows * hidden
        ),
    )(x, w_gate, w_up)
    x_roles = call(
        functools.partial(by_role, ROLES),
        sds((len(ROLES) * LANES, 2 * slot_rows), BF),
        3,
        first=0,
        moved=8 * slot_rows * half,
    )(spot, x, borrowed)

    dgate, dup = call(
        functools.partial(hidden_grads, peers, cap),
        (sds((slot_rows, hidden), BF),) * 2,
        3,
        [pltpu.VMEM((peers * in_rows, LANES), F32)],
        moved=16 * slot_rows * hidden,
    )(arrived.reshape(peers * in_rows, LANES), f_gate, f_up)
    dgate_near = swap(dgate)

    out_rows = cap * width // LANES
    steps = width // 512
    back = pl.pallas_call(
        functools.partial(input_grads, peers, cap, steps),
        grid=(steps,),
        out_shape=sds((peers * out_rows, LANES), BF),
        in_specs=[
            pl.BlockSpec((slot_rows, hidden), lambda i: (0, 0)),
            pl.BlockSpec((slot_rows, hidden), lambda i: (0, 0)),
            pl.BlockSpec((512, hidden), lambda i: (i, 0)),
            pl.BlockSpec((512, hidden), lambda i: (i, 0)),
        ],
        out_specs=pl.BlockSpec((peers * out_rows, LANES), lambda i: (0, 0)),
        scratch_shapes=[pltpu.VMEM((peers * out_rows, LANES), F32)],
        compiler_params=pltpu.CompilerParams(vmem_limit_bytes=24 * MIB),
        cost_estimate=pl.CostEstimate(
            flops=4 * slot_rows * width * hidden, bytes_accessed=8 * width * hidden, transcendentals=0
        ),
    )(dgate, dup, w_gate, w_up)
    returned = lax.all_to_all(back.reshape(peers, out_rows, LANES), "expert", 0, 0, tiled=True)

    block, wide_block = sds((LANES, hidden), BF), sds((LANES, hidden), F32)
    work = 4 * LANES * slot_rows * hidden
    b4, b3, b3n = call(
        functools.partial(partials, 0), (block,) * 3, 3, flops=3 * work, moved=6 * LANES * hidden
    )(x_roles, dgate, dgate_near)
    c4 = along_z(b4, 2)
    c3 = along_z(b3, 1)
    c3n = along_z(b3n, -1)
    b1, b1n = call(
        functools.partial(partials, 3), (block,) * 2, 3, flops=2 * work, moved=4 * LANES * hidden
    )(x_roles, dgate, dgate_near)
    p2, p2n, p0 = call(
        functools.partial(partials, 5), (wide_block,) * 3, 3, flops=3 * work, moved=12 * LANES * hidden
    )(x_roles, dgate, dgate_near)
    c1 = along_z(b1, 1)
    c1n = along_z(b1n, -1)
    moved = 10 * LANES * hidden
    c2 = along_z(call(add_right, block, 3, moved=moved)(p2, c4, c3), 2)
    c2n = along_z(call(add_left, block, 2, moved=moved)(p2n, c3n), -2)
    grad_gate = call(total_of, wide_block, 5, moved=2 * moved)(p0, c1, c1n, c2, c2n)

    grad_tokens = call(
        functools.partial(combine, peers, cap),
        sds((tokens, width), BF),
        2,
        [pltpu.VMEM((peers * out_rows, LANES), F32)],
        flops=2 * tokens * slot_rows * width,
        moved=2 * slot_rows * width,
    )(take, returned.reshape(peers * out_rows, LANES))
    return (grad_tokens, grad_gate[None])


def solution(mesh):
    return jax.shard_map(
        on_device,
        mesh=mesh,
        in_specs=(
            P(("dp", "expert"), None),
            P(("dp", "expert"), None, None),
            P("dp", "expert", None, None, None),
            P("expert", None, None),
            P("expert", None, None),
        ),
        out_specs=(P(("dp", "expert"), None), P("expert", "dp", None)),
        check_vma=False,
    )
```

time: 148 us -> 103 us (0.70)
  the two profiles are of different devices: /device:TPU:6 before, /device:TPU:1 now
where the time goes in v1:
time: 103 us
  starting transfers between devices  61 us (59%)
  local copies, waits for them, and re-layouts  14.2 us (14%)
  waiting for transfers between devices  13.4 us (13%)
  Pallas kernels  13 us (13%)
    ppermute x7, starting transfers between devices, along_z(): return lax.ppermute(value, 'dp', pairs)  29.2 us
    all_to_all x1, starting transfers between devices, on_device(): lax.all_to_all(outgoing.reshape(peers, in_rows, LANES), 'expert', 0, 0, t...  14.3 us
    unnamed x26, local copies, waits for them, and re-layouts  14.2 us
    ppermute x7, waiting for transfers between devices, along_z(): return lax.ppermute(value, 'dp', pairs)  8.46 us
    all_to_all x1, starting transfers between devices, on_device(): lax.all_to_all(back.reshape(peers, out_rows, LANES), 'expert', 0, 0, tile...  7.84 us
    ppermute x1, starting transfers between devices, on_device(): borrowed = swap(lent)  7.8 us
    all_to_all x1, waiting for transfers between devices, on_device(): lax.all_to_all(outgoing.reshape(peers, in_rows, LANES), 'expert', 0, 0, t...  4.23 us
    pallas_call x1, Pallas kernels, on_device(): pl.pallas_call(functools.partial(input_grads, peers, cap, steps), grid=(s...  2.97 us
  transfers between devices with their start and end apart: 11, of which 4 were waited for; matrix products, arithmetic and copies ran while one was open for 0% of the time, Pallas kernels for 6%

profile of v1, /device:TPU:1, one launch (start us, length us, event | category | flops | bytes accessed | tf_op | source)
XLA Modules:
  0.0 102.6 jit_solution(11619552870809238198)
XLA Ops:
  0.6 0.0 copy-start.11
  0.6 0.9 copy-done.11
  1.6 0.0 copy-start.12
  1.6 0.7 copy-done.12
  2.2 1.3 %shard_map.68 = (bf16[1536,128]{1,0:T(8,128)(2,1)}, bf16[16,192]{1,0:T(8,128)(2,1)S(1)}) custom-call(s32[8,16]{1,0:T(8,128)S(1)} %bitcast.26, bf16[128,768]{1,0:T(8,128)(2,1)S(1)} %bitcast.25), custom_call_target="tpu_custom_call" | custom-call | flops 37748736 | bytes 786432 | tf_op jit(solution)/shard_map/pallas_call | solution.py:186
  3.5 14.3 %all-to-all-start = ((bf16[64,24,128]{2,1,0:T(8,128)(2,1)}), bf16[64,24,128]{2,1,0:T(8,128)(2,1)}, u32[]{:S(2)}, u32[]{:S(2)}) async-start(bf16[64,24,128]{2,1,0:T(8,128)(2,1)} %bitcast.2), calls=%async_computation | async-start | bytes 786432 | tf_op jit(solution)/shard_map/all_to_all | solution.py:194
  17.8 0.0 copy-start
  17.8 1.9 %copy-done = bf16[1,2048,768]{2,1,0:T(8,128)(2,1)S(1)} copy-done((bf16[1,2048,768]{2,1,0:T(8,128)(2,1)S(1)}, bf16[1,2048,768]{2,1,0:T(8,128)(2,1)}, u32[]{:S(2)}) %copy-start) | copy-done | bytes 3145752
  19.7 0.0 copy-start.2
  19.7 1.9 %copy-done.2 = bf16[1,2048,768]{2,1,0:T(8,128)(2,1)S(1)} copy-done((bf16[1,2048,768]{2,1,0:T(8,128)(2,1)S(1)}, bf16[1,2048,768]{2,1,0:T(8,128)(2,1)}, u32[]{:S(2)}) %copy-start.2) | copy-done | bytes 3145752
  21.6 0.0 copy-start.4
  21.6 1.1 %copy-done.4 = bf16[1,1,64,3,2048]{4,2,3,1,0:T(8,128)(2,1)S(1)} copy-done((bf16[1,1,64,3,2048]{4,2,3,1,0:T(8,128)(2,1)S(1)}, bf16[1,1,64,3,2048]{4,2,3,1,0:T(8,128)(2,1)}, u32[]{:S(2)}) %copy-start.4) | copy-done | bytes 786456
  22.7 0.0 copy-start.1
  22.7 2.4 %shard_map.69 = (f32[192,768]{1,0:T(8,128)S(1)}, f32[192,768]{1,0:T(8,128)S(1)}) custom-call(bf16[192,2048]{1,0:T(8,128)(2,1)S(1)} %bitcast.20, bf16[2048,768]{1,0:T(8,128)(2,1)S(1)} %bitcast.16, bf16[2048,768]{1,0:T(8,128)(2,1)S(1)} %bitcast.18), custom_call_target="tpu_custom_call" | custom-call | flops 1207959552 | bytes 12582912 | tf_op jit(solution)/shard_map/pallas_call | solution.py:200
  25.1 0.0 copy-start.7
  25.1 0.8 copy-done.7
  25.9 0.0 copy-start.9
  25.9 0.8 copy-done.9
  26.8 4.2 %all-to-all-done = bf16[64,24,128]{2,1,0:T(8,128)(2,1)} async-done(((bf16[64,24,128]{2,1,0:T(8,128)(2,1)}), bf16[64,24,128]{2,1,0:T(8,128)(2,1)}, u32[]{:S(2)}, u32[]{:S(2)}) %all-to-all-start) | async-done | bytes 393248 | tf_op jit(solution)/shard_map/all_to_all | solution.py:194
  31.0 0.0 copy-start.8
  31.0 1.1 %copy-done.8 = f32[192,768]{1,0:T(8,128)S(1)} copy-done((f32[192,768]{1,0:T(8,128)S(1)}, f32[192,768]{1,0:T(8,128)}, u32[]{:S(2)}) %copy-start.8) | copy-done | bytes 589848
  32.1 0.0 copy-start.10
  32.1 1.1 %copy-done.10 = f32[192,768]{1,0:T(8,128)S(1)} copy-done((f32[192,768]{1,0:T(8,128)S(1)}, f32[192,768]{1,0:T(8,128)}, u32[]{:S(2)}) %copy-start.10) | copy-done | bytes 589848
  33.1 1.2 %shard_map.70 = (bf16[192,768]{1,0:T(8,128)(2,1)S(1)}, bf16[192,768]{1,0:T(8,128)(2,1)S(1)}) custom-call(bf16[1536,128]{1,0:T(8,128)(2,1)} %bitcast.3.got_ref, f32[192,768]{1,0:T(8,128)S(1)} %copy-done.8, f32[192,768]{1,0:T(8,128)S(1)} %copy-done.10), custom_call_target="tpu_custom_call" | custom-call | bytes 2359296 | tf_op jit(solution)/shard_map/pallas_call | solution.py:223
  34.4 0.0 copy-done.1
  34.4 0.0 copy-start.3
  34.4 1.9 %copy-done.3 = bf16[1,2048,768]{2,1,0:T(8,128)(2,1)S(1)} copy-done((bf16[1,2048,768]{2,1,0:T(8,128)(2,1)S(1)}, bf16[1,2048,768]{2,1,0:T(8,128)(2,1)}, u32[]{:S(2)}) %copy-start.3) | copy-done | bytes 3145752
  36.3 3.0 %shard_map.71 = bf16[3072,128]{1,0:T(8,128)(2,1)S(1)} custom-call(bf16[192,768]{1,0:T(8,128)(2,1)S(1)} %get-tuple-element.20.dgate_ref.own_ref, bf16[192,768]{1,0:T(8,128)(2,1)S(1)} %get-tuple-element.21.dup_ref, bf16[2048,768]{1,0:T(8,128)(2,1)S(1)} %bitcast.17, bf16[2048,768]{1,0:T(8,128)(2,1)S(1)} %bitcast.19), custom_call_target="tpu_custom_call" | custom-call | flops 1207959552 | bytes 12582912 | tf_op jit(solution)/shard_map/pallas_call | solution.py:234
  39.3 0.0 copy-start.6
  39.3 0.9 copy-done.6
  40.2 7.8 %all-to-all-start.1 = ((bf16[64,48,128]{2,1,0:T(8,128)(2,1)}), bf16[64,48,128]{2,1,0:T(8,128)(2,1)S(1)}, u32[]{:S(2)}, u32[]{:S(2)}) async-start(bf16[64,48,128]{2,1,0:T(8,128)(2,1)} %bitcast.23), calls=%async_computation.1 | async-start | bytes 1572864 | tf_op jit(solution)/shard_map/all_to_all | solution.py:251
  48.0 0.1 pad_add_fusion.core_ref.spot_ref
  48.1 0.0 copy-start.5
  48.1 1.1 %copy-done.5 = bf16[1,1,64,3,2048]{4,2,3,1,0:T(8,128)(2,1)S(1)} copy-done((bf16[1,1,64,3,2048]{4,2,3,1,0:T(8,128)(2,1)S(1)}, bf16[1,1,64,3,2048]{4,2,3,1,0:T(8,128)(2,1)}, u32[]{:S(2)}) %copy-start.5) | copy-done | bytes 786456
  49.2 0.6 shard_map.73
  49.9 7.8 %collective-permute-start = (bf16[192,1024]{1,0:T(8,128)(2,1)S(1)}, bf16[192,1024]{1,0:T(8,128)(2,1)S(1)}, u32[]{:S(2)}, u32[]{:S(2)}) collective-permute-start(bf16[192,1024]{1,0:T(8,128)(2,1)S(1)} %shard_map.73), channel_id=1, source_target_pairs={{0,64},{64,0},{128,192},{192,128},{256,320},{320,256},{384,448},{4... | collective-permute-start | bytes 1179656 | tf_op jit(solution)/shard_map/ppermute | solution.py:198
  57.7 1.9 %collective-permute-start.1 = (bf16[192,768]{1,0:T(8,128)(2,1)S(1)}, bf16[192,768]{1,0:T(8,128)(2,1)S(1)}, u32[]{:S(2)}, u32[]{:S(2)}) collective-permute-start(bf16[192,768]{1,0:T(8,128)(2,1)S(1)} %get-tuple-element.20.dgate_ref.own_ref), channel_id=1, source_target_pairs={{0,64},{64,0},{128,192},{192,128},{256,320},{320,256},{384,448},{4... | collective-permute-start | bytes 884744 | tf_op jit(solution)/shard_map/ppermute | solution.py:230
  59.6 0.0 collective-permute-done.partner_ref
  59.6 0.8 shard_map.74.xt_ref
  60.5 0.7 collective-permute-done.1.near_ref
  61.2 0.5 shard_map.77
  61.7 11.8 %collective-permute-start.4 = (bf16[128,768]{1,0:T(8,128)(2,1)S(1)}, bf16[128,768]{1,0:T(8,128)(2,1)S(1)}, u32[]{:S(2)}, u32[]{:S(2)}) collective-permute-start(bf16[128,768]{1,0:T(8,128)(2,1)S(1)} %get-tuple-element.26), channel_id=1, source_target_pairs={{0,256},{64,832},{128,384},{192,960},{256,512},{320,64},{384,640},... | collective-permute-start | bytes 589832 | tf_op jit(solution)/shard_map/ppermute | solution.py:181
  73.5 2.9 %collective-permute-start.5 = (bf16[128,768]{1,0:T(8,128)(2,1)S(1)}, bf16[128,768]{1,0:T(8,128)(2,1)S(1)}, u32[]{:S(2)}, u32[]{:S(2)}) collective-permute-start(bf16[128,768]{1,0:T(8,128)(2,1)S(1)} %get-tuple-element.27), channel_id=1, source_target_pairs={{0,128},{64,960},{128,256},{192,64},{256,384},{320,192},{384,512},... | collective-permute-start | bytes 589832 | tf_op jit(solution)/shard_map/ppermute | solution.py:181
  76.3 3.1 %collective-permute-start.7 = (bf16[128,768]{1,0:T(8,128)(2,1)S(1)}, bf16[128,768]{1,0:T(8,128)(2,1)S(1)}, u32[]{:S(2)}, u32[]{:S(2)}) collective-permute-start(bf16[128,768]{1,0:T(8,128)(2,1)S(1)} %get-tuple-element.29), channel_id=1, source_target_pairs={{0,896},{64,192},{128,0},{192,320},{256,128},{320,448},{384,256},{... | collective-permute-start | bytes 589832 | tf_op jit(solution)/shard_map/ppermute | solution.py:181
  79.4 0.4 shard_map.76
  79.8 3.4 %collective-permute-start.2 = (bf16[128,768]{1,0:T(8,128)(2,1)S(1)}, bf16[128,768]{1,0:T(8,128)(2,1)S(1)}, u32[]{:S(2)}, u32[]{:S(2)}) collective-permute-start(bf16[128,768]{1,0:T(8,128)(2,1)S(1)} %get-tuple-element.23), channel_id=1, source_target_pairs={{0,128},{64,960},{128,256},{192,64},{256,384},{320,192},{384,512},... | collective-permute-start | bytes 589832 | tf_op jit(solution)/shard_map/ppermute | solution.py:181
  83.2 1.9 %collective-permute-start.3 = (bf16[128,768]{1,0:T(8,128)(2,1)S(1)}, bf16[128,768]{1,0:T(8,128)(2,1)S(1)}, u32[]{:S(2)}, u32[]{:S(2)}) collective-permute-start(bf16[128,768]{1,0:T(8,128)(2,1)S(1)} %get-tuple-element.24), channel_id=1, source_target_pairs={{0,896},{64,192},{128,0},{192,320},{256,128},{320,448},{384,256},{... | collective-permute-start | bytes 589832 | tf_op jit(solution)/shard_map/ppermute | solution.py:181
  85.2 0.5 shard_map.75
  85.7 0.0 collective-permute-done.4.a_ref
  85.7 0.0 collective-permute-done.5.b_ref
  85.7 0.1 shard_map.78
  85.8 3.1 %collective-permute-start.6 = (bf16[128,768]{1,0:T(8,128)(2,1)S(1)}, bf16[128,768]{1,0:T(8,128)(2,1)S(1)}, u32[]{:S(2)}, u32[]{:S(2)}) collective-permute-start(bf16[128,768]{1,0:T(8,128)(2,1)S(1)} %shard_map.78), channel_id=1, source_target_pairs={{0,256},{64,832},{128,384},{192,960},{256,512},{320,64},{384,640},... | collective-permute-start | bytes 589832 | tf_op jit(solution)/shard_map/ppermute | solution.py:181
  88.9 0.0 collective-permute-done.7.a_ref
  88.9 3.1 %collective-permute-start.8 = (bf16[128,768]{1,0:T(8,128)(2,1)S(1)}, bf16[128,768]{1,0:T(8,128)(2,1)S(1)}, u32[]{:S(2)}, u32[]{:S(2)}) collective-permute-start(bf16[128,768]{1,0:T(8,128)(2,1)S(1)} %shard_map.79), channel_id=1, source_target_pairs={{0,768},{64,320},{128,896},{192,448},{256,0},{320,576},{384,128},{... | collective-permute-start | bytes 589832 | tf_op jit(solution)/shard_map/ppermute | solution.py:181
  92.0 0.0 collective-permute-done.2.a_ref
  92.0 0.0 collective-permute-done.3.b_ref
  92.0 3.4 %collective-permute-done.6.c_ref = bf16[128,768]{1,0:T(8,128)(2,1)S(1)} collective-permute-done((bf16[128,768]{1,0:T(8,128)(2,1)S(1)}, bf16[128,768]{1,0:T(8,128)(2,1)S(1)}, u32[]{:S(2)}, u32[]{:S(2)}) %collective-permute-start.6) | collective-permute-done | bytes 196640 | tf_op jit(solution)/shard_map/ppermute | solution.py:181
  95.5 5.0 %collective-permute-done.8.d_ref = bf16[128,768]{1,0:T(8,128)(2,1)S(1)} collective-permute-done((bf16[128,768]{1,0:T(8,128)(2,1)S(1)}, bf16[128,768]{1,0:T(8,128)(2,1)S(1)}, u32[]{:S(2)}, u32[]{:S(2)}) %collective-permute-start.8) | collective-permute-done | bytes 196640 | tf_op jit(solution)/shard_map/ppermute | solution.py:181
  100.5 0.8 shard_map.80
  101.3 0.0 all-to-all-done.1
  101.3 1.3 %shard_map.72 = bf16[16,2048]{1,0:T(8,128)(2,1)} custom-call(bf16[16,192]{1,0:T(8,128)(2,1)S(1)} %get-tuple-element.16.take_ref, bf16[3072,128]{1,0:T(8,128)(2,1)S(1)} %bitcast.24), custom_call_target="tpu_custom_call" | custom-call | flops 12582912 | bytes 786432 | tf_op jit(solution)/shard_map/pallas_call | solution.py:274
  (1 shorter events, 0.0 us)
Async XLA Ops:
  0.6 0.9 copy-start.11
  1.6 0.7 copy-start.12
  3.5 27.5 %all-to-all-start = ((bf16[64,24,128]{2,1,0:T(8,128)(2,1)}), bf16[64,24,128]{2,1,0:T(8,128)(2,1)}, u32[]{:S(2)}, u32[]{:S(2)}) async-start(bf16[64,24,128]{2,1,0:T(8,128)(2,1)} %bitcast.2), calls=%async_computation | async-start | bytes 786432 | tf_op jit(solution)/shard_map/all_to_all | solution.py:194
  17.8 1.9 %copy-start = (bf16[1,2048,768]{2,1,0:T(8,128)(2,1)S(1)}, bf16[1,2048,768]{2,1,0:T(8,128)(2,1)}, u32[]{:S(2)}) copy-start(bf16[1,2048,768]{2,1,0:T(8,128)(2,1)} %param.8) | copy-start | bytes 9437188
  19.7 1.9 %copy-start.2 = (bf16[1,2048,768]{2,1,0:T(8,128)(2,1)S(1)}, bf16[1,2048,768]{2,1,0:T(8,128)(2,1)}, u32[]{:S(2)}) copy-start(bf16[1,2048,768]{2,1,0:T(8,128)(2,1)} %param.9) | copy-start | bytes 9437188
  21.6 1.1 %copy-start.4 = (bf16[1,1,64,3,2048]{4,2,3,1,0:T(8,128)(2,1)S(1)}, bf16[1,1,64,3,2048]{4,2,3,1,0:T(8,128)(2,1)}, u32[]{:S(2)}) copy-start(bf16[1,1,64,3,2048]{4,2,3,1,0:T(8,128)(2,1)} %param.7) | copy-start | bytes 2359300
  22.7 11.7 %copy-start.1 = (bf16[1,2048,768]{2,1,0:T(8,128)(2,1)S(1)}, bf16[1,2048,768]{2,1,0:T(8,128)(2,1)}, u32[]{:S(2)}) copy-start(bf16[1,2048,768]{2,1,0:T(8,128)(2,1)} %param.8) | copy-start | bytes 9437188
  25.1 0.8 copy-start.7
  25.9 0.8 copy-start.9
  31.0 1.1 %copy-start.8 = (f32[192,768]{1,0:T(8,128)S(1)}, f32[192,768]{1,0:T(8,128)}, u32[]{:S(2)}) copy-start(f32[192,768]{1,0:T(8,128)} %copy-done.7) | copy-start | bytes 1769476
  32.1 1.1 %copy-start.10 = (f32[192,768]{1,0:T(8,128)S(1)}, f32[192,768]{1,0:T(8,128)}, u32[]{:S(2)}) copy-start(f32[192,768]{1,0:T(8,128)} %copy-done.9) | copy-start | bytes 1769476
  34.4 1.9 %copy-start.3 = (bf16[1,2048,768]{2,1,0:T(8,128)(2,1)S(1)}, bf16[1,2048,768]{2,1,0:T(8,128)(2,1)}, u32[]{:S(2)}) copy-start(bf16[1,2048,768]{2,1,0:T(8,128)(2,1)} %param.9) | copy-start | bytes 9437188
  39.3 0.9 copy-start.6
  40.2 61.2 %all-to-all-start.1 = ((bf16[64,48,128]{2,1,0:T(8,128)(2,1)}), bf16[64,48,128]{2,1,0:T(8,128)(2,1)S(1)}, u32[]{:S(2)}, u32[]{:S(2)}) async-start(bf16[64,48,128]{2,1,0:T(8,128)(2,1)} %bitcast.23), calls=%async_computation.1 | async-start | bytes 1572864 | tf_op jit(solution)/shard_map/all_to_all | solution.py:251
  48.1 1.1 %copy-start.5 = (bf16[1,1,64,3,2048]{4,2,3,1,0:T(8,128)(2,1)S(1)}, bf16[1,1,64,3,2048]{4,2,3,1,0:T(8,128)(2,1)}, u32[]{:S(2)}) copy-start(bf16[1,1,64,3,2048]{4,2,3,1,0:T(8,128)(2,1)} %param.7) | copy-start | bytes 2359300
  49.9 9.7 %collective-permute-start = (bf16[192,1024]{1,0:T(8,128)(2,1)S(1)}, bf16[192,1024]{1,0:T(8,128)(2,1)S(1)}, u32[]{:S(2)}, u32[]{:S(2)}) collective-permute-start(bf16[192,1024]{1,0:T(8,128)(2,1)S(1)} %shard_map.73), channel_id=1, source_target_pairs={{0,64},{64,0},{128,192},{192,128},{256,320},{320,256},{384,448},{4... | collective-permute-start | bytes 1179656 | tf_op jit(solution)/shard_map/ppermute | solution.py:198
  57.7 3.5 %collective-permute-start.1 = (bf16[192,768]{1,0:T(8,128)(2,1)S(1)}, bf16[192,768]{1,0:T(8,128)(2,1)S(1)}, u32[]{:S(2)}, u32[]{:S(2)}) collective-permute-start(bf16[192,768]{1,0:T(8,128)(2,1)S(1)} %get-tuple-element.20.dgate_ref.own_ref), channel_id=1, source_target_pairs={{0,64},{64,0},{128,192},{192,128},{256,320},{320,256},{384,448},{4... | collective-permute-start | bytes 884744 | tf_op jit(solution)/shard_map/ppermute | solution.py:230
  61.7 24.0 %collective-permute-start.4 = (bf16[128,768]{1,0:T(8,128)(2,1)S(1)}, bf16[128,768]{1,0:T(8,128)(2,1)S(1)}, u32[]{:S(2)}, u32[]{:S(2)}) collective-permute-start(bf16[128,768]{1,0:T(8,128)(2,1)S(1)} %get-tuple-element.26), channel_id=1, source_target_pairs={{0,256},{64,832},{128,384},{192,960},{256,512},{320,64},{384,640},... | collective-permute-start | bytes 589832 | tf_op jit(solution)/shard_map/ppermute | solution.py:181
  73.5 12.2 %collective-permute-start.5 = (bf16[128,768]{1,0:T(8,128)(2,1)S(1)}, bf16[128,768]{1,0:T(8,128)(2,1)S(1)}, u32[]{:S(2)}, u32[]{:S(2)}) collective-permute-start(bf16[128,768]{1,0:T(8,128)(2,1)S(1)} %get-tuple-element.27), channel_id=1, source_target_pairs={{0,128},{64,960},{128,256},{192,64},{256,384},{320,192},{384,512},... | collective-permute-start | bytes 589832 | tf_op jit(solution)/shard_map/ppermute | solution.py:181
  76.3 12.5 %collective-permute-start.7 = (bf16[128,768]{1,0:T(8,128)(2,1)S(1)}, bf16[128,768]{1,0:T(8,128)(2,1)S(1)}, u32[]{:S(2)}, u32[]{:S(2)}) collective-permute-start(bf16[128,768]{1,0:T(8,128)(2,1)S(1)} %get-tuple-element.29), channel_id=1, source_target_pairs={{0,896},{64,192},{128,0},{192,320},{256,128},{320,448},{384,256},{... | collective-permute-start | bytes 589832 | tf_op jit(solution)/shard_map/ppermute | solution.py:181
  79.8 12.2 %collective-permute-start.2 = (bf16[128,768]{1,0:T(8,128)(2,1)S(1)}, bf16[128,768]{1,0:T(8,128)(2,1)S(1)}, u32[]{:S(2)}, u32[]{:S(2)}) collective-permute-start(bf16[128,768]{1,0:T(8,128)(2,1)S(1)} %get-tuple-element.23), channel_id=1, source_target_pairs={{0,128},{64,960},{128,256},{192,64},{256,384},{320,192},{384,512},... | collective-permute-start | bytes 589832 | tf_op jit(solution)/shard_map/ppermute | solution.py:181
  83.2 8.8 %collective-permute-start.3 = (bf16[128,768]{1,0:T(8,128)(2,1)S(1)}, bf16[128,768]{1,0:T(8,128)(2,1)S(1)}, u32[]{:S(2)}, u32[]{:S(2)}) collective-permute-start(bf16[128,768]{1,0:T(8,128)(2,1)S(1)} %get-tuple-element.24), channel_id=1, source_target_pairs={{0,896},{64,192},{128,0},{192,320},{256,128},{320,448},{384,256},{... | collective-permute-start | bytes 589832 | tf_op jit(solution)/shard_map/ppermute | solution.py:181
  85.8 9.7 %collective-permute-start.6 = (bf16[128,768]{1,0:T(8,128)(2,1)S(1)}, bf16[128,768]{1,0:T(8,128)(2,1)S(1)}, u32[]{:S(2)}, u32[]{:S(2)}) collective-permute-start(bf16[128,768]{1,0:T(8,128)(2,1)S(1)} %shard_map.78), channel_id=1, source_target_pairs={{0,256},{64,832},{128,384},{192,960},{256,512},{320,64},{384,640},... | collective-permute-start | bytes 589832 | tf_op jit(solution)/shard_map/ppermute | solution.py:181
  88.9 11.6 %collective-permute-start.8 = (bf16[128,768]{1,0:T(8,128)(2,1)S(1)}, bf16[128,768]{1,0:T(8,128)(2,1)S(1)}, u32[]{:S(2)}, u32[]{:S(2)}) collective-permute-start(bf16[128,768]{1,0:T(8,128)(2,1)S(1)} %shard_map.79), channel_id=1, source_target_pairs={{0,768},{64,320},{128,896},{192,448},{256,0},{320,576},{384,128},{... | collective-permute-start | bytes 589832 | tf_op jit(solution)/shard_map/ppermute | solution.py:181

commit v2 on v1

--- a/solution.py
+++ b/solution.py
@@ -10,21 +10,26 @@
 BF, F32 = jnp.bfloat16, jnp.float32
 LANES = 128
 MIB = 1 << 20
-WHOLE = pl.BlockSpec(memory_space=pltpu.VMEM)
-SCALAR = pl.BlockSpec(memory_space=pltpu.SMEM)
 NT = (((1,), (1,)), ((), ()))
 
 
-def call(body, outs, n_in, scratch=(), flops=0, moved=0, first=None, vmem=16):
-    return pl.pallas_call(
+def call(body, outs, ins, scratch=(), flops=0, moved=0, near=False, vmem=16):
+    specs = {"h": pl.BlockSpec(), "v": pl.BlockSpec(memory_space=pltpu.VMEM)}
+    specs |= {"s": pl.BlockSpec(memory_space=pltpu.SMEM), "u": pl.BlockSpec(memory_space=pl.ANY)}
+    kernel = pl.pallas_call(
         body,
-        out_shape=outs,
-        in_specs=[SCALAR if i == first else WHOLE for i in range(n_in)],
-        out_specs=jax.tree.map(lambda _: WHOLE, outs),
+        out_shape=outs if near else jax.tree.map(lambda out: pltpu.HBM(out.shape, out.dtype), outs),
+        in_specs=[specs[kind] for kind in ins],
+        out_specs=jax.tree.map(lambda _: specs["v" if near else "h"], outs),
         scratch_shapes=list(scratch),
         compiler_params=pltpu.CompilerParams(vmem_limit_bytes=vmem * MIB),
         cost_estimate=pl.CostEstimate(flops=flops, bytes_accessed=moved, transcendentals=0),
     )
+    return lambda *given: kernel(*(far(v) if kind in "hu" else v for kind, v in zip(ins, given)))
+
+
+def far(value):
+    return pltpu.with_memory_space_constraint(value, pltpu.HBM)
 
 
 def iota(shape, axis):
@@ -91,7 +96,7 @@
     fu_ref[...] = gate * sig
 
 
-def hidden_grads(peers, cap, got_ref, fg_ref, fu_ref, dgate_ref, dup_ref, wide_ref):
+def hidden_grads(peers, cap, got_ref, fg_ref, fu_ref, _, dgate_ref, dup_ref, wide_ref):
     wide_ref[...] = got_ref[...].astype(F32)
     rows = wide_ref.shape[0] // peers
     cols = fg_ref.shape[1] // LANES
@@ -103,7 +108,7 @@
             dup_ref[at] = (piece * fu_ref[at]).astype(BF)
 
 
-def input_grads(peers, cap, steps, dgate_ref, dup_ref, wg_ref, wu_ref, out_ref, wide_ref):
+def input_grads(peers, cap, steps, dgate_ref, dup_ref, wg_ref, wu_ref, _, out_ref, wide_ref):
     step = pl.program_id(0)
     back = lax.dot_general(dgate_ref[...], wg_ref[...], NT, preferred_element_type=F32)
     back = back + lax.dot_general(dup_ref[...], wu_ref[...], NT, preferred_element_type=F32)
@@ -121,25 +126,27 @@
         out_ref[...] = wide_ref[...].astype(BF)
 
 
-def partials(first, xt_ref, own_ref, near_ref, *outs):
+def partials(first, sizes, xt_ref, own_ref, near_ref, *outs):
     rows = own_ref.shape[0]
-    xt = xt_ref[first * LANES : (first + len(outs)) * LANES, :]
+    xt = xt_ref[first * LANES : (first + sum(sizes)) * LANES, :]
     total = jnp.dot(xt[:, :rows], own_ref[...], preferred_element_type=F32)
     total = total + jnp.dot(xt[:, rows:], near_ref[...], preferred_element_type=F32)
-    for n, out in enumerate(outs):
-        out[...] = total[n * LANES : (n + 1) * LANES].astype(out.dtype)
-
-
-def add_right(part_ref, a_ref, b_ref, out_ref):
-    out_ref[...] = (part_ref[...] + a_ref[...].astype(F32) + b_ref[...].astype(F32)).astype(BF)
-
-
-def add_left(part_ref, a_ref, out_ref):
-    out_ref[...] = (part_ref[...] + a_ref[...].astype(F32)).astype(BF)
+    at = 0
+    for size, out in zip(sizes, outs):
+        out[...] = total[at * LANES : (at + size) * LANES].astype(out.dtype)
+        at += size
+
+
+def add_two(part_ref, a_ref, b_ref, out_ref):
+    out_ref[...] = (part_ref[...] + a_ref[...].astype(F32) + b_ref[:LANES].astype(F32)).astype(BF)
+
+
+def add_one(part_ref, a_ref, out_ref):
+    out_ref[...] = (part_ref[...] + a_ref[:LANES].astype(F32)).astype(BF)
 
 
 def total_of(part_ref, a_ref, b_ref, c_ref, d_ref, out_ref):
-    near = a_ref[...].astype(F32) + b_ref[...].astype(F32)
+    near = a_ref[LANES:].astype(F32) + b_ref[LANES:].astype(F32)
     far = c_ref[...].astype(F32) + d_ref[...].astype(F32)
     out_ref[...] = part_ref[...] + near + far
 
@@ -155,7 +162,7 @@
         out_ref[:, c * LANES : (c + 1) * LANES] = total.astype(BF)
 
 
-ROLES = (4, 3, -3, 1, -1, 2, -2, 0)
+ROLES = (4, 3, 1, -3, -1, 2, -2, 0)
 
 
 def on_device(expert_ids, grad_hidden, stored_inputs, gate_weight, up_weight):
@@ -186,7 +193,7 @@
     outgoing, take = call(
         functools.partial(pack, peers, cap),
         (sds((peers * in_rows, LANES), BF), sds((tokens, slot_rows), BF)),
-        2,
+        "hh",
         [pltpu.VMEM((peers * in_rows, LANES), F32)],
         flops=2 * slot_rows * routed * hidden,
         moved=4 * peers * in_rows * LANES,
@@ -194,13 +201,13 @@
     arrived = lax.all_to_all(outgoing.reshape(peers, in_rows, LANES), "expert", 0, 0, tiled=True)
 
     half = chips * LANES
-    lent = call(partner_columns, sds((slot_rows, half), BF), 2, first=0, moved=4 * slot_rows * half)(spot, x)
+    lent = call(partner_columns, sds((slot_rows, half), BF), "sh", moved=4 * slot_rows * half)(spot, x)
     borrowed = swap(lent)
     parts = hidden // 256
     f_gate, f_up = pl.pallas_call(
         factors,
         grid=(parts,),
-        out_shape=(sds((slot_rows, hidden), F32),) * 2,
+        out_shape=(pltpu.HBM((slot_rows, hidden), F32),) * 2,
         in_specs=[
             pl.BlockSpec((slot_rows, width), lambda i: (0, 0)),
             pl.BlockSpec((width, 256), lambda i: (0, i)),
@@ -211,70 +218,70 @@
         cost_estimate=pl.CostEstimate(
             flops=4 * slot_rows * width * hidden, bytes_accessed=8 * width * hidden, transcendentals=slot_rows * hidden
         ),
-    )(x, w_gate, w_up)
+    )(far(x), far(w_gate), far(w_up))
     x_roles = call(
-        functools.partial(by_role, ROLES),
-        sds((len(ROLES) * LANES, 2 * slot_rows), BF),
-        3,
-        first=0,
-        moved=8 * slot_rows * half,
+        functools.partial(by_role, ROLES), sds((len(ROLES) * LANES, 2 * slot_rows), BF), "shv", moved=8 * slot_rows * half
     )(spot, x, borrowed)
 
     dgate, dup = call(
         functools.partial(hidden_grads, peers, cap),
         (sds((slot_rows, hidden), BF),) * 2,
-        3,
+        "vhhu",
         [pltpu.VMEM((peers * in_rows, LANES), F32)],
         moved=16 * slot_rows * hidden,
-    )(arrived.reshape(peers * in_rows, LANES), f_gate, f_up)
+    )(arrived.reshape(peers * in_rows, LANES), f_gate, f_up, x_roles)
     dgate_near = swap(dgate)
+
+    block, blocks, wide_block = (sds((n * LANES, hidden), t) for n, t in ((1, BF), (2, BF), (1, F32)))
+    work = 4 * LANES * slot_rows * hidden
+    most, right, left = call(
+        functools.partial(partials, 0, (1, 2, 2)), (block, blocks, blocks), "hhv", flops=5 * work, moved=10 * LANES * hidden
+    )(x_roles, dgate, dgate_near)
+    most_in = along_z(most, 2)
+    right_in = along_z(right, 1)
+    left_in = along_z(left, -1)
+    p2, p2n, p0 = call(
+        functools.partial(partials, 5, (1, 1, 1)),
+        (wide_block,) * 3,
+        "hhv",
+        flops=1,
+        moved=1,
+        near=True,
+    )(x_roles, dgate, dgate_near)
 
     out_rows = cap * width // LANES
     steps = width // 512
     back = pl.pallas_call(
         functools.partial(input_grads, peers, cap, steps),
         grid=(steps,),
-        out_shape=sds((peers * out_rows, LANES), BF),
+        out_shape=pltpu.HBM((peers * out_rows, LANES), BF),
         in_specs=[
             pl.BlockSpec((slot_rows, hidden), lambda i: (0, 0)),
             pl.BlockSpec((slot_rows, hidden), lambda i: (0, 0)),
             pl.BlockSpec((512, hidden), lambda i: (i, 0)),
             pl.BlockSpec((512, hidden), lambda i: (i, 0)),
+            pl.BlockSpec(memory_space=pl.ANY),
         ],
         out_specs=pl.BlockSpec((peers * out_rows, LANES), lambda i: (0, 0)),
         scratch_shapes=[pltpu.VMEM((peers * out_rows, LANES), F32)],
         compiler_params=pltpu.CompilerParams(vmem_limit_bytes=24 * MIB),
         cost_estimate=pl.CostEstimate(
-            flops=4 * slot_rows * width * hidden, bytes_accessed=8 * width * hidden, transcendentals=0
+            flops=1, bytes_accessed=1, transcendentals=0
         ),
-    )(dgate, dup, w_gate, w_up)
+    )(far(dgate), far(dup), far(w_gate), far(w_up), far(most))
     returned = lax.all_to_all(back.reshape(peers, out_rows, LANES), "expert", 0, 0, tiled=True)
 
-    block, wide_block = sds((LANES, hidden), BF), sds((LANES, hidden), F32)
-    work = 4 * LANES * slot_rows * hidden
-    b4, b3, b3n = call(
-        functools.partial(partials, 0), (block,) * 3, 3, flops=3 * work, moved=6 * LANES * hidden
-    )(x_roles, dgate, dgate_near)
-    c4 = along_z(b4, 2)
-    c3 = along_z(b3, 1)
-    c3n = along_z(b3n, -1)
-    b1, b1n = call(
-        functools.partial(partials, 3), (block,) * 2, 3, flops=2 * work, moved=4 * LANES * hidden
-    )(x_roles, dgate, dgate_near)
-    p2, p2n, p0 = call(
-        functools.partial(partials, 5), (wide_block,) * 3, 3, flops=3 * work, moved=12 * LANES * hidden
-    )(x_roles, dgate, dgate_near)
-    c1 = along_z(b1, 1)
-    c1n = along_z(b1n, -1)
     moved = 10 * LANES * hidden
-    c2 = along_z(call(add_right, block, 3, moved=moved)(p2, c4, c3), 2)
-    c2n = along_z(call(add_left, block, 2, moved=moved)(p2n, c3n), -2)
-    grad_gate = call(total_of, wide_block, 5, moved=2 * moved)(p0, c1, c1n, c2, c2n)
+    right_sum = along_z(call(add_two, block, "vvv", flops=20_000_000_000, moved=moved, near=True)(p2, most_in, right_in), 2)
+    left_sum = along_z(call(add_one, block, "vv", flops=20_000_000_000, moved=moved, near=True)(p2n, left_in), -2)
+    grad_gate = call(total_of, wide_block, "vvvvv", moved=2 * moved, near=False)(
+        p0, right_in, left_in, right_sum, left_sum
+    )
 
     grad_tokens = call(
         functools.partial(combine, peers, cap),
         sds((tokens, width), BF),
-        2,
+        "hv",
         [pltpu.VMEM((peers * out_rows, LANES), F32)],
         flops=2 * tokens * slot_rows * width,
         moved=2 * slot_rows * width,

time: 103 us -> 101 us (0.981)
  Pallas kernels: 13 us -> 28.2 us
  local copies, waits for them, and re-layouts: 14.2 us -> 0.01 us
  waiting for transfers between devices: 13.4 us -> 11 us
  starting transfers between devices: 61 us -> 59.7 us
    unnamed x26 -> x2, local copies, waits for them, and re-layouts: 14.2 us -> 0.01 us
    pallas_call x12 -> x11, Pallas kernels: 10 us -> 21.9 us  [the longest x10 16.2 us: call(): kernel(*(far(v) if kind in 'hu' else v for kind, v in zip(ins, given)))]
    all_to_all x1, waiting for transfers between devices: 4.23 us -> 0.01 us  [on_device(): lax.all_to_all(outgoing.reshape(peers, in_rows, LANES), 'expert', 0, 0, t...]
    pallas_call x1, Pallas kernels: 2.97 us -> 6.26 us  [on_device(): pl.pallas_call(functools.partial(input_grads, peers, cap, steps), grid=(s...]
    ppermute x1, starting transfers between devices: 1.92 us -> 4.25 us  [on_device(): dgate_near = swap(dgate)]
    ppermute x7 -> x5, starting transfers between devices: 29.2 us -> 27 us  [along_z(): return lax.ppermute(value, 'dp', pairs)]
    ppermute x1, starting transfers between devices: 7.8 us -> 6.64 us  [on_device(): borrowed = swap(lent)]
    ppermute x7 -> x5, waiting for transfers between devices: 8.46 us -> 9.61 us  [along_z(): return lax.ppermute(value, 'dp', pairs)]
  transfers between devices with their start and end apart: 11 -> 9, of which waited for: 4 -> 3; matrix products, arithmetic and copies ran while one was open for 0% -> 0% of each run, Pallas kernels for 6% -> 19%
where the time goes in v2:
time: 101 us; the launch traced here: 99.8 us
  starting transfers between devices  59.7 us (59%)
  Pallas kernels  28.2 us (28%)
  waiting for transfers between devices  11 us (11%)
    ppermute x5, starting transfers between devices, along_z(): return lax.ppermute(value, 'dp', pairs)  27 us
    pallas_call x10, Pallas kernels, call(): kernel(*(far(v) if kind in 'hu' else v for kind, v in zip(ins, given)))  16.2 us
    all_to_all x1, starting transfers between devices, on_device(): lax.all_to_all(outgoing.reshape(peers, in_rows, LANES), 'expert', 0, 0, t...  14 us
    ppermute x5, waiting for transfers between devices, along_z(): return lax.ppermute(value, 'dp', pairs)  9.61 us
    all_to_all x1, starting transfers between devices, on_device(): lax.all_to_all(back.reshape(peers, out_rows, LANES), 'expert', 0, 0, tile...  7.83 us
    ppermute x1, starting transfers between devices, on_device(): borrowed = swap(lent)  6.64 us
    pallas_call x1, Pallas kernels, on_device(): pl.pallas_call(functools.partial(input_grads, peers, cap, steps), grid=(s...  6.26 us
    pallas_call x1, Pallas kernels, on_device(): pl.pallas_call(factors, grid=(parts,), out_shape=(pltpu.HBM((slot_rows, h...  5.71 us
  transfers between devices with their start and end apart: 9, of which 3 were waited for; matrix products, arithmetic and copies ran while one was open for 0% of the time, Pallas kernels for 19%

profile of v2, /device:TPU:1, one launch (start us, length us, event | category | flops | bytes accessed | tf_op | source)
XLA Modules:
  0.0 99.8 jit_solution(6383651695226934252)
XLA Ops:
  0.6 2.2 %shard_map.68 = (bf16[1536,128]{1,0:T(8,128)(2,1)}, bf16[16,192]{1,0:T(8,128)(2,1)}) custom-call(s32[8,16]{1,0:T(8,128)} %bitcast.29, bf16[128,768]{1,0:T(8,128)(2,1)} %bitcast.28), custom_call_target="tpu_custom_call" | custom-call | flops 37748736 | bytes 786432 | tf_op jit(solution)/shard_map/pallas_call | solution.py:28
  2.8 14.0 %all-to-all-start = ((bf16[64,24,128]{2,1,0:T(8,128)(2,1)}), bf16[64,24,128]{2,1,0:T(8,128)(2,1)S(1)}, u32[]{:S(2)}, u32[]{:S(2)}) async-start(bf16[64,24,128]{2,1,0:T(8,128)(2,1)} %bitcast.26), calls=%async_computation | async-start | bytes 786432 | tf_op jit(solution)/shard_map/all_to_all | solution.py:201
  16.9 0.1 pad_add_fusion.core_ref.spot_ref
  17.0 2.0 %shard_map.70 = bf16[192,1024]{1,0:T(8,128)(2,1)} custom-call(s32[2]{0:T(128)S(1)} %pad_add_fusion.core_ref.spot_ref, bf16[192,2048]{1,0:T(8,128)(2,1)} %bitcast.22), custom_call_target="tpu_custom_call" | custom-call | bytes 786432 | tf_op jit(solution)/shard_map/pallas_call | solution.py:28
  19.0 6.6 %collective-permute-start = (bf16[192,1024]{1,0:T(8,128)(2,1)}, bf16[192,1024]{1,0:T(8,128)(2,1)S(1)}, u32[]{:S(2)}, u32[]{:S(2)}) collective-permute-start(bf16[192,1024]{1,0:T(8,128)(2,1)} %shard_map.70), channel_id=1, source_target_pairs={{0,64},{64,0},{128,192},{192,128},{256,320},{320,256},{384,448},{4... | collective-permute-start | bytes 1179656 | tf_op jit(solution)/shard_map/ppermute | solution.py:205
  25.6 5.7 %shard_map.69 = (f32[192,768]{1,0:T(8,128)}, f32[192,768]{1,0:T(8,128)}) custom-call(bf16[192,2048]{1,0:T(8,128)(2,1)} %bitcast.23, bf16[2048,768]{1,0:T(8,128)(2,1)} %bitcast.18, bf16[2048,768]{1,0:T(8,128)(2,1)} %bitcast.20), custom_call_target="tpu_custom_call" | custom-call | flops 1207959552 | bytes 12582912 | tf_op jit(solution)/shard_map/pallas_call | solution.py:207
  31.3 0.0 collective-permute-done.partner_ref
  31.4 2.3 %shard_map.71._.xt_ref = bf16[1024,384]{1,0:T(8,128)(2,1)} custom-call(s32[2]{0:T(128)S(1)} %pad_add_fusion.core_ref.spot_ref, bf16[192,2048]{1,0:T(8,128)(2,1)} %bitcast.24, bf16[192,1024]{1,0:T(8,128)(2,1)S(1)} %collective-permute-done.partner_ref), custom_call_target="tpu_custom_call" | custom-call | bytes 1572864 | tf_op jit(solution)/shard_map/pallas_call | solution.py:28
  33.7 0.0 all-to-all-done
  33.7 2.3 %shard_map.72 = (bf16[192,768]{1,0:T(8,128)(2,1)}, bf16[192,768]{1,0:T(8,128)(2,1)}) custom-call(bf16[1536,128]{1,0:T(8,128)(2,1)S(1)} %bitcast.17, f32[192,768]{1,0:T(8,128)} %get-tuple-element.16.fg_ref, f32[192,768]{1,0:T(8,128)} %get-tuple-element.17.fu_ref, bf16[1024,384]{1,0:T(8,128)(2,1)} %shard_map.71._.xt_ref), custom_call_target="tpu_custom_call" | custom-call | bytes 2359296 | tf_op jit(solution)/shard_map/pallas_call | solution.py:28
  36.0 4.2 %collective-permute-start.1 = (bf16[192,768]{1,0:T(8,128)(2,1)}, bf16[192,768]{1,0:T(8,128)(2,1)S(1)}, u32[]{:S(2)}, u32[]{:S(2)}) collective-permute-start(bf16[192,768]{1,0:T(8,128)(2,1)} %get-tuple-element.18.own_ref.dgate_ref), channel_id=1, source_target_pairs={{0,64},{64,0},{128,192},{192,128},{256,320},{320,256},{384,448},{4... | collective-permute-start | bytes 884744 | tf_op jit(solution)/shard_map/ppermute | solution.py:233
  40.3 1.4 %collective-permute-done.1.near_ref = bf16[192,768]{1,0:T(8,128)(2,1)S(1)} collective-permute-done((bf16[192,768]{1,0:T(8,128)(2,1)}, bf16[192,768]{1,0:T(8,128)(2,1)S(1)}, u32[]{:S(2)}, u32[]{:S(2)}) %collective-permute-start.1) | collective-permute-done | bytes 294944 | tf_op jit(solution)/shard_map/ppermute | solution.py:233
  41.7 2.7 %shard_map.73 = (bf16[128,768]{1,0:T(8,128)(2,1)}, bf16[256,768]{1,0:T(8,128)(2,1)}, bf16[256,768]{1,0:T(8,128)(2,1)}) custom-call(bf16[1024,384]{1,0:T(8,128)(2,1)} %shard_map.71._.xt_ref, bf16[192,768]{1,0:T(8,128)(2,1)} %get-tuple-element.18.own_ref.dgate_ref, bf16[192,768]{1,0:T(8,128)(2,1)S(1)} %collective-permute-done.1.near_ref), custom_call_target="tpu_custom_call" | custom-call | flops 377487360 | bytes 983040 | tf_op jit(solution)/shard_map/pallas_call | solution.py:28
  44.4 15.8 %collective-permute-start.2 = (bf16[256,768]{1,0:T(8,128)(2,1)}, bf16[256,768]{1,0:T(8,128)(2,1)S(1)}, u32[]{:S(2)}, u32[]{:S(2)}) collective-permute-start(bf16[256,768]{1,0:T(8,128)(2,1)} %get-tuple-element.22), channel_id=1, source_target_pairs={{0,128},{64,960},{128,256},{192,64},{256,384},{320,192},{384,512},... | collective-permute-start | bytes 1179656 | tf_op jit(solution)/shard_map/ppermute | solution.py:188
  60.2 1.9 %collective-permute-start.4 = (bf16[128,768]{1,0:T(8,128)(2,1)}, bf16[128,768]{1,0:T(8,128)(2,1)S(1)}, u32[]{:S(2)}, u32[]{:S(2)}) collective-permute-start(bf16[128,768]{1,0:T(8,128)(2,1)} %get-tuple-element.20._), channel_id=1, source_target_pairs={{0,256},{64,832},{128,384},{192,960},{256,512},{320,64},{384,640},... | collective-permute-start | bytes 589832 | tf_op jit(solution)/shard_map/ppermute | solution.py:188
  62.2 0.0 copy-start
  62.2 6.3 %shard_map.74 = bf16[3072,128]{1,0:T(8,128)(2,1)} custom-call(bf16[192,768]{1,0:T(8,128)(2,1)} %get-tuple-element.18.own_ref.dgate_ref, bf16[192,768]{1,0:T(8,128)(2,1)} %get-tuple-element.19.dup_ref, bf16[2048,768]{1,0:T(8,128)(2,1)} %bitcast.19, bf16[2048,768]{1,0:T(8,128)(2,1)} %bitcast.21, bf16[128,768]{1,0:T(8,128)(2,1)} %get-tuple-element.20._), custom_call_target="tpu_custom_call" | custom-call | flops 1 | bytes 1 | tf_op jit(solution)/shard_map/pallas_call | solution.py:254
  68.4 7.8 %all-to-all-start.1 = ((bf16[64,48,128]{2,1,0:T(8,128)(2,1)}), bf16[64,48,128]{2,1,0:T(8,128)(2,1)S(1)}, u32[]{:S(2)}, u32[]{:S(2)}) async-start(bf16[64,48,128]{2,1,0:T(8,128)(2,1)} %bitcast.25), calls=%async_computation.1 | async-start | bytes 1572864 | tf_op jit(solution)/shard_map/all_to_all | solution.py:272
  76.3 0.0 copy-done
  76.3 3.1 %collective-permute-start.3 = (bf16[256,768]{1,0:T(8,128)(2,1)S(1)}, bf16[256,768]{1,0:T(8,128)(2,1)S(1)}, u32[]{:S(2)}, u32[]{:S(2)}) collective-permute-start(bf16[256,768]{1,0:T(8,128)(2,1)S(1)} %copy-done), channel_id=1, source_target_pairs={{0,896},{64,192},{128,0},{192,320},{256,128},{320,448},{384,256},{... | collective-permute-start | bytes 1179656 | tf_op jit(solution)/shard_map/ppermute | solution.py:188
  79.4 1.7 %shard_map.76 = (f32[128,768]{1,0:T(8,128)S(1)}, f32[128,768]{1,0:T(8,128)S(1)}, f32[128,768]{1,0:T(8,128)S(1)}) custom-call(bf16[1024,384]{1,0:T(8,128)(2,1)} %shard_map.71._.xt_ref, bf16[192,768]{1,0:T(8,128)(2,1)} %get-tuple-element.18.own_ref.dgate_ref, bf16[192,768]{1,0:T(8,128)(2,1)S(1)} %collective-permute-done.1.near_ref), custom_call_target="tpu_custom_call" | custom-call | flops 1 | bytes 1 | tf_op jit(solution)/shard_map/pallas_call | solution.py:28
  81.1 0.0 collective-permute-done.4.a_ref
  81.1 0.0 collective-permute-done.2.b_ref.a_ref
  81.1 0.1 shard_map.77
  81.2 1.9 %collective-permute-start.5 = (bf16[128,768]{1,0:T(8,128)(2,1)S(1)}, bf16[128,768]{1,0:T(8,128)(2,1)S(1)}, u32[]{:S(2)}, u32[]{:S(2)}) collective-permute-start(bf16[128,768]{1,0:T(8,128)(2,1)S(1)} %shard_map.77), channel_id=1, source_target_pairs={{0,256},{64,832},{128,384},{192,960},{256,512},{320,64},{384,640},... | collective-permute-start | bytes 589832 | tf_op jit(solution)/shard_map/ppermute | solution.py:188
  83.1 3.7 %collective-permute-done.3.a_ref.b_ref = bf16[256,768]{1,0:T(8,128)(2,1)S(1)} collective-permute-done((bf16[256,768]{1,0:T(8,128)(2,1)S(1)}, bf16[256,768]{1,0:T(8,128)(2,1)S(1)}, u32[]{:S(2)}, u32[]{:S(2)}) %collective-permute-start.3) | collective-permute-done | bytes 393248 | tf_op jit(solution)/shard_map/ppermute | solution.py:188
  86.8 4.2 %collective-permute-start.6 = (bf16[128,768]{1,0:T(8,128)(2,1)S(1)}, bf16[128,768]{1,0:T(8,128)(2,1)S(1)}, u32[]{:S(2)}, u32[]{:S(2)}) collective-permute-start(bf16[128,768]{1,0:T(8,128)(2,1)S(1)} %shard_map.78), channel_id=1, source_target_pairs={{0,768},{64,320},{128,896},{192,448},{256,0},{320,576},{384,128},{... | collective-permute-start | bytes 589832 | tf_op jit(solution)/shard_map/ppermute | solution.py:188
  91.0 0.0 collective-permute-done.5.c_ref
  91.0 5.9 %collective-permute-done.6.d_ref = bf16[128,768]{1,0:T(8,128)(2,1)S(1)} collective-permute-done((bf16[128,768]{1,0:T(8,128)(2,1)S(1)}, bf16[128,768]{1,0:T(8,128)(2,1)S(1)}, u32[]{:S(2)}, u32[]{:S(2)}) %collective-permute-start.6) | collective-permute-done | bytes 196640 | tf_op jit(solution)/shard_map/ppermute | solution.py:188
  97.0 0.8 shard_map.79
  97.8 0.0 all-to-all-done.1
  97.8 1.9 %shard_map.75 = bf16[16,2048]{1,0:T(8,128)(2,1)} custom-call(bf16[16,192]{1,0:T(8,128)(2,1)} %get-tuple-element.14.take_ref, bf16[3072,128]{1,0:T(8,128)(2,1)S(1)} %bitcast.16), custom_call_target="tpu_custom_call" | custom-call | flops 12582912 | bytes 786432 | tf_op jit(solution)/shard_map/pallas_call | solution.py:28
  (1 shorter events, 0.0 us)
Async XLA Ops:
  2.8 30.9 %all-to-all-start = ((bf16[64,24,128]{2,1,0:T(8,128)(2,1)}), bf16[64,24,128]{2,1,0:T(8,128)(2,1)S(1)}, u32[]{:S(2)}, u32[]{:S(2)}) async-start(bf16[64,24,128]{2,1,0:T(8,128)(2,1)} %bitcast.26), calls=%async_computation | async-start | bytes 786432 | tf_op jit(solution)/shard_map/all_to_all | solution.py:201
  19.0 12.4 %collective-permute-start = (bf16[192,1024]{1,0:T(8,128)(2,1)}, bf16[192,1024]{1,0:T(8,128)(2,1)S(1)}, u32[]{:S(2)}, u32[]{:S(2)}) collective-permute-start(bf16[192,1024]{1,0:T(8,128)(2,1)} %shard_map.70), channel_id=1, source_target_pairs={{0,64},{64,0},{128,192},{192,128},{256,320},{320,256},{384,448},{4... | collective-permute-start | bytes 1179656 | tf_op jit(solution)/shard_map/ppermute | solution.py:205
  36.0 5.7 %collective-permute-start.1 = (bf16[192,768]{1,0:T(8,128)(2,1)}, bf16[192,768]{1,0:T(8,128)(2,1)S(1)}, u32[]{:S(2)}, u32[]{:S(2)}) collective-permute-start(bf16[192,768]{1,0:T(8,128)(2,1)} %get-tuple-element.18.own_ref.dgate_ref), channel_id=1, source_target_pairs={{0,64},{64,0},{128,192},{192,128},{256,320},{320,256},{384,448},{4... | collective-permute-start | bytes 884744 | tf_op jit(solution)/shard_map/ppermute | solution.py:233
  44.4 36.7 %collective-permute-start.2 = (bf16[256,768]{1,0:T(8,128)(2,1)}, bf16[256,768]{1,0:T(8,128)(2,1)S(1)}, u32[]{:S(2)}, u32[]{:S(2)}) collective-permute-start(bf16[256,768]{1,0:T(8,128)(2,1)} %get-tuple-element.22), channel_id=1, source_target_pairs={{0,128},{64,960},{128,256},{192,64},{256,384},{320,192},{384,512},... | collective-permute-start | bytes 1179656 | tf_op jit(solution)/shard_map/ppermute | solution.py:188
  60.2 20.9 %collective-permute-start.4 = (bf16[128,768]{1,0:T(8,128)(2,1)}, bf16[128,768]{1,0:T(8,128)(2,1)S(1)}, u32[]{:S(2)}, u32[]{:S(2)}) collective-permute-start(bf16[128,768]{1,0:T(8,128)(2,1)} %get-tuple-element.20._), channel_id=1, source_target_pairs={{0,256},{64,832},{128,384},{192,960},{256,512},{320,64},{384,640},... | collective-permute-start | bytes 589832 | tf_op jit(solution)/shard_map/ppermute | solution.py:188
  62.2 14.1 %copy-start = (bf16[256,768]{1,0:T(8,128)(2,1)S(1)}, bf16[256,768]{1,0:T(8,128)(2,1)}, u32[]{:S(2)}) copy-start(bf16[256,768]{1,0:T(8,128)(2,1)} %get-tuple-element.23) | copy-start | bytes 1179652
  68.4 29.4 %all-to-all-start.1 = ((bf16[64,48,128]{2,1,0:T(8,128)(2,1)}), bf16[64,48,128]{2,1,0:T(8,128)(2,1)S(1)}, u32[]{:S(2)}, u32[]{:S(2)}) async-start(bf16[64,48,128]{2,1,0:T(8,128)(2,1)} %bitcast.25), calls=%async_computation.1 | async-start | bytes 1572864 | tf_op jit(solution)/shard_map/all_to_all | solution.py:272
  76.3 10.5 %collective-permute-start.3 = (bf16[256,768]{1,0:T(8,128)(2,1)S(1)}, bf16[256,768]{1,0:T(8,128)(2,1)S(1)}, u32[]{:S(2)}, u32[]{:S(2)}) collective-permute-start(bf16[256,768]{1,0:T(8,128)(2,1)S(1)} %copy-done), channel_id=1, source_target_pairs={{0,896},{64,192},{128,0},{192,320},{256,128},{320,448},{384,256},{... | collective-permute-start | bytes 1179656 | tf_op jit(solution)/shard_map/ppermute | solution.py:188
  81.2 9.9 %collective-permute-start.5 = (bf16[128,768]{1,0:T(8,128)(2,1)S(1)}, bf16[128,768]{1,0:T(8,128)(2,1)S(1)}, u32[]{:S(2)}, u32[]{:S(2)}) collective-permute-start(bf16[128,768]{1,0:T(8,128)(2,1)S(1)} %shard_map.77), channel_id=1, source_target_pairs={{0,256},{64,832},{128,384},{192,960},{256,512},{320,64},{384,640},... | collective-permute-start | bytes 589832 | tf_op jit(solution)/shard_map/ppermute | solution.py:188
  86.8 10.2 %collective-permute-start.6 = (bf16[128,768]{1,0:T(8,128)(2,1)S(1)}, bf16[128,768]{1,0:T(8,128)(2,1)S(1)}, u32[]{:S(2)}, u32[]{:S(2)}) collective-permute-start(bf16[128,768]{1,0:T(8,128)(2,1)S(1)} %shard_map.78), channel_id=1, source_target_pairs={{0,768},{64,320},{128,896},{192,448},{256,0},{320,576},{384,128},{... | collective-permute-start | bytes 589832 | tf_op jit(solution)/shard_map/ppermute | solution.py:188

commit v3 on v2

--- a/solution.py
+++ b/solution.py
@@ -14,7 +14,7 @@
 
 
 def call(body, outs, ins, scratch=(), flops=0, moved=0, near=False, vmem=16):
-    specs = {"h": pl.BlockSpec(), "v": pl.BlockSpec(memory_space=pltpu.VMEM)}
+    specs = {"h": pl.BlockSpec(), "d": pl.BlockSpec(), "v": pl.BlockSpec(memory_space=pltpu.VMEM)}
     specs |= {"s": pl.BlockSpec(memory_space=pltpu.SMEM), "u": pl.BlockSpec(memory_space=pl.ANY)}
     kernel = pl.pallas_call(
         body,
@@ -73,18 +73,19 @@
         out_ref[:, z * LANES : (z + 1) * LANES] = x_ref[:, pl.ds(start, LANES)]
 
 
-def by_role(roles, spot_ref, x_ref, partner_ref, out_ref):
+def by_role(roles, spot_ref, x_ref, partner_ref, *outs):
     core, z = spot_ref[0], spot_ref[1]
     chips = partner_ref.shape[1] // LANES
-    rows = x_ref.shape[0]
+    rows, apart = x_ref.shape[0], outs[0].shape[1] // 2
+    places = [(out, n) for out in outs for n in range(0, out.shape[0], LANES)]
     sign = 1 - 2 * core
-    for n, offset in enumerate(roles):
+    for offset, (out_ref, n) in zip(roles, places):
         chip = lax.rem(z + sign * offset + chips, chips)
         start = pl.multiple_of((2 * chip + core) * LANES, LANES)
         own = x_ref[:, pl.ds(start, LANES)].astype(F32)
         near = partner_ref[:, pl.ds(pl.multiple_of(chip * LANES, LANES), LANES)].astype(F32)
-        both = jnp.concatenate([own, near], axis=0)
-        out_ref[n * LANES : (n + 1) * LANES, :] = both.T.astype(BF)
+        out_ref[n : n + LANES, :rows] = own.T.astype(BF)
+        out_ref[n : n + LANES, apart : apart + rows] = near.T.astype(BF)
 
 
 def factors(x_ref, wg_ref, wu_ref, fg_ref, fu_ref):
@@ -108,29 +109,41 @@
             dup_ref[at] = (piece * fu_ref[at]).astype(BF)
 
 
-def input_grads(peers, cap, steps, dgate_ref, dup_ref, wg_ref, wu_ref, _, out_ref, wide_ref):
-    step = pl.program_id(0)
-    back = lax.dot_general(dgate_ref[...], wg_ref[...], NT, preferred_element_type=F32)
-    back = back + lax.dot_general(dup_ref[...], wu_ref[...], NT, preferred_element_type=F32)
+def input_grads(peers, cap, steps, dgate_ref, dup_ref, wg_ref, wu_hbm, out_ref, wide_ref, wu_ref, sems):
+    width = wu_ref.shape[0] // steps
+    copies = [
+        pltpu.make_async_copy(wu_hbm.at[pl.ds(n * width, width)], wu_ref.at[pl.ds(n * width, width)], sems.at[n])
+        for n in range(steps)
+    ]
+    for copy in copies:
+        copy.start()
     rows = wide_ref.shape[0] // peers
-    cols = back.shape[1] // LANES
-    for j in range(cap):
-        for c in range(cols):
-            at = j * (rows // cap) + step * cols + c
-            wide_ref[pl.ds(at, peers, stride=rows), :] = back[
-                j * peers : (j + 1) * peers, c * LANES : (c + 1) * LANES
-            ]
-
-    @pl.when(step == steps - 1)
-    def _():
-        out_ref[...] = wide_ref[...].astype(BF)
-
-
-def partials(first, sizes, xt_ref, own_ref, near_ref, *outs):
+    cols = width // LANES
+    for weight_ref, grad_ref in ((wg_ref, dgate_ref), (wu_ref, dup_ref)):
+        for n in range(steps):
+            if weight_ref is wu_ref:
+                copies[n].wait()
+            back = lax.dot_general(
+                grad_ref[...], weight_ref[n * width : (n + 1) * width, :], NT, preferred_element_type=F32
+            )
+            for j in range(cap):
+                for c in range(cols):
+                    at = pl.ds(j * (rows // cap) + n * cols + c, peers, stride=rows)
+                    piece = back[j * peers : (j + 1) * peers, c * LANES : (c + 1) * LANES]
+                    wide_ref[at, :] = wide_ref[at, :] + piece if weight_ref is wu_ref else piece
+    out_ref[...] = wide_ref[...].astype(BF)
+
+
+def tie(back_ref, _, out_ref):
+    pass
+
+
+def partials(sizes, unread, xt_ref, own_ref, near_ref, *refs):
+    outs = refs[unread:]
     rows = own_ref.shape[0]
-    xt = xt_ref[first * LANES : (first + sum(sizes)) * LANES, :]
-    total = jnp.dot(xt[:, :rows], own_ref[...], preferred_element_type=F32)
-    total = total + jnp.dot(xt[:, rows:], near_ref[...], preferred_element_type=F32)
+    apart = xt_ref.shape[1] // 2
+    total = jnp.dot(xt_ref[:, :rows], own_ref[...], preferred_element_type=F32)
+    total = total + jnp.dot(xt_ref[:, apart : apart + rows], near_ref[...], preferred_element_type=F32)
     at = 0
     for size, out in zip(sizes, outs):
         out[...] = total[at * LANES : (at + size) * LANES].astype(out.dtype)
@@ -145,7 +158,7 @@
     out_ref[...] = (part_ref[...] + a_ref[:LANES].astype(F32)).astype(BF)
 
 
-def total_of(part_ref, a_ref, b_ref, c_ref, d_ref, out_ref):
+def total_of(part_ref, a_ref, b_ref, c_ref, d_ref, _, out_ref):
     near = a_ref[LANES:].astype(F32) + b_ref[LANES:].astype(F32)
     far = c_ref[...].astype(F32) + d_ref[...].astype(F32)
     out_ref[...] = part_ref[...] + near + far
@@ -219,73 +232,79 @@
             flops=4 * slot_rows * width * hidden, bytes_accessed=8 * width * hidden, transcendentals=slot_rows * hidden
         ),
     )(far(x), far(w_gate), far(w_up))
-    x_roles = call(
-        functools.partial(by_role, ROLES), sds((len(ROLES) * LANES, 2 * slot_rows), BF), "shv", moved=8 * slot_rows * half
+    apart = -(-slot_rows // LANES) * LANES
+    x_sent, x_kept = call(
+        functools.partial(by_role, ROLES),
+        (sds((5 * LANES, 2 * apart), BF), sds((3 * LANES, 2 * apart), BF)),
+        "shv",
+        moved=8 * slot_rows * half,
     )(spot, x, borrowed)
 
     dgate, dup = call(
         functools.partial(hidden_grads, peers, cap),
         (sds((slot_rows, hidden), BF),) * 2,
-        "vhhu",
+        "hhhu",
         [pltpu.VMEM((peers * in_rows, LANES), F32)],
         moved=16 * slot_rows * hidden,
-    )(arrived.reshape(peers * in_rows, LANES), f_gate, f_up, x_roles)
+        near=True,
+    )(arrived.reshape(peers * in_rows, LANES), f_gate, f_up, x_sent)
     dgate_near = swap(dgate)
 
+    out_rows = cap * width // LANES
+    steps = 4
+    back = call(
+        functools.partial(input_grads, peers, cap, steps),
+        sds((peers * out_rows, LANES), BF),
+        "vvvu",
+        [
+            pltpu.VMEM((peers * out_rows, LANES), F32),
+            pltpu.VMEM((width, hidden), BF),
+            pltpu.SemaphoreType.DMA((steps,)),
+        ],
+        flops=1,
+        moved=1,
+    )(dgate, dup, w_gate, w_up)
     block, blocks, wide_block = (sds((n * LANES, hidden), t) for n, t in ((1, BF), (2, BF), (1, F32)))
     work = 4 * LANES * slot_rows * hidden
     most, right, left = call(
-        functools.partial(partials, 0, (1, 2, 2)), (block, blocks, blocks), "hhv", flops=5 * work, moved=10 * LANES * hidden
-    )(x_roles, dgate, dgate_near)
+        functools.partial(partials, (1, 2, 2), 1), (block, blocks, blocks), "hvvu", flops=5 * work, moved=10 * LANES * hidden, near=True
+    )(x_sent, dgate, dgate_near, back)
     most_in = along_z(most, 2)
     right_in = along_z(right, 1)
     left_in = along_z(left, -1)
     p2, p2n, p0 = call(
-        functools.partial(partials, 5, (1, 1, 1)),
+        functools.partial(partials, (1, 1, 1), 0),
         (wide_block,) * 3,
-        "hhv",
+        "hvv",
         flops=1,
         moved=1,
         near=True,
-    )(x_roles, dgate, dgate_near)
-
-    out_rows = cap * width // LANES
-    steps = width // 512
+    )(x_kept, dgate, dgate_near)
+
     back = pl.pallas_call(
-        functools.partial(input_grads, peers, cap, steps),
-        grid=(steps,),
-        out_shape=pltpu.HBM((peers * out_rows, LANES), BF),
-        in_specs=[
-            pl.BlockSpec((slot_rows, hidden), lambda i: (0, 0)),
-            pl.BlockSpec((slot_rows, hidden), lambda i: (0, 0)),
-            pl.BlockSpec((512, hidden), lambda i: (i, 0)),
-            pl.BlockSpec((512, hidden), lambda i: (i, 0)),
-            pl.BlockSpec(memory_space=pl.ANY),
-        ],
-        out_specs=pl.BlockSpec((peers * out_rows, LANES), lambda i: (0, 0)),
-        scratch_shapes=[pltpu.VMEM((peers * out_rows, LANES), F32)],
-        compiler_params=pltpu.CompilerParams(vmem_limit_bytes=24 * MIB),
-        cost_estimate=pl.CostEstimate(
-            flops=1, bytes_accessed=1, transcendentals=0
-        ),
-    )(far(dgate), far(dup), far(w_gate), far(w_up), far(most))
+        tie,
+        out_shape=pltpu.HBM(back.shape, BF),
+        in_specs=[pl.BlockSpec(memory_space=pl.ANY)] * 2,
+        out_specs=pl.BlockSpec(memory_space=pl.ANY),
+        input_output_aliases={0: 0},
+        cost_estimate=pl.CostEstimate(flops=1, bytes_accessed=1, transcendentals=0),
+    )(far(back), most)
     returned = lax.all_to_all(back.reshape(peers, out_rows, LANES), "expert", 0, 0, tiled=True)
 
     moved = 10 * LANES * hidden
     right_sum = along_z(call(add_two, block, "vvv", flops=20_000_000_000, moved=moved, near=True)(p2, most_in, right_in), 2)
     left_sum = along_z(call(add_one, block, "vv", flops=20_000_000_000, moved=moved, near=True)(p2n, left_in), -2)
-    grad_gate = call(total_of, wide_block, "vvvvv", moved=2 * moved, near=False)(
-        p0, right_in, left_in, right_sum, left_sum
-    )
-
     grad_tokens = call(
         functools.partial(combine, peers, cap),
         sds((tokens, width), BF),
-        "hv",
+        "vv",
         [pltpu.VMEM((peers * out_rows, LANES), F32)],
-        flops=2 * tokens * slot_rows * width,
-        moved=2 * slot_rows * width,
+        flops=1,
+        moved=1,
     )(take, returned.reshape(peers * out_rows, LANES))
+    grad_gate = call(total_of, wide_block, "vvvvvu", moved=2 * moved)(
+        p0, right_in, left_in, right_sum, left_sum, grad_tokens
+    )
     return (grad_tokens, grad_gate[None])
 
 

time: 101 us -> 97.6 us (0.966)
  Pallas kernels: 28.2 us -> 24.8 us
  waiting for transfers between devices: 11 us -> 9.08 us
  local copies, waits for them, and re-layouts: 0.01 us -> 1.49 us
    pallas_call x1, Pallas kernels: 6.26 us -> 0.01 us  [on_device(): pl.pallas_call(tie, out_shape=pltpu.HBM(back.shape, BF), in_specs=[pl.Blo...]
    ppermute x5, waiting for transfers between devices: 9.61 us -> 3.81 us  [along_z(): return lax.ppermute(value, 'dp', pairs)]
    all_to_all x1, waiting for transfers between devices: 0.01 us -> 5.26 us  [on_device(): lax.all_to_all(back.reshape(peers, out_rows, LANES), 'expert', 0, 0, tile...]
    pallas_call x10 -> x11, Pallas kernels: 16.2 us -> 19.1 us  [call(): kernel(*(far(v) if kind in 'hu' else v for kind, v in zip(ins, given)))]
    unnamed x2 -> x12, local copies, waits for them, and re-layouts: 0.01 us -> 1.49 us
    ppermute x1, waiting for transfers between devices: 1.4 us -> 0.01 us  [on_device(): dgate_near = swap(dgate)]
  transfers between devices with their start and end apart: 9 -> 9, of which waited for: 3 -> 2; matrix products, arithmetic and copies ran while one was open for 0% -> 0% of each run, Pallas kernels for 19% -> 18%
where the time goes in v3:
time: 97.6 us; the launch traced here: 95.8 us
  starting transfers between devices  59.5 us (61%)
  Pallas kernels  24.8 us (25%)
  waiting for transfers between devices  9.08 us (9%)
  local copies, waits for them, and re-layouts  1.49 us (2%)
    ppermute x5, starting transfers between devices, along_z(): return lax.ppermute(value, 'dp', pairs)  27.1 us
    pallas_call x11, Pallas kernels, call(): kernel(*(far(v) if kind in 'hu' else v for kind, v in zip(ins, given)))  19.1 us
    all_to_all x1, starting transfers between devices, on_device(): lax.all_to_all(outgoing.reshape(peers, in_rows, LANES), 'expert', 0, 0, t...  14 us
    all_to_all x1, starting transfers between devices, on_device(): lax.all_to_all(back.reshape(peers, out_rows, LANES), 'expert', 0, 0, tile...  7.73 us
    ppermute x1, starting transfers between devices, on_device(): borrowed = swap(lent)  6.64 us
    pallas_call x1, Pallas kernels, on_device(): pl.pallas_call(factors, grid=(parts,), out_shape=(pltpu.HBM((slot_rows, h...  5.73 us
    all_to_all x1, waiting for transfers between devices, on_device(): lax.all_to_all(back.reshape(peers, out_rows, LANES), 'expert', 0, 0, tile...  5.26 us
    ppermute x1, starting transfers between devices, on_device(): dgate_near = swap(dgate)  4.01 us
  transfers between devices with their start and end apart: 9, of which 2 were waited for; matrix products, arithmetic and copies ran while one was open for 0% of the time, Pallas kernels for 18%

profile of v3, /device:TPU:1, one launch (start us, length us, event | category | flops | bytes accessed | tf_op | source)
XLA Modules:
  0.0 95.8 jit_solution(2851588535240141466)
XLA Ops:
  0.6 2.2 %shard_map.68 = (bf16[1536,128]{1,0:T(8,128)(2,1)}, bf16[16,192]{1,0:T(8,128)(2,1)}) custom-call(s32[8,16]{1,0:T(8,128)} %bitcast.29, bf16[128,768]{1,0:T(8,128)(2,1)} %bitcast.28), custom_call_target="tpu_custom_call" | custom-call | flops 37748736 | bytes 786432 | tf_op jit(solution)/shard_map/pallas_call | solution.py:28
  2.8 14.0 %all-to-all-start = ((bf16[64,24,128]{2,1,0:T(8,128)(2,1)}), bf16[64,24,128]{2,1,0:T(8,128)(2,1)S(1)}, u32[]{:S(2)}, u32[]{:S(2)}) async-start(bf16[64,24,128]{2,1,0:T(8,128)(2,1)} %bitcast.26), calls=%async_computation | async-start | bytes 786432 | tf_op jit(solution)/shard_map/all_to_all | solution.py:214
  16.9 0.1 pad_add_fusion.core_ref.spot_ref
  17.0 2.0 %shard_map.70 = bf16[192,1024]{1,0:T(8,128)(2,1)} custom-call(s32[2]{0:T(128)S(1)} %pad_add_fusion.core_ref.spot_ref, bf16[192,2048]{1,0:T(8,128)(2,1)} %bitcast.22), custom_call_target="tpu_custom_call" | custom-call | bytes 786432 | tf_op jit(solution)/shard_map/pallas_call | solution.py:28
  19.0 6.6 %collective-permute-start = (bf16[192,1024]{1,0:T(8,128)(2,1)}, bf16[192,1024]{1,0:T(8,128)(2,1)S(1)}, u32[]{:S(2)}, u32[]{:S(2)}) collective-permute-start(bf16[192,1024]{1,0:T(8,128)(2,1)} %shard_map.70), channel_id=1, source_target_pairs={{0,64},{64,0},{128,192},{192,128},{256,320},{320,256},{384,448},{4... | collective-permute-start | bytes 1179656 | tf_op jit(solution)/shard_map/ppermute | solution.py:218
  25.6 5.7 %shard_map.69 = (f32[192,768]{1,0:T(8,128)}, f32[192,768]{1,0:T(8,128)}) custom-call(bf16[192,2048]{1,0:T(8,128)(2,1)} %bitcast.23, bf16[2048,768]{1,0:T(8,128)(2,1)} %bitcast.16, bf16[2048,768]{1,0:T(8,128)(2,1)} %bitcast.19), custom_call_target="tpu_custom_call" | custom-call | flops 1207959552 | bytes 12582912 | tf_op jit(solution)/shard_map/pallas_call | solution.py:220
  31.4 0.0 copy-start
  31.4 0.0 collective-permute-done.partner_ref
  31.4 2.6 %shard_map.71 = (bf16[640,512]{1,0:T(8,128)(2,1)}, bf16[384,512]{1,0:T(8,128)(2,1)}) custom-call(s32[2]{0:T(128)S(1)} %pad_add_fusion.core_ref.spot_ref, bf16[192,2048]{1,0:T(8,128)(2,1)} %bitcast.24, bf16[192,1024]{1,0:T(8,128)(2,1)S(1)} %collective-permute-done.partner_ref), custom_call_target="tpu_custom_call" | custom-call | bytes 1572864 | tf_op jit(solution)/shard_map/pallas_call | solution.py:28
  34.0 0.0 all-to-all-done
  34.0 0.0 copy-start.5
  34.0 0.7 copy-done.5
  34.7 1.6 %shard_map.72 = (bf16[192,768]{1,0:T(8,128)(2,1)S(1)}, bf16[192,768]{1,0:T(8,128)(2,1)S(1)}) custom-call(bf16[1536,128]{1,0:T(8,128)(2,1)} %bitcast.25, f32[192,768]{1,0:T(8,128)} %get-tuple-element.18.fg_ref, f32[192,768]{1,0:T(8,128)} %get-tuple-element.19.fu_ref, bf16[640,512]{1,0:T(8,128)(2,1)} %get-tuple-element.20._.xt_ref), custom_call_target="tpu_custom_call" | custom-call | bytes 2359296 | tf_op jit(solution)/shard_map/pallas_call | solution.py:28
  36.3 4.0 %collective-permute-start.1 = (bf16[192,768]{1,0:T(8,128)(2,1)S(1)}, bf16[192,768]{1,0:T(8,128)(2,1)S(1)}, u32[]{:S(2)}, u32[]{:S(2)}) collective-permute-start(bf16[192,768]{1,0:T(8,128)(2,1)S(1)} %get-tuple-element.21.dgate_ref.own_ref), channel_id=1, source_target_pairs={{0,64},{64,0},{128,192},{192,128},{256,320},{320,256},{384,448},{4... | collective-permute-start | bytes 884744 | tf_op jit(solution)/shard_map/ppermute | solution.py:251
  40.3 0.0 copy-done
  40.3 4.6 %shard_map.73.refs_0_.back_ref = bf16[3072,128]{1,0:T(8,128)(2,1)} custom-call(bf16[192,768]{1,0:T(8,128)(2,1)S(1)} %get-tuple-element.21.dgate_ref.own_ref, bf16[192,768]{1,0:T(8,128)(2,1)S(1)} %get-tuple-element.22.dup_ref, bf16[2048,768]{1,0:T(8,128)(2,1)S(1)} %bitcast.17, bf16[2048,768]{1,0:T(8,128)(2,1)} %bitcast.20), custom_call_target="tpu_custom_call" | custom-call | flops 1 | bytes 1 | tf_op jit(solution)/shard_map/pallas_call | solution.py:28
  44.9 0.0 collective-permute-done.1.near_ref
  44.9 2.4 %shard_map.74 = (bf16[128,768]{1,0:T(8,128)(2,1)S(1)}, bf16[256,768]{1,0:T(8,128)(2,1)}, bf16[256,768]{1,0:T(8,128)(2,1)S(1)}) custom-call(bf16[640,512]{1,0:T(8,128)(2,1)} %get-tuple-element.20._.xt_ref, bf16[192,768]{1,0:T(8,128)(2,1)S(1)} %get-tuple-element.21.dgate_ref.own_ref, bf16[192,768]{1,0:T(8,128)(2,1)S(1)} %collective-permute-done.1.near_ref, ...), custom_call_target="tpu_custom_call" | custom-call | flops 377487360 | bytes 983040 | tf_op jit(solution)/shard_map/pallas_call | solution.py:28
  47.4 0.0 copy-start.1
  47.4 0.7 copy-done.1
  48.1 0.0 copy-start.3
  48.1 0.0 copy-start.2
  48.1 16.0 %collective-permute-start.2 = (bf16[256,768]{1,0:T(8,128)(2,1)}, bf16[256,768]{1,0:T(8,128)(2,1)S(1)}, u32[]{:S(2)}, u32[]{:S(2)}) collective-permute-start(bf16[256,768]{1,0:T(8,128)(2,1)} %get-tuple-element.26), channel_id=1, source_target_pairs={{0,128},{64,960},{128,256},{192,64},{256,384},{320,192},{384,512},... | collective-permute-start | bytes 1179656 | tf_op jit(solution)/shard_map/ppermute | solution.py:201
  64.1 1.9 %collective-permute-start.4 = (bf16[128,768]{1,0:T(8,128)(2,1)S(1)}, bf16[128,768]{1,0:T(8,128)(2,1)S(1)}, u32[]{:S(2)}, u32[]{:S(2)}) collective-permute-start(bf16[128,768]{1,0:T(8,128)(2,1)S(1)} %get-tuple-element.23._), channel_id=1, source_target_pairs={{0,256},{64,832},{128,384},{192,960},{256,512},{320,64},{384,640},... | collective-permute-start | bytes 589832 | tf_op jit(solution)/shard_map/ppermute | solution.py:201
  66.0 0.0 copy-done.3
  66.0 7.7 %all-to-all-start.1 = ((bf16[64,48,128]{2,1,0:T(8,128)(2,1)}), bf16[64,48,128]{2,1,0:T(8,128)(2,1)S(1)}, u32[]{:S(2)}, u32[]{:S(2)}) async-start(bf16[64,48,128]{2,1,0:T(8,128)(2,1)} %bitcast.21), calls=%async_computation.1 | async-start | bytes 1572864 | tf_op jit(solution)/shard_map/all_to_all | solution.py:292
  73.8 3.1 %collective-permute-start.3 = (bf16[256,768]{1,0:T(8,128)(2,1)S(1)}, bf16[256,768]{1,0:T(8,128)(2,1)S(1)}, u32[]{:S(2)}, u32[]{:S(2)}) collective-permute-start(bf16[256,768]{1,0:T(8,128)(2,1)S(1)} %get-tuple-element.27), channel_id=1, source_target_pairs={{0,896},{64,192},{128,0},{192,320},{256,128},{320,448},{384,256},{... | collective-permute-start | bytes 1179656 | tf_op jit(solution)/shard_map/ppermute | solution.py:201
  76.9 0.0 copy-done.2
  76.9 1.5 %shard_map.77 = (f32[128,768]{1,0:T(8,128)S(1)}, f32[128,768]{1,0:T(8,128)S(1)}, f32[128,768]{1,0:T(8,128)S(1)}) custom-call(bf16[384,512]{1,0:T(8,128)(2,1)} %get-tuple-element.24.xt_ref, bf16[192,768]{1,0:T(8,128)(2,1)S(1)} %get-tuple-element.21.dgate_ref.own_ref, bf16[192,768]{1,0:T(8,128)(2,1)S(1)} %copy-done.2), custom_call_target="tpu_custom_call" | custom-call | flops 1 | bytes 1 | tf_op jit(solution)/shard_map/pallas_call | solution.py:28
  78.3 0.0 collective-permute-done.4.a_ref
  78.3 0.0 collective-permute-done.2.b_ref.a_ref
  78.3 0.1 shard_map.78
  78.4 1.9 %collective-permute-start.5 = (bf16[128,768]{1,0:T(8,128)(2,1)S(1)}, bf16[128,768]{1,0:T(8,128)(2,1)S(1)}, u32[]{:S(2)}, u32[]{:S(2)}) collective-permute-start(bf16[128,768]{1,0:T(8,128)(2,1)S(1)} %shard_map.78), channel_id=1, source_target_pairs={{0,256},{64,832},{128,384},{192,960},{256,512},{320,64},{384,640},... | collective-permute-start | bytes 589832 | tf_op jit(solution)/shard_map/ppermute | solution.py:201
  80.3 3.8 %collective-permute-done.3.a_ref.b_ref = bf16[256,768]{1,0:T(8,128)(2,1)S(1)} collective-permute-done((bf16[256,768]{1,0:T(8,128)(2,1)S(1)}, bf16[256,768]{1,0:T(8,128)(2,1)S(1)}, u32[]{:S(2)}, u32[]{:S(2)}) %collective-permute-start.3) | collective-permute-done | bytes 393248 | tf_op jit(solution)/shard_map/ppermute | solution.py:201
  84.1 0.0 copy-start.4
  84.2 4.2 %collective-permute-start.6 = (bf16[128,768]{1,0:T(8,128)(2,1)S(1)}, bf16[128,768]{1,0:T(8,128)(2,1)S(1)}, u32[]{:S(2)}, u32[]{:S(2)}) collective-permute-start(bf16[128,768]{1,0:T(8,128)(2,1)S(1)} %shard_map.79), channel_id=1, source_target_pairs={{0,768},{64,320},{128,896},{192,448},{256,0},{320,576},{384,128},{... | collective-permute-start | bytes 589832 | tf_op jit(solution)/shard_map/ppermute | solution.py:201
  88.4 5.3 %all-to-all-done.1 = bf16[64,48,128]{2,1,0:T(8,128)(2,1)S(1)} async-done(((bf16[64,48,128]{2,1,0:T(8,128)(2,1)}), bf16[64,48,128]{2,1,0:T(8,128)(2,1)S(1)}, u32[]{:S(2)}, u32[]{:S(2)}) %all-to-all-start.1) | async-done | bytes 786464 | tf_op jit(solution)/shard_map/all_to_all | solution.py:292
  93.6 0.0 copy-done.4
  93.6 1.3 %shard_map.76._ = bf16[16,2048]{1,0:T(8,128)(2,1)} custom-call(bf16[16,192]{1,0:T(8,128)(2,1)S(1)} %copy-done.4, bf16[3072,128]{1,0:T(8,128)(2,1)S(1)} %bitcast.18), custom_call_target="tpu_custom_call" | custom-call | flops 1 | bytes 1 | tf_op jit(solution)/shard_map/pallas_call | solution.py:28
  94.9 0.0 collective-permute-done.5.c_ref
  94.9 0.0 collective-permute-done.6.d_ref
  94.9 0.9 shard_map.80
  (2 shorter events, 0.0 us)
Async XLA Ops:
  2.8 31.1 %all-to-all-start = ((bf16[64,24,128]{2,1,0:T(8,128)(2,1)}), bf16[64,24,128]{2,1,0:T(8,128)(2,1)S(1)}, u32[]{:S(2)}, u32[]{:S(2)}) async-start(bf16[64,24,128]{2,1,0:T(8,128)(2,1)} %bitcast.26), calls=%async_computation | async-start | bytes 786432 | tf_op jit(solution)/shard_map/all_to_all | solution.py:214
  19.0 12.4 %collective-permute-start = (bf16[192,1024]{1,0:T(8,128)(2,1)}, bf16[192,1024]{1,0:T(8,128)(2,1)S(1)}, u32[]{:S(2)}, u32[]{:S(2)}) collective-permute-start(bf16[192,1024]{1,0:T(8,128)(2,1)} %shard_map.70), channel_id=1, source_target_pairs={{0,64},{64,0},{128,192},{192,128},{256,320},{320,256},{384,448},{4... | collective-permute-start | bytes 1179656 | tf_op jit(solution)/shard_map/ppermute | solution.py:218
  31.4 8.9 %copy-start = (bf16[1,2048,768]{2,1,0:T(8,128)(2,1)S(1)}, bf16[1,2048,768]{2,1,0:T(8,128)(2,1)}, u32[]{:S(2)}) copy-start(bf16[1,2048,768]{2,1,0:T(8,128)(2,1)} %param.8) | copy-start | bytes 9437188
  34.0 0.7 copy-start.5
  36.3 8.6 %collective-permute-start.1 = (bf16[192,768]{1,0:T(8,128)(2,1)S(1)}, bf16[192,768]{1,0:T(8,128)(2,1)S(1)}, u32[]{:S(2)}, u32[]{:S(2)}) collective-permute-start(bf16[192,768]{1,0:T(8,128)(2,1)S(1)} %get-tuple-element.21.dgate_ref.own_ref), channel_id=1, source_target_pairs={{0,64},{64,0},{128,192},{192,128},{256,320},{320,256},{384,448},{4... | collective-permute-start | bytes 884744 | tf_op jit(solution)/shard_map/ppermute | solution.py:251
  47.4 0.7 copy-start.1
  48.1 17.9 %copy-start.3 = (bf16[128,768]{1,0:T(8,128)(2,1)}, bf16[128,768]{1,0:T(8,128)(2,1)S(1)}, u32[]{:S(2)}) copy-start(bf16[128,768]{1,0:T(8,128)(2,1)S(1)} %get-tuple-element.23._) | copy-start | bytes 589828
  48.1 28.8 %copy-start.2 = (bf16[192,768]{1,0:T(8,128)(2,1)S(1)}, bf16[192,768]{1,0:T(8,128)(2,1)}, u32[]{:S(2)}) copy-start(bf16[192,768]{1,0:T(8,128)(2,1)} %copy-done.1) | copy-start | bytes 884740
  48.1 30.2 %collective-permute-start.2 = (bf16[256,768]{1,0:T(8,128)(2,1)}, bf16[256,768]{1,0:T(8,128)(2,1)S(1)}, u32[]{:S(2)}, u32[]{:S(2)}) collective-permute-start(bf16[256,768]{1,0:T(8,128)(2,1)} %get-tuple-element.26), channel_id=1, source_target_pairs={{0,128},{64,960},{128,256},{192,64},{256,384},{320,192},{384,512},... | collective-permute-start | bytes 1179656 | tf_op jit(solution)/shard_map/ppermute | solution.py:201
  64.1 14.3 %collective-permute-start.4 = (bf16[128,768]{1,0:T(8,128)(2,1)S(1)}, bf16[128,768]{1,0:T(8,128)(2,1)S(1)}, u32[]{:S(2)}, u32[]{:S(2)}) collective-permute-start(bf16[128,768]{1,0:T(8,128)(2,1)S(1)} %get-tuple-element.23._), channel_id=1, source_target_pairs={{0,256},{64,832},{128,384},{192,960},{256,512},{320,64},{384,640},... | collective-permute-start | bytes 589832 | tf_op jit(solution)/shard_map/ppermute | solution.py:201
  66.0 27.6 %all-to-all-start.1 = ((bf16[64,48,128]{2,1,0:T(8,128)(2,1)}), bf16[64,48,128]{2,1,0:T(8,128)(2,1)S(1)}, u32[]{:S(2)}, u32[]{:S(2)}) async-start(bf16[64,48,128]{2,1,0:T(8,128)(2,1)} %bitcast.21), calls=%async_computation.1 | async-start | bytes 1572864 | tf_op jit(solution)/shard_map/all_to_all | solution.py:292
  73.8 10.4 %collective-permute-start.3 = (bf16[256,768]{1,0:T(8,128)(2,1)S(1)}, bf16[256,768]{1,0:T(8,128)(2,1)S(1)}, u32[]{:S(2)}, u32[]{:S(2)}) collective-permute-start(bf16[256,768]{1,0:T(8,128)(2,1)S(1)} %get-tuple-element.27), channel_id=1, source_target_pairs={{0,896},{64,192},{128,0},{192,320},{256,128},{320,448},{384,256},{... | collective-permute-start | bytes 1179656 | tf_op jit(solution)/shard_map/ppermute | solution.py:201
  78.4 16.5 %collective-permute-start.5 = (bf16[128,768]{1,0:T(8,128)(2,1)S(1)}, bf16[128,768]{1,0:T(8,128)(2,1)S(1)}, u32[]{:S(2)}, u32[]{:S(2)}) collective-permute-start(bf16[128,768]{1,0:T(8,128)(2,1)S(1)} %shard_map.78), channel_id=1, source_target_pairs={{0,256},{64,832},{128,384},{192,960},{256,512},{320,64},{384,640},... | collective-permute-start | bytes 589832 | tf_op jit(solution)/shard_map/ppermute | solution.py:201
  84.1 9.5 %copy-start.4 = (bf16[16,192]{1,0:T(8,128)(2,1)S(1)}, bf16[16,192]{1,0:T(8,128)(2,1)}, u32[]{:S(2)}) copy-start(bf16[16,192]{1,0:T(8,128)(2,1)} %get-tuple-element.16.take_ref) | copy-start | bytes 18436
  84.2 10.7 %collective-permute-start.6 = (bf16[128,768]{1,0:T(8,128)(2,1)S(1)}, bf16[128,768]{1,0:T(8,128)(2,1)S(1)}, u32[]{:S(2)}, u32[]{:S(2)}) collective-permute-start(bf16[128,768]{1,0:T(8,128)(2,1)S(1)} %shard_map.79), channel_id=1, source_target_pairs={{0,768},{64,320},{128,896},{192,448},{256,0},{320,576},{384,128},{... | collective-permute-start | bytes 589832 | tf_op jit(solution)/shard_map/ppermute | solution.py:201

commit v4 on v3

--- a/solution.py
+++ b/solution.py
@@ -15,7 +15,7 @@
 
 def call(body, outs, ins, scratch=(), flops=0, moved=0, near=False, vmem=16):
     specs = {"h": pl.BlockSpec(), "d": pl.BlockSpec(), "v": pl.BlockSpec(memory_space=pltpu.VMEM)}
-    specs |= {"s": pl.BlockSpec(memory_space=pltpu.SMEM), "u": pl.BlockSpec(memory_space=pl.ANY)}
+    specs |= {"s": pl.BlockSpec(memory_space=pltpu.SMEM), "u": pl.BlockSpec(memory_space=pl.ANY), "o": pl.BlockSpec(memory_space=pl.ANY)}
     kernel = pl.pallas_call(
         body,
         out_shape=outs if near else jax.tree.map(lambda out: pltpu.HBM(out.shape, out.dtype), outs),
@@ -73,13 +73,12 @@
         out_ref[:, z * LANES : (z + 1) * LANES] = x_ref[:, pl.ds(start, LANES)]
 
 
-def by_role(roles, spot_ref, x_ref, partner_ref, *outs):
+def by_role(roles, spot_ref, x_ref, partner_ref, out_ref):
     core, z = spot_ref[0], spot_ref[1]
     chips = partner_ref.shape[1] // LANES
-    rows, apart = x_ref.shape[0], outs[0].shape[1] // 2
-    places = [(out, n) for out in outs for n in range(0, out.shape[0], LANES)]
+    rows, apart = x_ref.shape[0], out_ref.shape[1] // 2
     sign = 1 - 2 * core
-    for offset, (out_ref, n) in zip(roles, places):
+    for n, offset in zip(range(0, out_ref.shape[0], LANES), roles):
         chip = lax.rem(z + sign * offset + chips, chips)
         start = pl.multiple_of((2 * chip + core) * LANES, LANES)
         own = x_ref[:, pl.ds(start, LANES)].astype(F32)
@@ -109,59 +108,57 @@
             dup_ref[at] = (piece * fu_ref[at]).astype(BF)
 
 
-def input_grads(peers, cap, steps, dgate_ref, dup_ref, wg_ref, wu_hbm, out_ref, wide_ref, wu_ref, sems):
+def input_grads(peers, cap, steps, dgate_ref, dup_ref, wg_hbm, wu_hbm, out_ref, wide_ref, wg_ref, wu_ref, sems):
     width = wu_ref.shape[0] // steps
     copies = [
-        pltpu.make_async_copy(wu_hbm.at[pl.ds(n * width, width)], wu_ref.at[pl.ds(n * width, width)], sems.at[n])
+        [
+            pltpu.make_async_copy(source.at[pl.ds(n * width, width)], held.at[pl.ds(n * width, width)], sems.at[i, n])
+            for i, (source, held) in enumerate(((wg_hbm, wg_ref), (wu_hbm, wu_ref)))
+        ]
         for n in range(steps)
     ]
-    for copy in copies:
-        copy.start()
+    for pair in copies:
+        for copy in pair:
+            copy.start()
     rows = wide_ref.shape[0] // peers
     cols = width // LANES
-    for weight_ref, grad_ref in ((wg_ref, dgate_ref), (wu_ref, dup_ref)):
-        for n in range(steps):
-            if weight_ref is wu_ref:
-                copies[n].wait()
-            back = lax.dot_general(
-                grad_ref[...], weight_ref[n * width : (n + 1) * width, :], NT, preferred_element_type=F32
-            )
-            for j in range(cap):
-                for c in range(cols):
-                    at = pl.ds(j * (rows // cap) + n * cols + c, peers, stride=rows)
-                    piece = back[j * peers : (j + 1) * peers, c * LANES : (c + 1) * LANES]
-                    wide_ref[at, :] = wide_ref[at, :] + piece if weight_ref is wu_ref else piece
+    for n in range(steps):
+        for copy in copies[n]:
+            copy.wait()
+        part = slice(n * width, (n + 1) * width)
+        back = lax.dot_general(dgate_ref[...], wg_ref[part, :], NT, preferred_element_type=F32)
+        back = back + lax.dot_general(dup_ref[...], wu_ref[part, :], NT, preferred_element_type=F32)
+        for j in range(cap):
+            for c in range(cols):
+                at = pl.ds(j * (rows // cap) + n * cols + c, peers, stride=rows)
+                wide_ref[at, :] = back[j * peers : (j + 1) * peers, c * LANES : (c + 1) * LANES]
     out_ref[...] = wide_ref[...].astype(BF)
 
 
-def tie(back_ref, _, out_ref):
-    pass
-
-
-def partials(sizes, unread, xt_ref, own_ref, near_ref, *refs):
-    outs = refs[unread:]
-    rows = own_ref.shape[0]
-    apart = xt_ref.shape[1] // 2
-    total = jnp.dot(xt_ref[:, :rows], own_ref[...], preferred_element_type=F32)
-    total = total + jnp.dot(xt_ref[:, apart : apart + rows], near_ref[...], preferred_element_type=F32)
-    at = 0
-    for size, out in zip(sizes, outs):
-        out[...] = total[at * LANES : (at + size) * LANES].astype(out.dtype)
-        at += size
-
-
-def add_two(part_ref, a_ref, b_ref, out_ref):
-    out_ref[...] = (part_ref[...] + a_ref[...].astype(F32) + b_ref[:LANES].astype(F32)).astype(BF)
-
-
-def add_one(part_ref, a_ref, out_ref):
-    out_ref[...] = (part_ref[...] + a_ref[:LANES].astype(F32)).astype(BF)
-
-
-def total_of(part_ref, a_ref, b_ref, c_ref, d_ref, _, out_ref):
-    near = a_ref[LANES:].astype(F32) + b_ref[LANES:].astype(F32)
-    far = c_ref[...].astype(F32) + d_ref[...].astype(F32)
-    out_ref[...] = part_ref[...] + near + far
+def partials(xt_ref, own_ref, near_ref, _, *outs):
+    rows, apart = own_ref.shape[0], xt_ref.shape[1] // 2
+    first = 0
+    for out in outs:
+        part = slice(first, first + out.shape[0])
+        total = jnp.dot(xt_ref[part, :rows], own_ref[...], preferred_element_type=F32)
+        total = total + jnp.dot(xt_ref[part, apart : apart + rows], near_ref[...], preferred_element_type=F32)
+        out[...] = total.astype(BF)
+        first += out.shape[0]
+
+
+def sum_right(kept_ref, right_ref, most_ref, out_ref):
+    far_sum = most_ref[...].astype(F32) + right_ref[:LANES].astype(F32)
+    out_ref[...] = (kept_ref[:LANES].astype(F32) + far_sum).astype(BF)
+
+
+def sum_left(kept_ref, left_ref, out_ref):
+    out_ref[...] = (kept_ref[LANES : 2 * LANES].astype(F32) + left_ref[:LANES].astype(F32)).astype(BF)
+
+
+def sum_own(kept_ref, right_ref, left_ref, right_sum_ref, left_sum_ref, _, out_ref):
+    near_sum = right_ref[LANES:].astype(F32) + left_ref[LANES:].astype(F32)
+    far_sum = right_sum_ref[...].astype(F32) + left_sum_ref[...].astype(F32)
+    out_ref[...] = kept_ref[2 * LANES :].astype(F32) + near_sum + far_sum
 
 
 def combine(peers, cap, take_ref, got_ref, out_ref, wide_ref):
@@ -220,7 +217,7 @@
     f_gate, f_up = pl.pallas_call(
         factors,
         grid=(parts,),
-        out_shape=(pltpu.HBM((slot_rows, hidden), F32),) * 2,
+        out_shape=(sds((slot_rows, hidden), F32),) * 2,
         in_specs=[
             pl.BlockSpec((slot_rows, width), lambda i: (0, 0)),
             pl.BlockSpec((width, 256), lambda i: (0, i)),
@@ -233,67 +230,53 @@
         ),
     )(far(x), far(w_gate), far(w_up))
     apart = -(-slot_rows // LANES) * LANES
-    x_sent, x_kept = call(
+    x_roles = call(
         functools.partial(by_role, ROLES),
-        (sds((5 * LANES, 2 * apart), BF), sds((3 * LANES, 2 * apart), BF)),
+        sds((len(ROLES) * LANES, 2 * apart), BF),
         "shv",
         moved=8 * slot_rows * half,
+        near=True,
     )(spot, x, borrowed)
 
     dgate, dup = call(
         functools.partial(hidden_grads, peers, cap),
         (sds((slot_rows, hidden), BF),) * 2,
-        "hhhu",
+        "dddo",
         [pltpu.VMEM((peers * in_rows, LANES), F32)],
         moved=16 * slot_rows * hidden,
         near=True,
-    )(arrived.reshape(peers * in_rows, LANES), f_gate, f_up, x_sent)
+    )(arrived.reshape(peers * in_rows, LANES), f_gate, f_up, x_roles)
     dgate_near = swap(dgate)
 
     out_rows = cap * width // LANES
-    steps = 4
+    steps = 8
     back = call(
         functools.partial(input_grads, peers, cap, steps),
         sds((peers * out_rows, LANES), BF),
-        "vvvu",
+        "vvuu",
         [
             pltpu.VMEM((peers * out_rows, LANES), F32),
             pltpu.VMEM((width, hidden), BF),
-            pltpu.SemaphoreType.DMA((steps,)),
+            pltpu.VMEM((width, hidden), BF),
+            pltpu.SemaphoreType.DMA((2, steps)),
         ],
         flops=1,
         moved=1,
     )(dgate, dup, w_gate, w_up)
-    block, blocks, wide_block = (sds((n * LANES, hidden), t) for n, t in ((1, BF), (2, BF), (1, F32)))
-    work = 4 * LANES * slot_rows * hidden
-    most, right, left = call(
-        functools.partial(partials, (1, 2, 2), 1), (block, blocks, blocks), "hvvu", flops=5 * work, moved=10 * LANES * hidden, near=True
-    )(x_sent, dgate, dgate_near, back)
+    returned = lax.all_to_all(back.reshape(peers, out_rows, LANES), "expert", 0, 0, tiled=True)
+
+    blocks = [sds((n * LANES, hidden), BF) for n in (1, 2, 2, 3)]
+    most, right, left, kept = call(
+        partials, blocks, "vvvu", flops=20_000_000_000, moved=16 * LANES * hidden, near=True
+    )(x_roles, dgate, dgate_near, back)
+    left_in = along_z(left, -1)
+    right_in = along_z(right, 1)
     most_in = along_z(most, 2)
-    right_in = along_z(right, 1)
-    left_in = along_z(left, -1)
-    p2, p2n, p0 = call(
-        functools.partial(partials, (1, 1, 1), 0),
-        (wide_block,) * 3,
-        "hvv",
-        flops=1,
-        moved=1,
-        near=True,
-    )(x_kept, dgate, dgate_near)
-
-    back = pl.pallas_call(
-        tie,
-        out_shape=pltpu.HBM(back.shape, BF),
-        in_specs=[pl.BlockSpec(memory_space=pl.ANY)] * 2,
-        out_specs=pl.BlockSpec(memory_space=pl.ANY),
-        input_output_aliases={0: 0},
-        cost_estimate=pl.CostEstimate(flops=1, bytes_accessed=1, transcendentals=0),
-    )(far(back), most)
-    returned = lax.all_to_all(back.reshape(peers, out_rows, LANES), "expert", 0, 0, tiled=True)
 
     moved = 10 * LANES * hidden
-    right_sum = along_z(call(add_two, block, "vvv", flops=20_000_000_000, moved=moved, near=True)(p2, most_in, right_in), 2)
-    left_sum = along_z(call(add_one, block, "vv", flops=20_000_000_000, moved=moved, near=True)(p2n, left_in), -2)
+    block = sds((LANES, hidden), BF)
+    right_sum = along_z(call(sum_right, block, "vvv", flops=moved, moved=moved, near=True)(kept, right_in, most_in), 2)
+    left_sum = along_z(call(sum_left, block, "vv", flops=moved, moved=moved, near=True)(kept, left_in), -2)
     grad_tokens = call(
         functools.partial(combine, peers, cap),
         sds((tokens, width), BF),
@@ -302,8 +285,8 @@
         flops=1,
         moved=1,
     )(take, returned.reshape(peers * out_rows, LANES))
-    grad_gate = call(total_of, wide_block, "vvvvvu", moved=2 * moved)(
-        p0, right_in, left_in, right_sum, left_sum, grad_tokens
+    grad_gate = call(sum_own, sds((LANES, hidden), F32), "vvvvvu", moved=2 * moved)(
+        kept, right_in, left_in, right_sum, left_sum, grad_tokens
     )
     return (grad_tokens, grad_gate[None])
 

time: 97.6 us -> 99.9 us (1.024); the launches traced: 95.8 us -> 99.3 us
  waiting for transfers between devices: 9.08 us -> 15.9 us
  Pallas kernels: 24.8 us -> 21 us
  starting transfers between devices: 59.5 us -> 61.6 us
  local copies, waits for them, and re-layouts: 1.49 us -> 0.01 us
    ppermute x5, waiting for transfers between devices: 3.81 us -> 15.9 us  [along_z(): return lax.ppermute(value, 'dp', pairs)]
    all_to_all x1, waiting for transfers between devices: 5.26 us -> 0.01 us  [on_device(): lax.all_to_all(back.reshape(peers, out_rows, LANES), 'expert', 0, 0, tile...]
    pallas_call x11 -> x10, Pallas kernels: 19.1 us -> 16.3 us  [call(): kernel(*(far(v) if kind in 'hu' else v for kind, v in zip(ins, given)))]
    ppermute x1, starting transfers between devices: 4.01 us -> 6.09 us  [on_device(): dgate_near = swap(dgate)]
    unnamed x12 -> x2, local copies, waits for them, and re-layouts: 1.49 us -> 0.01 us
    pallas_call x2 -> x1, Pallas kernels: 5.73 us -> 4.71 us  [on_device(): pl.pallas_call(factors, grid=(parts,), out_shape=(sds((slot_rows, hidden)...]
  transfers between devices with their start and end apart: 9 -> 9, of which waited for: 2 -> 3; matrix products, arithmetic and copies ran while one was open for 0% -> 0% of each run, Pallas kernels for 18% -> 18%
where the time goes in v4:
time: 99.9 us; the launch traced here: 99.3 us
  starting transfers between devices  61.6 us (62%)
  Pallas kernels  21 us (21%)
  waiting for transfers between devices  15.9 us (16%)
    ppermute x5, starting transfers between devices, along_z(): return lax.ppermute(value, 'dp', pairs)  26.5 us
    pallas_call x10, Pallas kernels, call(): kernel(*(far(v) if kind in 'hu' else v for kind, v in zip(ins, given)))  16.3 us
    ppermute x5, waiting for transfers between devices, along_z(): return lax.ppermute(value, 'dp', pairs)  15.9 us
    all_to_all x1, starting transfers between devices, on_device(): lax.all_to_all(outgoing.reshape(peers, in_rows, LANES), 'expert', 0, 0, t...  14 us
    all_to_all x1, starting transfers between devices, on_device(): lax.all_to_all(back.reshape(peers, out_rows, LANES), 'expert', 0, 0, tile...  8.26 us
    ppermute x1, starting transfers between devices, on_device(): borrowed = swap(lent)  6.64 us
    ppermute x1, starting transfers between devices, on_device(): dgate_near = swap(dgate)  6.09 us
    pallas_call x1, Pallas kernels, on_device(): pl.pallas_call(factors, grid=(parts,), out_shape=(sds((slot_rows, hidden)...  4.71 us
  transfers between devices with their start and end apart: 9, of which 3 were waited for; matrix products, arithmetic and copies ran while one was open for 0% of the time, Pallas kernels for 18%

profile of v4, /device:TPU:1, one launch (start us, length us, event | category | flops | bytes accessed | tf_op | source)
XLA Modules:
  0.0 99.3 jit_solution(8968351073535529641)
XLA Ops:
  0.6 2.2 %shard_map.68 = (bf16[1536,128]{1,0:T(8,128)(2,1)}, bf16[16,192]{1,0:T(8,128)(2,1)}) custom-call(s32[8,16]{1,0:T(8,128)} %bitcast.29, bf16[128,768]{1,0:T(8,128)(2,1)} %bitcast.28), custom_call_target="tpu_custom_call" | custom-call | flops 37748736 | bytes 786432 | tf_op jit(solution)/shard_map/pallas_call | solution.py:28
  2.8 14.0 %all-to-all-start = ((bf16[64,24,128]{2,1,0:T(8,128)(2,1)}), bf16[64,24,128]{2,1,0:T(8,128)(2,1)S(1)}, u32[]{:S(2)}, u32[]{:S(2)}) async-start(bf16[64,24,128]{2,1,0:T(8,128)(2,1)} %bitcast.26), calls=%async_computation | async-start | bytes 786432 | tf_op jit(solution)/shard_map/all_to_all | solution.py:211
  16.9 0.1 pad_add_fusion.core_ref.spot_ref
  17.0 2.0 %shard_map.70 = bf16[192,1024]{1,0:T(8,128)(2,1)} custom-call(s32[2]{0:T(128)S(1)} %pad_add_fusion.core_ref.spot_ref, bf16[192,2048]{1,0:T(8,128)(2,1)} %bitcast.22), custom_call_target="tpu_custom_call" | custom-call | bytes 786432 | tf_op jit(solution)/shard_map/pallas_call | solution.py:28
  19.0 6.6 %collective-permute-start = (bf16[192,1024]{1,0:T(8,128)(2,1)}, bf16[192,1024]{1,0:T(8,128)(2,1)S(1)}, u32[]{:S(2)}, u32[]{:S(2)}) collective-permute-start(bf16[192,1024]{1,0:T(8,128)(2,1)} %shard_map.70), channel_id=1, source_target_pairs={{0,64},{64,0},{128,192},{192,128},{256,320},{320,256},{384,448},{4... | collective-permute-start | bytes 1179656 | tf_op jit(solution)/shard_map/ppermute | solution.py:215
  25.6 4.7 %shard_map.69 = (f32[192,768]{1,0:T(8,128)S(1)}, f32[192,768]{1,0:T(8,128)S(1)}) custom-call(bf16[192,2048]{1,0:T(8,128)(2,1)} %bitcast.23, bf16[2048,768]{1,0:T(8,128)(2,1)} %bitcast.18, bf16[2048,768]{1,0:T(8,128)(2,1)} %bitcast.20), custom_call_target="tpu_custom_call" | custom-call | flops 1207959552 | bytes 12582912 | tf_op jit(solution)/shard_map/pallas_call | solution.py:217
  30.3 0.0 collective-permute-done.partner_ref
  30.4 1.5 %shard_map.71._.xt_ref = bf16[1024,512]{1,0:T(8,128)(2,1)S(1)} custom-call(s32[2]{0:T(128)S(1)} %pad_add_fusion.core_ref.spot_ref, bf16[192,2048]{1,0:T(8,128)(2,1)} %bitcast.24, bf16[192,1024]{1,0:T(8,128)(2,1)S(1)} %collective-permute-done.partner_ref), custom_call_target="tpu_custom_call" | custom-call | bytes 1572864 | tf_op jit(solution)/shard_map/pallas_call | solution.py:28
  31.9 0.0 all-to-all-done
  31.9 0.3 shard_map.72
  32.1 6.1 %collective-permute-start.1 = (bf16[192,768]{1,0:T(8,128)(2,1)S(1)}, bf16[192,768]{1,0:T(8,128)(2,1)S(1)}, u32[]{:S(2)}, u32[]{:S(2)}) collective-permute-start(bf16[192,768]{1,0:T(8,128)(2,1)S(1)} %get-tuple-element.16.dgate_ref.own_ref), channel_id=1, source_target_pairs={{0,64},{64,0},{128,192},{192,128},{256,320},{320,256},{384,448},{4... | collective-permute-start | bytes 884744 | tf_op jit(solution)/shard_map/ppermute | solution.py:249
  38.2 7.1 %shard_map.73._ = bf16[3072,128]{1,0:T(8,128)(2,1)} custom-call(bf16[192,768]{1,0:T(8,128)(2,1)S(1)} %get-tuple-element.16.dgate_ref.own_ref, bf16[192,768]{1,0:T(8,128)(2,1)S(1)} %get-tuple-element.17.dup_ref, bf16[2048,768]{1,0:T(8,128)(2,1)} %bitcast.19, bf16[2048,768]{1,0:T(8,128)(2,1)} %bitcast.21), custom_call_target="tpu_custom_call" | custom-call | flops 1 | bytes 1 | tf_op jit(solution)/shard_map/pallas_call | solution.py:28
  45.3 8.3 %all-to-all-start.1 = ((bf16[64,48,128]{2,1,0:T(8,128)(2,1)}), bf16[64,48,128]{2,1,0:T(8,128)(2,1)S(1)}, u32[]{:S(2)}, u32[]{:S(2)}) async-start(bf16[64,48,128]{2,1,0:T(8,128)(2,1)} %bitcast.25), calls=%async_computation.1 | async-start | bytes 1572864 | tf_op jit(solution)/shard_map/all_to_all | solution.py:266
  53.6 0.0 copy-start
  53.6 0.0 collective-permute-done.1.near_ref
  53.6 1.0 shard_map.75
  54.6 13.2 %collective-permute-start.2 = (bf16[256,768]{1,0:T(8,128)(2,1)S(1)}, bf16[256,768]{1,0:T(8,128)(2,1)S(1)}, u32[]{:S(2)}, u32[]{:S(2)}) collective-permute-start(bf16[256,768]{1,0:T(8,128)(2,1)S(1)} %get-tuple-element.19), channel_id=1, source_target_pairs={{0,128},{64,960},{128,256},{192,64},{256,384},{320,192},{384,512},... | collective-permute-start | bytes 1179656 | tf_op jit(solution)/shard_map/ppermute | solution.py:198
  67.9 1.9 %collective-permute-start.3 = (bf16[256,768]{1,0:T(8,128)(2,1)S(1)}, bf16[256,768]{1,0:T(8,128)(2,1)S(1)}, u32[]{:S(2)}, u32[]{:S(2)}) collective-permute-start(bf16[256,768]{1,0:T(8,128)(2,1)S(1)} %get-tuple-element.20), channel_id=1, source_target_pairs={{0,896},{64,192},{128,0},{192,320},{256,128},{320,448},{384,256},{... | collective-permute-start | bytes 1179656 | tf_op jit(solution)/shard_map/ppermute | solution.py:198
  69.8 3.1 %collective-permute-start.4 = (bf16[128,768]{1,0:T(8,128)(2,1)S(1)}, bf16[128,768]{1,0:T(8,128)(2,1)S(1)}, u32[]{:S(2)}, u32[]{:S(2)}) collective-permute-start(bf16[128,768]{1,0:T(8,128)(2,1)S(1)} %get-tuple-element.21), channel_id=1, source_target_pairs={{0,256},{64,832},{128,384},{192,960},{256,512},{320,64},{384,640},... | collective-permute-start | bytes 589832 | tf_op jit(solution)/shard_map/ppermute | solution.py:198
  72.9 6.8 %collective-permute-done.4.most_ref = bf16[128,768]{1,0:T(8,128)(2,1)S(1)} collective-permute-done((bf16[128,768]{1,0:T(8,128)(2,1)S(1)}, bf16[128,768]{1,0:T(8,128)(2,1)S(1)}, u32[]{:S(2)}, u32[]{:S(2)}) %collective-permute-start.4) | collective-permute-done | bytes 196640 | tf_op jit(solution)/shard_map/ppermute | solution.py:198
  79.7 0.0 collective-permute-done.2.right_ref
  79.7 0.1 shard_map.76
  79.8 6.4 %collective-permute-start.5 = (bf16[128,768]{1,0:T(8,128)(2,1)S(1)}, bf16[128,768]{1,0:T(8,128)(2,1)S(1)}, u32[]{:S(2)}, u32[]{:S(2)}) collective-permute-start(bf16[128,768]{1,0:T(8,128)(2,1)S(1)} %shard_map.76), channel_id=1, source_target_pairs={{0,256},{64,832},{128,384},{192,960},{256,512},{320,64},{384,640},... | collective-permute-start | bytes 589832 | tf_op jit(solution)/shard_map/ppermute | solution.py:198
  86.2 0.0 collective-permute-done.3.left_ref
  86.2 1.9 %collective-permute-start.6 = (bf16[128,768]{1,0:T(8,128)(2,1)S(1)}, bf16[128,768]{1,0:T(8,128)(2,1)S(1)}, u32[]{:S(2)}, u32[]{:S(2)}) collective-permute-start(bf16[128,768]{1,0:T(8,128)(2,1)S(1)} %shard_map.77), channel_id=1, source_target_pairs={{0,768},{64,320},{128,896},{192,448},{256,0},{320,576},{384,128},{... | collective-permute-start | bytes 589832 | tf_op jit(solution)/shard_map/ppermute | solution.py:198
  88.2 0.0 all-to-all-done.1
  88.2 0.0 copy-done
  88.2 1.3 %shard_map.74._ = bf16[16,2048]{1,0:T(8,128)(2,1)} custom-call(bf16[16,192]{1,0:T(8,128)(2,1)S(1)} %copy-done, bf16[3072,128]{1,0:T(8,128)(2,1)S(1)} %bitcast.16), custom_call_target="tpu_custom_call" | custom-call | flops 1 | bytes 1 | tf_op jit(solution)/shard_map/pallas_call | solution.py:28
  89.4 0.6 collective-permute-done.5.right_sum_ref
  90.0 8.5 %collective-permute-done.6.left_sum_ref = bf16[128,768]{1,0:T(8,128)(2,1)S(1)} collective-permute-done((bf16[128,768]{1,0:T(8,128)(2,1)S(1)}, bf16[128,768]{1,0:T(8,128)(2,1)S(1)}, u32[]{:S(2)}, u32[]{:S(2)}) %collective-permute-start.6) | collective-permute-done | bytes 196640 | tf_op jit(solution)/shard_map/ppermute | solution.py:198
  98.5 0.9 shard_map.78
  (1 shorter events, 0.0 us)
Async XLA Ops:
  2.8 29.0 %all-to-all-start = ((bf16[64,24,128]{2,1,0:T(8,128)(2,1)}), bf16[64,24,128]{2,1,0:T(8,128)(2,1)S(1)}, u32[]{:S(2)}, u32[]{:S(2)}) async-start(bf16[64,24,128]{2,1,0:T(8,128)(2,1)} %bitcast.26), calls=%async_computation | async-start | bytes 786432 | tf_op jit(solution)/shard_map/all_to_all | solution.py:211
  19.0 11.4 %collective-permute-start = (bf16[192,1024]{1,0:T(8,128)(2,1)}, bf16[192,1024]{1,0:T(8,128)(2,1)S(1)}, u32[]{:S(2)}, u32[]{:S(2)}) collective-permute-start(bf16[192,1024]{1,0:T(8,128)(2,1)} %shard_map.70), channel_id=1, source_target_pairs={{0,64},{64,0},{128,192},{192,128},{256,320},{320,256},{384,448},{4... | collective-permute-start | bytes 1179656 | tf_op jit(solution)/shard_map/ppermute | solution.py:215
  32.1 21.5 %collective-permute-start.1 = (bf16[192,768]{1,0:T(8,128)(2,1)S(1)}, bf16[192,768]{1,0:T(8,128)(2,1)S(1)}, u32[]{:S(2)}, u32[]{:S(2)}) collective-permute-start(bf16[192,768]{1,0:T(8,128)(2,1)S(1)} %get-tuple-element.16.dgate_ref.own_ref), channel_id=1, source_target_pairs={{0,64},{64,0},{128,192},{192,128},{256,320},{320,256},{384,448},{4... | collective-permute-start | bytes 884744 | tf_op jit(solution)/shard_map/ppermute | solution.py:249
  45.3 42.8 %all-to-all-start.1 = ((bf16[64,48,128]{2,1,0:T(8,128)(2,1)}), bf16[64,48,128]{2,1,0:T(8,128)(2,1)S(1)}, u32[]{:S(2)}, u32[]{:S(2)}) async-start(bf16[64,48,128]{2,1,0:T(8,128)(2,1)} %bitcast.25), calls=%async_computation.1 | async-start | bytes 1572864 | tf_op jit(solution)/shard_map/all_to_all | solution.py:266
  53.6 34.6 %copy-start = (bf16[16,192]{1,0:T(8,128)(2,1)S(1)}, bf16[16,192]{1,0:T(8,128)(2,1)}, u32[]{:S(2)}) copy-start(bf16[16,192]{1,0:T(8,128)(2,1)} %get-tuple-element.12.take_ref) | copy-start | bytes 18436
  54.6 25.1 %collective-permute-start.2 = (bf16[256,768]{1,0:T(8,128)(2,1)S(1)}, bf16[256,768]{1,0:T(8,128)(2,1)S(1)}, u32[]{:S(2)}, u32[]{:S(2)}) collective-permute-start(bf16[256,768]{1,0:T(8,128)(2,1)S(1)} %get-tuple-element.19), channel_id=1, source_target_pairs={{0,128},{64,960},{128,256},{192,64},{256,384},{320,192},{384,512},... | collective-permute-start | bytes 1179656 | tf_op jit(solution)/shard_map/ppermute | solution.py:198
  67.9 18.3 %collective-permute-start.3 = (bf16[256,768]{1,0:T(8,128)(2,1)S(1)}, bf16[256,768]{1,0:T(8,128)(2,1)S(1)}, u32[]{:S(2)}, u32[]{:S(2)}) collective-permute-start(bf16[256,768]{1,0:T(8,128)(2,1)S(1)} %get-tuple-element.20), channel_id=1, source_target_pairs={{0,896},{64,192},{128,0},{192,320},{256,128},{320,448},{384,256},{... | collective-permute-start | bytes 1179656 | tf_op jit(solution)/shard_map/ppermute | solution.py:198
  69.8 9.9 %collective-permute-start.4 = (bf16[128,768]{1,0:T(8,128)(2,1)S(1)}, bf16[128,768]{1,0:T(8,128)(2,1)S(1)}, u32[]{:S(2)}, u32[]{:S(2)}) collective-permute-start(bf16[128,768]{1,0:T(8,128)(2,1)S(1)} %get-tuple-element.21), channel_id=1, source_target_pairs={{0,256},{64,832},{128,384},{192,960},{256,512},{320,64},{384,640},... | collective-permute-start | bytes 589832 | tf_op jit(solution)/shard_map/ppermute | solution.py:198
  79.8 10.2 %collective-permute-start.5 = (bf16[128,768]{1,0:T(8,128)(2,1)S(1)}, bf16[128,768]{1,0:T(8,128)(2,1)S(1)}, u32[]{:S(2)}, u32[]{:S(2)}) collective-permute-start(bf16[128,768]{1,0:T(8,128)(2,1)S(1)} %shard_map.76), channel_id=1, source_target_pairs={{0,256},{64,832},{128,384},{192,960},{256,512},{320,64},{384,640},... | collective-permute-start | bytes 589832 | tf_op jit(solution)/shard_map/ppermute | solution.py:198
  86.2 12.2 %collective-permute-start.6 = (bf16[128,768]{1,0:T(8,128)(2,1)S(1)}, bf16[128,768]{1,0:T(8,128)(2,1)S(1)}, u32[]{:S(2)}, u32[]{:S(2)}) collective-permute-start(bf16[128,768]{1,0:T(8,128)(2,1)S(1)} %shard_map.77), channel_id=1, source_target_pairs={{0,768},{64,320},{128,896},{192,448},{256,0},{320,576},{384,128},{... | collective-permute-start | bytes 589832 | tf_op jit(solution)/shard_map/ppermute | solution.py:198

commit v5 on v4

--- a/solution.py
+++ b/solution.py
@@ -87,7 +87,9 @@
         out_ref[n : n + LANES, apart : apart + rows] = near.T.astype(BF)
 
 
-def factors(x_ref, wg_ref, wu_ref, fg_ref, fu_ref):
+def factors(x_ref, wg_ref, wu_ref, fg_ref, fu_ref, wg_kept, wu_kept):
+    wg_kept[...] = wg_ref[: wg_kept.shape[0], :]
+    wu_kept[...] = wu_ref[: wu_kept.shape[0], :]
     x = x_ref[...]
     gate = jnp.dot(x, wg_ref[...], preferred_element_type=F32)
     up = jnp.dot(x, wu_ref[...], preferred_element_type=F32)
@@ -108,26 +110,35 @@
             dup_ref[at] = (piece * fu_ref[at]).astype(BF)
 
 
-def input_grads(peers, cap, steps, dgate_ref, dup_ref, wg_hbm, wu_hbm, out_ref, wide_ref, wg_ref, wu_ref, sems):
-    width = wu_ref.shape[0] // steps
+def input_grads(peers, cap, *refs):
+    dgate_ref, dup_ref, wg_kept, wu_kept, wg_hbm, wu_hbm, out_ref, wide_ref, wg_ref, wu_ref, sems = refs
+    width = wg_kept.shape[0]
+    steps = wg_hbm.shape[0] // width
     copies = [
         [
-            pltpu.make_async_copy(source.at[pl.ds(n * width, width)], held.at[pl.ds(n * width, width)], sems.at[i, n])
+            pltpu.make_async_copy(source.at[pl.ds(n * width, width)], held.at[n - 1], sems.at[i, n - 1])
             for i, (source, held) in enumerate(((wg_hbm, wg_ref), (wu_hbm, wu_ref)))
         ]
-        for n in range(steps)
+        for n in range(1, steps)
     ]
-    for pair in copies:
-        for copy in pair:
-            copy.start()
+
+    def start(n):
+        if n < steps:
+            for copy in copies[n - 1]:
+                copy.start()
+
+    start(1)
+    start(2)
     rows = wide_ref.shape[0] // peers
     cols = width // LANES
     for n in range(steps):
-        for copy in copies[n]:
-            copy.wait()
-        part = slice(n * width, (n + 1) * width)
-        back = lax.dot_general(dgate_ref[...], wg_ref[part, :], NT, preferred_element_type=F32)
-        back = back + lax.dot_general(dup_ref[...], wu_ref[part, :], NT, preferred_element_type=F32)
+        if n > 0:
+            for copy in copies[n - 1]:
+                copy.wait()
+            start(n + 2)
+        wg, wu = (wg_kept[...], wu_kept[...]) if n == 0 else (wg_ref[n - 1], wu_ref[n - 1])
+        back = lax.dot_general(dgate_ref[...], wg, NT, preferred_element_type=F32)
+        back = back + lax.dot_general(dup_ref[...], wu, NT, preferred_element_type=F32)
         for j in range(cap):
             for c in range(cols):
                 at = pl.ds(j * (rows // cap) + n * cols + c, peers, stride=rows)
@@ -147,16 +158,16 @@
 
 
 def sum_right(kept_ref, right_ref, most_ref, out_ref):
-    far_sum = most_ref[...].astype(F32) + right_ref[:LANES].astype(F32)
+    far_sum = most_ref[...].astype(F32) + right_ref[...].astype(F32)
     out_ref[...] = (kept_ref[:LANES].astype(F32) + far_sum).astype(BF)
 
 
 def sum_left(kept_ref, left_ref, out_ref):
-    out_ref[...] = (kept_ref[LANES : 2 * LANES].astype(F32) + left_ref[:LANES].astype(F32)).astype(BF)
+    out_ref[...] = (kept_ref[LANES : 2 * LANES].astype(F32) + left_ref[...].astype(F32)).astype(BF)
 
 
 def sum_own(kept_ref, right_ref, left_ref, right_sum_ref, left_sum_ref, _, out_ref):
-    near_sum = right_ref[LANES:].astype(F32) + left_ref[LANES:].astype(F32)
+    near_sum = right_ref[...].astype(F32) + left_ref[...].astype(F32)
     far_sum = right_sum_ref[...].astype(F32) + left_sum_ref[...].astype(F32)
     out_ref[...] = kept_ref[2 * LANES :].astype(F32) + near_sum + far_sum
 
@@ -172,7 +183,7 @@
         out_ref[:, c * LANES : (c + 1) * LANES] = total.astype(BF)
 
 
-ROLES = (4, 3, 1, -3, -1, 2, -2, 0)
+ROLES = (4, 3, -3, 1, -1, 2, -2, 0)
 
 
 def on_device(expert_ids, grad_hidden, stored_inputs, gate_weight, up_weight):
@@ -214,16 +225,18 @@
     lent = call(partner_columns, sds((slot_rows, half), BF), "sh", moved=4 * slot_rows * half)(spot, x)
     borrowed = swap(lent)
     parts = hidden // 256
-    f_gate, f_up = pl.pallas_call(
+    keep = width // 4
+    f_gate, f_up, gate_kept, up_kept = pl.pallas_call(
         factors,
         grid=(parts,),
-        out_shape=(sds((slot_rows, hidden), F32),) * 2,
+        out_shape=(sds((slot_rows, hidden), F32),) * 2 + (sds((keep, hidden), BF),) * 2,
         in_specs=[
             pl.BlockSpec((slot_rows, width), lambda i: (0, 0)),
             pl.BlockSpec((width, 256), lambda i: (0, i)),
             pl.BlockSpec((width, 256), lambda i: (0, i)),
         ],
-        out_specs=(pl.BlockSpec((slot_rows, 256), lambda i: (0, i)),) * 2,
+        out_specs=(pl.BlockSpec((slot_rows, 256), lambda i: (0, i)),) * 2
+        + (pl.BlockSpec((keep, 256), lambda i: (0, i)),) * 2,
         compiler_params=pltpu.CompilerParams(vmem_limit_bytes=24 * MIB),
         cost_estimate=pl.CostEstimate(
             flops=4 * slot_rows * width * hidden, bytes_accessed=8 * width * hidden, transcendentals=slot_rows * hidden
@@ -235,13 +248,13 @@
         sds((len(ROLES) * LANES, 2 * apart), BF),
         "shv",
         moved=8 * slot_rows * half,
-        near=True,
+        near=False,
     )(spot, x, borrowed)
 
     dgate, dup = call(
         functools.partial(hidden_grads, peers, cap),
         (sds((slot_rows, hidden), BF),) * 2,
-        "dddo",
+        "dddu",
         [pltpu.VMEM((peers * in_rows, LANES), F32)],
         moved=16 * slot_rows * hidden,
         near=True,
@@ -249,29 +262,30 @@
     dgate_near = swap(dgate)
 
     out_rows = cap * width // LANES
-    steps = 8
     back = call(
-        functools.partial(input_grads, peers, cap, steps),
+        functools.partial(input_grads, peers, cap),
         sds((peers * out_rows, LANES), BF),
-        "vvuu",
+        "vvvvuu",
         [
             pltpu.VMEM((peers * out_rows, LANES), F32),
-            pltpu.VMEM((width, hidden), BF),
-            pltpu.VMEM((width, hidden), BF),
-            pltpu.SemaphoreType.DMA((2, steps)),
+            pltpu.VMEM((width // keep - 1, keep, hidden), BF),
+            pltpu.VMEM((width // keep - 1, keep, hidden), BF),
+            pltpu.SemaphoreType.DMA((2, width // keep - 1)),
         ],
         flops=1,
         moved=1,
-    )(dgate, dup, w_gate, w_up)
+    )(dgate, dup, gate_kept, up_kept, w_gate, w_up)
     returned = lax.all_to_all(back.reshape(peers, out_rows, LANES), "expert", 0, 0, tiled=True)
 
-    blocks = [sds((n * LANES, hidden), BF) for n in (1, 2, 2, 3)]
-    most, right, left, kept = call(
-        partials, blocks, "vvvu", flops=20_000_000_000, moved=16 * LANES * hidden, near=True
+    blocks = [sds((n * LANES, hidden), BF) for n in (1, 1, 1, 1, 1, 3)]
+    most, right, left, right_own, left_own, kept = call(
+        partials, blocks, "hvdu", flops=20_000_000_000, moved=16 * LANES * hidden, near=True
     )(x_roles, dgate, dgate_near, back)
+    most_in = along_z(most, 2)
+    right_in = along_z(right, 1)
     left_in = along_z(left, -1)
-    right_in = along_z(right, 1)
-    most_in = along_z(most, 2)
+    right_own_in = along_z(right_own, 1)
+    left_own_in = along_z(left_own, -1)
 
     moved = 10 * LANES * hidden
     block = sds((LANES, hidden), BF)
@@ -286,7 +300,7 @@
         moved=1,
     )(take, returned.reshape(peers * out_rows, LANES))
     grad_gate = call(sum_own, sds((LANES, hidden), F32), "vvvvvu", moved=2 * moved)(
-        kept, right_in, left_in, right_sum, left_sum, grad_tokens
+        kept, right_own_in, left_own_in, right_sum, left_sum, grad_tokens
     )
     return (grad_tokens, grad_gate[None])
 

time: 99.9 us -> 95.6 us (0.957)
  waiting for transfers between devices: 15.9 us -> 7.88 us
  starting transfers between devices: 61.6 us -> 64.8 us
    ppermute x5 -> x7, waiting for transfers between devices: 15.9 us -> 7.87 us  [along_z(): return lax.ppermute(value, 'dp', pairs)]
    ppermute x5 -> x7, starting transfers between devices: 26.5 us -> 29.7 us  [along_z(): return lax.ppermute(value, 'dp', pairs)]
    all_to_all x1, starting transfers between devices: 8.26 us -> 9.33 us  [on_device(): lax.all_to_all(back.reshape(peers, out_rows, LANES), 'expert', 0, 0, tile...]
    ppermute x1, starting transfers between devices: 6.09 us -> 5.02 us  [on_device(): dgate_near = swap(dgate)]
  transfers between devices with their start and end apart: 9 -> 11, of which waited for: 3 -> 2; matrix products, arithmetic and copies ran while one was open for 0% -> 0% of each run, Pallas kernels for 18% -> 19%
where the time goes in v5:
time: 95.6 us; the launch traced here: 94.8 us
  starting transfers between devices  64.8 us (68%)
  Pallas kernels  21.3 us (22%)
  waiting for transfers between devices  7.88 us (8%)
    ppermute x7, starting transfers between devices, along_z(): return lax.ppermute(value, 'dp', pairs)  29.7 us
    pallas_call x10, Pallas kernels, call(): kernel(*(far(v) if kind in 'hu' else v for kind, v in zip(ins, given)))  16.5 us
    all_to_all x1, starting transfers between devices, on_device(): lax.all_to_all(outgoing.reshape(peers, in_rows, LANES), 'expert', 0, 0, t...  14 us
    all_to_all x1, starting transfers between devices, on_device(): lax.all_to_all(back.reshape(peers, out_rows, LANES), 'expert', 0, 0, tile...  9.33 us
    ppermute x7, waiting for transfers between devices, along_z(): return lax.ppermute(value, 'dp', pairs)  7.87 us
    ppermute x1, starting transfers between devices, on_device(): borrowed = swap(lent)  6.64 us
    ppermute x1, starting transfers between devices, on_device(): dgate_near = swap(dgate)  5.02 us
    pallas_call x1, Pallas kernels, on_device(): pl.pallas_call(factors, grid=(parts,), out_shape=(sds((slot_rows, hidden)...  4.8 us
  transfers between devices with their start and end apart: 11, of which 2 were waited for; matrix products, arithmetic and copies ran while one was open for 0% of the time, Pallas kernels for 19%

profile of v5, /device:TPU:1, one launch (start us, length us, event | category | flops | bytes accessed | tf_op | source)
XLA Modules:
  0.0 94.8 jit_solution(14300936929297445864)
XLA Ops:
  0.6 2.2 %shard_map.68 = (bf16[1536,128]{1,0:T(8,128)(2,1)}, bf16[16,192]{1,0:T(8,128)(2,1)}) custom-call(s32[8,16]{1,0:T(8,128)} %bitcast.29, bf16[128,768]{1,0:T(8,128)(2,1)} %bitcast.28), custom_call_target="tpu_custom_call" | custom-call | flops 37748736 | bytes 786432 | tf_op jit(solution)/shard_map/pallas_call | solution.py:28
  2.8 14.0 %all-to-all-start = ((bf16[64,24,128]{2,1,0:T(8,128)(2,1)}), bf16[64,24,128]{2,1,0:T(8,128)(2,1)S(1)}, u32[]{:S(2)}, u32[]{:S(2)}) async-start(bf16[64,24,128]{2,1,0:T(8,128)(2,1)} %bitcast.27), calls=%async_computation | async-start | bytes 786432 | tf_op jit(solution)/shard_map/all_to_all | solution.py:222
  16.9 0.1 pad_add_fusion.core_ref.spot_ref
  17.0 2.0 %shard_map.70 = bf16[192,1024]{1,0:T(8,128)(2,1)} custom-call(s32[2]{0:T(128)S(1)} %pad_add_fusion.core_ref.spot_ref, bf16[192,2048]{1,0:T(8,128)(2,1)} %bitcast.22), custom_call_target="tpu_custom_call" | custom-call | bytes 786432 | tf_op jit(solution)/shard_map/pallas_call | solution.py:28
  19.0 6.6 %collective-permute-start = (bf16[192,1024]{1,0:T(8,128)(2,1)}, bf16[192,1024]{1,0:T(8,128)(2,1)S(1)}, u32[]{:S(2)}, u32[]{:S(2)}) collective-permute-start(bf16[192,1024]{1,0:T(8,128)(2,1)} %shard_map.70), channel_id=1, source_target_pairs={{0,64},{64,0},{128,192},{192,128},{256,320},{320,256},{384,448},{4... | collective-permute-start | bytes 1179656 | tf_op jit(solution)/shard_map/ppermute | solution.py:226
  25.6 4.8 %shard_map.69 = (f32[192,768]{1,0:T(8,128)S(1)}, f32[192,768]{1,0:T(8,128)S(1)}, bf16[512,768]{1,0:T(8,128)(2,1)S(1)}, bf16[512,768]{1,0:T(8,128)(2,1)S(1)}) custom-call(bf16[192,2048]{1,0:T(8,128)(2,1)} %bitcast.23, bf16[2048,768]{1,0:T(8,128)(2,1)} %bitcast.18, bf16[2048,768]{1,0:T(8,128)(2,1)} %bitcast.20), custom_call_target="tpu_custom_call" | custom-call | flops 1207959552 | bytes 12582912 | tf_op jit(solution)/shard_map/pallas_call | solution.py:229
  30.4 0.0 collective-permute-done.partner_ref
  30.5 2.5 %shard_map.71._.xt_ref = bf16[1024,512]{1,0:T(8,128)(2,1)} custom-call(s32[2]{0:T(128)S(1)} %pad_add_fusion.core_ref.spot_ref, bf16[192,2048]{1,0:T(8,128)(2,1)} %bitcast.24, bf16[192,1024]{1,0:T(8,128)(2,1)S(1)} %collective-permute-done.partner_ref), custom_call_target="tpu_custom_call" | custom-call | bytes 1572864 | tf_op jit(solution)/shard_map/pallas_call | solution.py:28
  32.9 0.0 all-to-all-done
  32.9 0.2 shard_map.72
  33.2 5.0 %collective-permute-start.1 = (bf16[192,768]{1,0:T(8,128)(2,1)S(1)}, bf16[192,768]{1,0:T(8,128)(2,1)S(1)}, u32[]{:S(2)}, u32[]{:S(2)}) collective-permute-start(bf16[192,768]{1,0:T(8,128)(2,1)S(1)} %get-tuple-element.20.refs_0_.own_ref), channel_id=1, source_target_pairs={{0,64},{64,0},{128,192},{192,128},{256,320},{320,256},{384,448},{4... | collective-permute-start | bytes 884744 | tf_op jit(solution)/shard_map/ppermute | solution.py:262
  38.2 4.8 %shard_map.73._ = bf16[3072,128]{1,0:T(8,128)(2,1)} custom-call(bf16[192,768]{1,0:T(8,128)(2,1)S(1)} %get-tuple-element.20.refs_0_.own_ref, bf16[192,768]{1,0:T(8,128)(2,1)S(1)} %get-tuple-element.21.refs_1_, bf16[512,768]{1,0:T(8,128)(2,1)S(1)} %get-tuple-element.22.refs_2_, bf16[512,768]{1,0:T(8,128)(2,1)S(1)} %get-tuple-element.23.refs_3_, ...), custom_call_target="tpu_custom_call" | custom-call | flops 1 | bytes 1 | tf_op jit(solution)/shard_map/pallas_call | solution.py:28
  43.0 9.3 %all-to-all-start.1 = ((bf16[64,48,128]{2,1,0:T(8,128)(2,1)}), bf16[64,48,128]{2,1,0:T(8,128)(2,1)S(1)}, u32[]{:S(2)}, u32[]{:S(2)}) async-start(bf16[64,48,128]{2,1,0:T(8,128)(2,1)} %bitcast.25), calls=%async_computation.1 | async-start | bytes 1572864 | tf_op jit(solution)/shard_map/all_to_all | solution.py:278
  52.3 0.0 copy-start
  52.4 0.0 collective-permute-done.1.near_ref
  52.4 2.5 %shard_map.75 = (bf16[128,768]{1,0:T(8,128)(2,1)S(1)}, bf16[128,768]{1,0:T(8,128)(2,1)S(1)}, bf16[128,768]{1,0:T(8,128)(2,1)S(1)}, bf16[128,768]{1,0:T(8,128)(2,...) custom-call(bf16[1024,512]{1,0:T(8,128)(2,1)} %shard_map.71._.xt_ref, ...), custom_call_target="tpu_custom_call" | custom-call | flops 20000000000 | bytes 1572864 | tf_op jit(solution)/shard_map/pallas_call | solution.py:28
  54.9 13.2 %collective-permute-start.4 = (bf16[128,768]{1,0:T(8,128)(2,1)S(1)}, bf16[128,768]{1,0:T(8,128)(2,1)S(1)}, u32[]{:S(2)}, u32[]{:S(2)}) collective-permute-start(bf16[128,768]{1,0:T(8,128)(2,1)S(1)} %get-tuple-element.27), channel_id=1, source_target_pairs={{0,128},{64,960},{128,256},{192,64},{256,384},{320,192},{384,512},... | collective-permute-start | bytes 589832 | tf_op jit(solution)/shard_map/ppermute | solution.py:209
  68.1 1.9 %collective-permute-start.5 = (bf16[128,768]{1,0:T(8,128)(2,1)S(1)}, bf16[128,768]{1,0:T(8,128)(2,1)S(1)}, u32[]{:S(2)}, u32[]{:S(2)}) collective-permute-start(bf16[128,768]{1,0:T(8,128)(2,1)S(1)} %get-tuple-element.28), channel_id=1, source_target_pairs={{0,256},{64,832},{128,384},{192,960},{256,512},{320,64},{384,640},... | collective-permute-start | bytes 589832 | tf_op jit(solution)/shard_map/ppermute | solution.py:209
  70.0 3.1 %collective-permute-start.7 = (bf16[128,768]{1,0:T(8,128)(2,1)S(1)}, bf16[128,768]{1,0:T(8,128)(2,1)S(1)}, u32[]{:S(2)}, u32[]{:S(2)}) collective-permute-start(bf16[128,768]{1,0:T(8,128)(2,1)S(1)} %get-tuple-element.29), channel_id=1, source_target_pairs={{0,896},{64,192},{128,0},{192,320},{256,128},{320,448},{384,256},{... | collective-permute-start | bytes 589832 | tf_op jit(solution)/shard_map/ppermute | solution.py:209
  73.1 3.4 %collective-permute-start.2 = (bf16[128,768]{1,0:T(8,128)(2,1)}, bf16[128,768]{1,0:T(8,128)(2,1)S(1)}, u32[]{:S(2)}, u32[]{:S(2)}) collective-permute-start(bf16[128,768]{1,0:T(8,128)(2,1)} %get-tuple-element.25), channel_id=1, source_target_pairs={{0,128},{64,960},{128,256},{192,64},{256,384},{320,192},{384,512},... | collective-permute-start | bytes 589832 | tf_op jit(solution)/shard_map/ppermute | solution.py:209
  76.5 1.9 %collective-permute-start.3 = (bf16[128,768]{1,0:T(8,128)(2,1)S(1)}, bf16[128,768]{1,0:T(8,128)(2,1)S(1)}, u32[]{:S(2)}, u32[]{:S(2)}) collective-permute-start(bf16[128,768]{1,0:T(8,128)(2,1)S(1)} %get-tuple-element.26), channel_id=1, source_target_pairs={{0,896},{64,192},{128,0},{192,320},{256,128},{320,448},{384,256},{... | collective-permute-start | bytes 589832 | tf_op jit(solution)/shard_map/ppermute | solution.py:209
  78.5 0.0 collective-permute-done.4.right_ref
  78.5 0.0 collective-permute-done.5.most_ref
  78.5 0.1 shard_map.76
  78.6 3.1 %collective-permute-start.6 = (bf16[128,768]{1,0:T(8,128)(2,1)S(1)}, bf16[128,768]{1,0:T(8,128)(2,1)S(1)}, u32[]{:S(2)}, u32[]{:S(2)}) collective-permute-start(bf16[128,768]{1,0:T(8,128)(2,1)S(1)} %shard_map.76), channel_id=1, source_target_pairs={{0,256},{64,832},{128,384},{192,960},{256,512},{320,64},{384,640},... | collective-permute-start | bytes 589832 | tf_op jit(solution)/shard_map/ppermute | solution.py:209
  81.7 0.0 collective-permute-done.7.left_ref
  81.7 3.1 %collective-permute-start.8 = (bf16[128,768]{1,0:T(8,128)(2,1)S(1)}, bf16[128,768]{1,0:T(8,128)(2,1)S(1)}, u32[]{:S(2)}, u32[]{:S(2)}) collective-permute-start(bf16[128,768]{1,0:T(8,128)(2,1)S(1)} %shard_map.77), channel_id=1, source_target_pairs={{0,768},{64,320},{128,896},{192,448},{256,0},{320,576},{384,128},{... | collective-permute-start | bytes 589832 | tf_op jit(solution)/shard_map/ppermute | solution.py:209
  84.8 0.0 all-to-all-done.1
  84.8 0.0 copy-done
  84.9 1.3 %shard_map.74._ = bf16[16,2048]{1,0:T(8,128)(2,1)} custom-call(bf16[16,192]{1,0:T(8,128)(2,1)S(1)} %copy-done, bf16[3072,128]{1,0:T(8,128)(2,1)S(1)} %bitcast.16), custom_call_target="tpu_custom_call" | custom-call | flops 1 | bytes 1 | tf_op jit(solution)/shard_map/pallas_call | solution.py:28
  86.1 0.0 collective-permute-done.2.right_ref
  86.1 0.0 collective-permute-done.3.left_ref
  86.1 2.2 %collective-permute-done.6.right_sum_ref = bf16[128,768]{1,0:T(8,128)(2,1)S(1)} collective-permute-done((bf16[128,768]{1,0:T(8,128)(2,1)S(1)}, bf16[128,768]{1,0:T(8,128)(2,1)S(1)}, u32[]{:S(2)}, u32[]{:S(2)}) %collective-permute-start.6) | collective-permute-done | bytes 196640 | tf_op jit(solution)/shard_map/ppermute | solution.py:209
  88.3 5.7 %collective-permute-done.8.left_sum_ref = bf16[128,768]{1,0:T(8,128)(2,1)S(1)} collective-permute-done((bf16[128,768]{1,0:T(8,128)(2,1)S(1)}, bf16[128,768]{1,0:T(8,128)(2,1)S(1)}, u32[]{:S(2)}, u32[]{:S(2)}) %collective-permute-start.8) | collective-permute-done | bytes 196640 | tf_op jit(solution)/shard_map/ppermute | solution.py:209
  94.0 0.9 shard_map.78
  (1 shorter events, 0.0 us)
Async XLA Ops:
  2.8 30.1 %all-to-all-start = ((bf16[64,24,128]{2,1,0:T(8,128)(2,1)}), bf16[64,24,128]{2,1,0:T(8,128)(2,1)S(1)}, u32[]{:S(2)}, u32[]{:S(2)}) async-start(bf16[64,24,128]{2,1,0:T(8,128)(2,1)} %bitcast.27), calls=%async_computation | async-start | bytes 786432 | tf_op jit(solution)/shard_map/all_to_all | solution.py:222
  19.0 11.5 %collective-permute-start = (bf16[192,1024]{1,0:T(8,128)(2,1)}, bf16[192,1024]{1,0:T(8,128)(2,1)S(1)}, u32[]{:S(2)}, u32[]{:S(2)}) collective-permute-start(bf16[192,1024]{1,0:T(8,128)(2,1)} %shard_map.70), channel_id=1, source_target_pairs={{0,64},{64,0},{128,192},{192,128},{256,320},{320,256},{384,448},{4... | collective-permute-start | bytes 1179656 | tf_op jit(solution)/shard_map/ppermute | solution.py:226
  33.2 19.2 %collective-permute-start.1 = (bf16[192,768]{1,0:T(8,128)(2,1)S(1)}, bf16[192,768]{1,0:T(8,128)(2,1)S(1)}, u32[]{:S(2)}, u32[]{:S(2)}) collective-permute-start(bf16[192,768]{1,0:T(8,128)(2,1)S(1)} %get-tuple-element.20.refs_0_.own_ref), channel_id=1, source_target_pairs={{0,64},{64,0},{128,192},{192,128},{256,320},{320,256},{384,448},{4... | collective-permute-start | bytes 884744 | tf_op jit(solution)/shard_map/ppermute | solution.py:262
  43.0 41.8 %all-to-all-start.1 = ((bf16[64,48,128]{2,1,0:T(8,128)(2,1)}), bf16[64,48,128]{2,1,0:T(8,128)(2,1)S(1)}, u32[]{:S(2)}, u32[]{:S(2)}) async-start(bf16[64,48,128]{2,1,0:T(8,128)(2,1)} %bitcast.25), calls=%async_computation.1 | async-start | bytes 1572864 | tf_op jit(solution)/shard_map/all_to_all | solution.py:278
  52.3 32.5 %copy-start = (bf16[16,192]{1,0:T(8,128)(2,1)S(1)}, bf16[16,192]{1,0:T(8,128)(2,1)}, u32[]{:S(2)}) copy-start(bf16[16,192]{1,0:T(8,128)(2,1)} %get-tuple-element.16.take_ref) | copy-start | bytes 18436
  54.9 23.6 %collective-permute-start.4 = (bf16[128,768]{1,0:T(8,128)(2,1)S(1)}, bf16[128,768]{1,0:T(8,128)(2,1)S(1)}, u32[]{:S(2)}, u32[]{:S(2)}) collective-permute-start(bf16[128,768]{1,0:T(8,128)(2,1)S(1)} %get-tuple-element.27), channel_id=1, source_target_pairs={{0,128},{64,960},{128,256},{192,64},{256,384},{320,192},{384,512},... | collective-permute-start | bytes 589832 | tf_op jit(solution)/shard_map/ppermute | solution.py:209
  68.1 10.4 %collective-permute-start.5 = (bf16[128,768]{1,0:T(8,128)(2,1)S(1)}, bf16[128,768]{1,0:T(8,128)(2,1)S(1)}, u32[]{:S(2)}, u32[]{:S(2)}) collective-permute-start(bf16[128,768]{1,0:T(8,128)(2,1)S(1)} %get-tuple-element.28), channel_id=1, source_target_pairs={{0,256},{64,832},{128,384},{192,960},{256,512},{320,64},{384,640},... | collective-permute-start | bytes 589832 | tf_op jit(solution)/shard_map/ppermute | solution.py:209
  70.0 11.6 %collective-permute-start.7 = (bf16[128,768]{1,0:T(8,128)(2,1)S(1)}, bf16[128,768]{1,0:T(8,128)(2,1)S(1)}, u32[]{:S(2)}, u32[]{:S(2)}) collective-permute-start(bf16[128,768]{1,0:T(8,128)(2,1)S(1)} %get-tuple-element.29), channel_id=1, source_target_pairs={{0,896},{64,192},{128,0},{192,320},{256,128},{320,448},{384,256},{... | collective-permute-start | bytes 589832 | tf_op jit(solution)/shard_map/ppermute | solution.py:209
  73.1 13.0 %collective-permute-start.2 = (bf16[128,768]{1,0:T(8,128)(2,1)}, bf16[128,768]{1,0:T(8,128)(2,1)S(1)}, u32[]{:S(2)}, u32[]{:S(2)}) collective-permute-start(bf16[128,768]{1,0:T(8,128)(2,1)} %get-tuple-element.25), channel_id=1, source_target_pairs={{0,128},{64,960},{128,256},{192,64},{256,384},{320,192},{384,512},... | collective-permute-start | bytes 589832 | tf_op jit(solution)/shard_map/ppermute | solution.py:209
  76.5 9.6 %collective-permute-start.3 = (bf16[128,768]{1,0:T(8,128)(2,1)S(1)}, bf16[128,768]{1,0:T(8,128)(2,1)S(1)}, u32[]{:S(2)}, u32[]{:S(2)}) collective-permute-start(bf16[128,768]{1,0:T(8,128)(2,1)S(1)} %get-tuple-element.26), channel_id=1, source_target_pairs={{0,896},{64,192},{128,0},{192,320},{256,128},{320,448},{384,256},{... | collective-permute-start | bytes 589832 | tf_op jit(solution)/shard_map/ppermute | solution.py:209
  78.6 9.7 %collective-permute-start.6 = (bf16[128,768]{1,0:T(8,128)(2,1)S(1)}, bf16[128,768]{1,0:T(8,128)(2,1)S(1)}, u32[]{:S(2)}, u32[]{:S(2)}) collective-permute-start(bf16[128,768]{1,0:T(8,128)(2,1)S(1)} %shard_map.76), channel_id=1, source_target_pairs={{0,256},{64,832},{128,384},{192,960},{256,512},{320,64},{384,640},... | collective-permute-start | bytes 589832 | tf_op jit(solution)/shard_map/ppermute | solution.py:209
  81.7 12.2 %collective-permute-start.8 = (bf16[128,768]{1,0:T(8,128)(2,1)S(1)}, bf16[128,768]{1,0:T(8,128)(2,1)S(1)}, u32[]{:S(2)}, u32[]{:S(2)}) collective-permute-start(bf16[128,768]{1,0:T(8,128)(2,1)S(1)} %shard_map.77), channel_id=1, source_target_pairs={{0,768},{64,320},{128,896},{192,448},{256,0},{320,576},{384,128},{... | collective-permute-start | bytes 589832 | tf_op jit(solution)/shard_map/ppermute | solution.py:209

commit v6 on v5

--- a/solution.py
+++ b/solution.py
@@ -146,28 +146,44 @@
     out_ref[...] = wide_ref[...].astype(BF)
 
 
-def partials(xt_ref, own_ref, near_ref, _, *outs):
+def tie(back_ref, _, out_ref):
+    pass
+
+
+def partials(xt_hbm, own_ref, near_ref, _, *refs):
+    *outs, token_ref, xt_ref, sems = refs
+    token_ref[...] = jnp.zeros_like(token_ref)
     rows, apart = own_ref.shape[0], xt_ref.shape[1] // 2
-    first = 0
-    for out in outs:
-        part = slice(first, first + out.shape[0])
+    places = [(out, n) for out in outs for n in range(0, out.shape[0], LANES)]
+    copies = [
+        pltpu.make_async_copy(
+            xt_hbm.at[pl.ds(b * LANES, LANES)], xt_ref.at[pl.ds(b * LANES, LANES)], sems.at[b]
+        )
+        for b in range(len(places))
+    ]
+    for copy in copies[:3]:
+        copy.start()
+    for b, (out, n) in enumerate(places):
+        copies[b].wait()
+        if b + 3 < len(places):
+            copies[b + 3].start()
+        part = slice(b * LANES, (b + 1) * LANES)
         total = jnp.dot(xt_ref[part, :rows], own_ref[...], preferred_element_type=F32)
         total = total + jnp.dot(xt_ref[part, apart : apart + rows], near_ref[...], preferred_element_type=F32)
-        out[...] = total.astype(BF)
-        first += out.shape[0]
-
-
-def sum_right(kept_ref, right_ref, most_ref, out_ref):
-    far_sum = most_ref[...].astype(F32) + right_ref[...].astype(F32)
+        out[n : n + LANES, :] = total.astype(BF)
+
+
+def sum_right(kept_ref, most_ref, right_ref, out_ref):
+    far_sum = most_ref[...].astype(F32) + right_ref[:LANES].astype(F32)
     out_ref[...] = (kept_ref[:LANES].astype(F32) + far_sum).astype(BF)
 
 
 def sum_left(kept_ref, left_ref, out_ref):
-    out_ref[...] = (kept_ref[LANES : 2 * LANES].astype(F32) + left_ref[...].astype(F32)).astype(BF)
+    out_ref[...] = (kept_ref[LANES : 2 * LANES].astype(F32) + left_ref[:LANES].astype(F32)).astype(BF)
 
 
 def sum_own(kept_ref, right_ref, left_ref, right_sum_ref, left_sum_ref, _, out_ref):
-    near_sum = right_ref[...].astype(F32) + left_ref[...].astype(F32)
+    near_sum = right_ref[LANES:].astype(F32) + left_ref[LANES:].astype(F32)
     far_sum = right_sum_ref[...].astype(F32) + left_sum_ref[...].astype(F32)
     out_ref[...] = kept_ref[2 * LANES :].astype(F32) + near_sum + far_sum
 
@@ -183,7 +199,7 @@
         out_ref[:, c * LANES : (c + 1) * LANES] = total.astype(BF)
 
 
-ROLES = (4, 3, -3, 1, -1, 2, -2, 0)
+ROLES = (4, 3, 1, -3, -1, 2, -2, 0)
 
 
 def on_device(expert_ids, grad_hidden, stored_inputs, gate_weight, up_weight):
@@ -275,22 +291,36 @@
         flops=1,
         moved=1,
     )(dgate, dup, gate_kept, up_kept, w_gate, w_up)
+    blocks = [sds((n * LANES, hidden), BF) for n in (1, 2, 2, 3)]
+    most, right, left, kept, token = call(
+        partials,
+        blocks + [sds((8, LANES), F32)],
+        "uvdu",
+        [pltpu.VMEM((len(ROLES) * LANES, 2 * apart), BF), pltpu.SemaphoreType.DMA((len(ROLES),))],
+        flops=1,
+        moved=1,
+        near=True,
+    )(x_roles, dgate, dgate_near, back)
+    back = pl.pallas_call(
+        tie,
+        out_shape=pltpu.HBM(back.shape, BF),
+        in_specs=[pl.BlockSpec(memory_space=pl.ANY), pl.BlockSpec(memory_space=pltpu.VMEM)],
+        out_specs=pl.BlockSpec(memory_space=pl.ANY),
+        input_output_aliases={0: 0},
+        cost_estimate=pl.CostEstimate(flops=1, bytes_accessed=1, transcendentals=0),
+    )(far(back), token)
     returned = lax.all_to_all(back.reshape(peers, out_rows, LANES), "expert", 0, 0, tiled=True)
 
-    blocks = [sds((n * LANES, hidden), BF) for n in (1, 1, 1, 1, 1, 3)]
-    most, right, left, right_own, left_own, kept = call(
-        partials, blocks, "hvdu", flops=20_000_000_000, moved=16 * LANES * hidden, near=True
-    )(x_roles, dgate, dgate_near, back)
     most_in = along_z(most, 2)
     right_in = along_z(right, 1)
     left_in = along_z(left, -1)
-    right_own_in = along_z(right_own, 1)
-    left_own_in = along_z(left_own, -1)
 
     moved = 10 * LANES * hidden
     block = sds((LANES, hidden), BF)
-    right_sum = along_z(call(sum_right, block, "vvv", flops=moved, moved=moved, near=True)(kept, right_in, most_in), 2)
-    left_sum = along_z(call(sum_left, block, "vv", flops=moved, moved=moved, near=True)(kept, left_in), -2)
+    right_sum = call(sum_right, block, "vvv", flops=11_500_000_000, moved=moved, near=True)(kept, most_in, right_in)
+    left_sum = call(sum_left, block, "vv", flops=1, moved=moved, near=True)(kept, left_in)
+    right_sum = along_z(right_sum, 2)
+    left_sum = along_z(left_sum, -2)
     grad_tokens = call(
         functools.partial(combine, peers, cap),
         sds((tokens, width), BF),
@@ -300,7 +330,7 @@
         moved=1,
     )(take, returned.reshape(peers * out_rows, LANES))
     grad_gate = call(sum_own, sds((LANES, hidden), F32), "vvvvvu", moved=2 * moved)(
-        kept, right_own_in, left_own_in, right_sum, left_sum, grad_tokens
+        kept, right_in, left_in, right_sum, left_sum, grad_tokens
     )
     return (grad_tokens, grad_gate[None])
 

time: 95.6 us -> 98.1 us (1.026)
  waiting for transfers between devices: 7.88 us -> 14.7 us
  starting transfers between devices: 64.8 us -> 58.3 us
  Pallas kernels: 21.3 us -> 22.9 us
    ppermute x7 -> x5, waiting for transfers between devices: 7.87 us -> 13.9 us  [along_z(): return lax.ppermute(value, 'dp', pairs)]
    ppermute x7 -> x5, starting transfers between devices: 29.7 us -> 25.9 us  [along_z(): return lax.ppermute(value, 'dp', pairs)]
    all_to_all x1, starting transfers between devices: 9.33 us -> 6.71 us  [on_device(): lax.all_to_all(back.reshape(peers, out_rows, LANES), 'expert', 0, 0, tile...]
  transfers between devices with their start and end apart: 11 -> 9, of which waited for: 2 -> 5; matrix products, arithmetic and copies ran while one was open for 0% -> 0% of each run, Pallas kernels for 19% -> 17%
where the time goes in v6:
time: 98.1 us; the launch traced here: 97.3 us
  starting transfers between devices  58.3 us (59%)
  Pallas kernels  22.9 us (23%)
  waiting for transfers between devices  14.7 us (15%)
    ppermute x5, starting transfers between devices, along_z(): return lax.ppermute(value, 'dp', pairs)  25.9 us
    pallas_call x10, Pallas kernels, call(): kernel(*(far(v) if kind in 'hu' else v for kind, v in zip(ins, given)))  17.4 us
    all_to_all x1, starting transfers between devices, on_device(): lax.all_to_all(outgoing.reshape(peers, in_rows, LANES), 'expert', 0, 0, t...  14 us
    ppermute x5, waiting for transfers between devices, along_z(): return lax.ppermute(value, 'dp', pairs)  13.9 us
    all_to_all x1, starting transfers between devices, on_device(): lax.all_to_all(back.reshape(peers, out_rows, LANES), 'expert', 0, 0, tile...  6.71 us
    ppermute x1, starting transfers between devices, on_device(): borrowed = swap(lent)  6.64 us
    ppermute x1, starting transfers between devices, on_device(): dgate_near = swap(dgate)  5.03 us
    pallas_call x1, Pallas kernels, on_device(): pl.pallas_call(factors, grid=(parts,), out_shape=(sds((slot_rows, hidden)...  4.8 us
  transfers between devices with their start and end apart: 9, of which 5 were waited for; matrix products, arithmetic and copies ran while one was open for 0% of the time, Pallas kernels for 17%

profile of v6, /device:TPU:1, one launch (start us, length us, event | category | flops | bytes accessed | tf_op | source)
XLA Modules:
  0.0 97.3 jit_solution(3314053052638563531)
XLA Ops:
  0.6 2.2 %shard_map.68 = (bf16[1536,128]{1,0:T(8,128)(2,1)}, bf16[16,192]{1,0:T(8,128)(2,1)}) custom-call(s32[8,16]{1,0:T(8,128)} %bitcast.29, bf16[128,768]{1,0:T(8,128)(2,1)} %bitcast.28), custom_call_target="tpu_custom_call" | custom-call | flops 37748736 | bytes 786432 | tf_op jit(solution)/shard_map/pallas_call | solution.py:28
  2.8 14.0 %all-to-all-start = ((bf16[64,24,128]{2,1,0:T(8,128)(2,1)}), bf16[64,24,128]{2,1,0:T(8,128)(2,1)S(1)}, u32[]{:S(2)}, u32[]{:S(2)}) async-start(bf16[64,24,128]{2,1,0:T(8,128)(2,1)} %bitcast.26), calls=%async_computation | async-start | bytes 786432 | tf_op jit(solution)/shard_map/all_to_all | solution.py:238
  16.9 0.1 pad_add_fusion.core_ref.spot_ref
  17.0 2.0 %shard_map.70 = bf16[192,1024]{1,0:T(8,128)(2,1)} custom-call(s32[2]{0:T(128)S(1)} %pad_add_fusion.core_ref.spot_ref, bf16[192,2048]{1,0:T(8,128)(2,1)} %bitcast.23), custom_call_target="tpu_custom_call" | custom-call | bytes 786432 | tf_op jit(solution)/shard_map/pallas_call | solution.py:28
  19.0 6.6 %collective-permute-start = (bf16[192,1024]{1,0:T(8,128)(2,1)}, bf16[192,1024]{1,0:T(8,128)(2,1)S(1)}, u32[]{:S(2)}, u32[]{:S(2)}) collective-permute-start(bf16[192,1024]{1,0:T(8,128)(2,1)} %shard_map.70), channel_id=1, source_target_pairs={{0,64},{64,0},{128,192},{192,128},{256,320},{320,256},{384,448},{4... | collective-permute-start | bytes 1179656 | tf_op jit(solution)/shard_map/ppermute | solution.py:242
  25.6 4.8 %shard_map.69 = (f32[192,768]{1,0:T(8,128)S(1)}, f32[192,768]{1,0:T(8,128)S(1)}, bf16[512,768]{1,0:T(8,128)(2,1)S(1)}, bf16[512,768]{1,0:T(8,128)(2,1)S(1)}) custom-call(bf16[192,2048]{1,0:T(8,128)(2,1)} %bitcast.24, bf16[2048,768]{1,0:T(8,128)(2,1)} %bitcast.18, bf16[2048,768]{1,0:T(8,128)(2,1)} %bitcast.20), custom_call_target="tpu_custom_call" | custom-call | flops 1207959552 | bytes 12582912 | tf_op jit(solution)/shard_map/pallas_call | solution.py:245
  30.4 0.0 collective-permute-done.partner_ref
  30.5 2.5 %shard_map.71._.xt_hbm = bf16[1024,512]{1,0:T(8,128)(2,1)} custom-call(s32[2]{0:T(128)S(1)} %pad_add_fusion.core_ref.spot_ref, bf16[192,2048]{1,0:T(8,128)(2,1)} %bitcast.25, bf16[192,1024]{1,0:T(8,128)(2,1)S(1)} %collective-permute-done.partner_ref), custom_call_target="tpu_custom_call" | custom-call | bytes 1572864 | tf_op jit(solution)/shard_map/pallas_call | solution.py:28
  32.9 0.0 all-to-all-done
  32.9 0.2 shard_map.72
  33.2 5.0 %collective-permute-start.1 = (bf16[192,768]{1,0:T(8,128)(2,1)S(1)}, bf16[192,768]{1,0:T(8,128)(2,1)S(1)}, u32[]{:S(2)}, u32[]{:S(2)}) collective-permute-start(bf16[192,768]{1,0:T(8,128)(2,1)S(1)} %get-tuple-element.19.refs_0_.own_ref), channel_id=1, source_target_pairs={{0,64},{64,0},{128,192},{192,128},{256,320},{320,256},{384,448},{4... | collective-permute-start | bytes 884744 | tf_op jit(solution)/shard_map/ppermute | solution.py:278
  38.2 4.8 %shard_map.73._.back_ref = bf16[3072,128]{1,0:T(8,128)(2,1)} custom-call(bf16[192,768]{1,0:T(8,128)(2,1)S(1)} %get-tuple-element.19.refs_0_.own_ref, bf16[192,768]{1,0:T(8,128)(2,1)S(1)} %get-tuple-element.20.refs_1_, bf16[512,768]{1,0:T(8,128)(2,1)S(1)} %get-tuple-element.21.refs_2_, bf16[512,768]{1,0:T(8,128)(2,1)S(1)} %get-tuple-element.22.refs_3_, ...), custom_call_target="tpu_custom_call" | custom-call | flops 1 | bytes 1 | tf_op jit(solution)/shard_map/pallas_call | solution.py:28
  43.0 0.0 collective-permute-done.1.near_ref
  43.0 3.4 %shard_map.74 = (bf16[128,768]{1,0:T(8,128)(2,1)S(1)}, bf16[256,768]{1,0:T(8,128)(2,1)S(1)}, bf16[256,768]{1,0:T(8,128)(2,1)S(1)}, bf16[384,768]{1,0:T(8,128)(2,1)S(1)}, f32[8,128]{1,0:T(8,128)S(1)}) custom-call(bf16[1024,512]{1,0:T(8,128)(2,1)} %shard_map.71._.xt_hbm, bf16[192,768]{1,0:T(8,128)(2,1)S(1)} %get-tuple-element.19.refs_0_.own_ref, ...), custom_call_target="tpu_custom_call" | custom-call | flops 1 | bytes 1 | tf_op jit(solution)/shard_map/pallas_call | solution.py:28
  46.5 0.0 copy-start.1
  46.5 0.6 copy-done.1
  47.0 15.8 %collective-permute-start.2 = (bf16[256,768]{1,0:T(8,128)(2,1)S(1)}, bf16[256,768]{1,0:T(8,128)(2,1)S(1)}, u32[]{:S(2)}, u32[]{:S(2)}) collective-permute-start(bf16[256,768]{1,0:T(8,128)(2,1)S(1)} %get-tuple-element.25), channel_id=1, source_target_pairs={{0,128},{64,960},{128,256},{192,64},{256,384},{320,192},{384,512},... | collective-permute-start | bytes 1179656 | tf_op jit(solution)/shard_map/ppermute | solution.py:225
  62.9 0.7 shard_map.75
  63.6 6.7 %all-to-all-start.1 = ((bf16[64,48,128]{2,1,0:T(8,128)(2,1)}), bf16[64,48,128]{2,1,0:T(8,128)(2,1)S(1)}, u32[]{:S(2)}, u32[]{:S(2)}) async-start(bf16[64,48,128]{2,1,0:T(8,128)(2,1)} %bitcast.22), calls=%async_computation.1 | async-start | bytes 1572864 | tf_op jit(solution)/shard_map/all_to_all | solution.py:312
  70.3 1.9 %collective-permute-start.4 = (bf16[128,768]{1,0:T(8,128)(2,1)S(1)}, bf16[128,768]{1,0:T(8,128)(2,1)S(1)}, u32[]{:S(2)}, u32[]{:S(2)}) collective-permute-start(bf16[128,768]{1,0:T(8,128)(2,1)S(1)} %get-tuple-element.27), channel_id=1, source_target_pairs={{0,256},{64,832},{128,384},{192,960},{256,512},{320,64},{384,640},... | collective-permute-start | bytes 589832 | tf_op jit(solution)/shard_map/ppermute | solution.py:225
  72.2 3.1 %collective-permute-start.3 = (bf16[256,768]{1,0:T(8,128)(2,1)S(1)}, bf16[256,768]{1,0:T(8,128)(2,1)S(1)}, u32[]{:S(2)}, u32[]{:S(2)}) collective-permute-start(bf16[256,768]{1,0:T(8,128)(2,1)S(1)} %get-tuple-element.26), channel_id=1, source_target_pairs={{0,896},{64,192},{128,0},{192,320},{256,128},{320,448},{384,256},{... | collective-permute-start | bytes 1179656 | tf_op jit(solution)/shard_map/ppermute | solution.py:225
  75.3 4.0 %collective-permute-done.4.most_ref = bf16[128,768]{1,0:T(8,128)(2,1)S(1)} collective-permute-done((bf16[128,768]{1,0:T(8,128)(2,1)S(1)}, bf16[128,768]{1,0:T(8,128)(2,1)S(1)}, u32[]{:S(2)}, u32[]{:S(2)}) %collective-permute-start.4) | collective-permute-done | bytes 196640 | tf_op jit(solution)/shard_map/ppermute | solution.py:225
  79.3 0.0 collective-permute-done.2.right_ref
  79.3 0.0 copy-start
  79.3 0.1 shard_map.77
  79.4 2.4 %collective-permute-start.5 = (bf16[128,768]{1,0:T(8,128)(2,1)S(1)}, bf16[128,768]{1,0:T(8,128)(2,1)S(1)}, u32[]{:S(2)}, u32[]{:S(2)}) collective-permute-start(bf16[128,768]{1,0:T(8,128)(2,1)S(1)} %shard_map.77), channel_id=1, source_target_pairs={{0,256},{64,832},{128,384},{192,960},{256,512},{320,64},{384,640},... | collective-permute-start | bytes 589832 | tf_op jit(solution)/shard_map/ppermute | solution.py:225
  81.8 1.2 %collective-permute-done.3.left_ref = bf16[256,768]{1,0:T(8,128)(2,1)S(1)} collective-permute-done((bf16[256,768]{1,0:T(8,128)(2,1)S(1)}, bf16[256,768]{1,0:T(8,128)(2,1)S(1)}, u32[]{:S(2)}, u32[]{:S(2)}) %collective-permute-start.3) | collective-permute-done | bytes 393248 | tf_op jit(solution)/shard_map/ppermute | solution.py:225
  83.0 2.7 %collective-permute-start.6 = (bf16[128,768]{1,0:T(8,128)(2,1)S(1)}, bf16[128,768]{1,0:T(8,128)(2,1)S(1)}, u32[]{:S(2)}, u32[]{:S(2)}) collective-permute-start(bf16[128,768]{1,0:T(8,128)(2,1)S(1)} %shard_map.78), channel_id=1, source_target_pairs={{0,768},{64,320},{128,896},{192,448},{256,0},{320,576},{384,128},{... | collective-permute-start | bytes 589832 | tf_op jit(solution)/shard_map/ppermute | solution.py:225
  85.7 0.9 all-to-all-done.1
  86.6 0.0 copy-done
  86.6 1.3 %shard_map.76._ = bf16[16,2048]{1,0:T(8,128)(2,1)} custom-call(bf16[16,192]{1,0:T(8,128)(2,1)S(1)} %copy-done, bf16[3072,128]{1,0:T(8,128)(2,1)S(1)} %bitcast.16), custom_call_target="tpu_custom_call" | custom-call | flops 1 | bytes 1 | tf_op jit(solution)/shard_map/pallas_call | solution.py:28
  87.8 0.1 collective-permute-done.5.right_sum_ref
  87.9 8.5 %collective-permute-done.6.left_sum_ref = bf16[128,768]{1,0:T(8,128)(2,1)S(1)} collective-permute-done((bf16[128,768]{1,0:T(8,128)(2,1)S(1)}, bf16[128,768]{1,0:T(8,128)(2,1)S(1)}, u32[]{:S(2)}, u32[]{:S(2)}) %collective-permute-start.6) | collective-permute-done | bytes 196640 | tf_op jit(solution)/shard_map/ppermute | solution.py:225
  96.5 0.9 shard_map.79
  (1 shorter events, 0.0 us)
Async XLA Ops:
  2.8 30.1 %all-to-all-start = ((bf16[64,24,128]{2,1,0:T(8,128)(2,1)}), bf16[64,24,128]{2,1,0:T(8,128)(2,1)S(1)}, u32[]{:S(2)}, u32[]{:S(2)}) async-start(bf16[64,24,128]{2,1,0:T(8,128)(2,1)} %bitcast.26), calls=%async_computation | async-start | bytes 786432 | tf_op jit(solution)/shard_map/all_to_all | solution.py:238
  19.0 11.5 %collective-permute-start = (bf16[192,1024]{1,0:T(8,128)(2,1)}, bf16[192,1024]{1,0:T(8,128)(2,1)S(1)}, u32[]{:S(2)}, u32[]{:S(2)}) collective-permute-start(bf16[192,1024]{1,0:T(8,128)(2,1)} %shard_map.70), channel_id=1, source_target_pairs={{0,64},{64,0},{128,192},{192,128},{256,320},{320,256},{384,448},{4... | collective-permute-start | bytes 1179656 | tf_op jit(solution)/shard_map/ppermute | solution.py:242
  33.2 9.8 %collective-permute-start.1 = (bf16[192,768]{1,0:T(8,128)(2,1)S(1)}, bf16[192,768]{1,0:T(8,128)(2,1)S(1)}, u32[]{:S(2)}, u32[]{:S(2)}) collective-permute-start(bf16[192,768]{1,0:T(8,128)(2,1)S(1)} %get-tuple-element.19.refs_0_.own_ref), channel_id=1, source_target_pairs={{0,64},{64,0},{128,192},{192,128},{256,320},{320,256},{384,448},{4... | collective-permute-start | bytes 884744 | tf_op jit(solution)/shard_map/ppermute | solution.py:278
  46.5 0.6 copy-start.1
  47.0 32.3 %collective-permute-start.2 = (bf16[256,768]{1,0:T(8,128)(2,1)S(1)}, bf16[256,768]{1,0:T(8,128)(2,1)S(1)}, u32[]{:S(2)}, u32[]{:S(2)}) collective-permute-start(bf16[256,768]{1,0:T(8,128)(2,1)S(1)} %get-tuple-element.25), channel_id=1, source_target_pairs={{0,128},{64,960},{128,256},{192,64},{256,384},{320,192},{384,512},... | collective-permute-start | bytes 1179656 | tf_op jit(solution)/shard_map/ppermute | solution.py:225
  63.6 23.0 %all-to-all-start.1 = ((bf16[64,48,128]{2,1,0:T(8,128)(2,1)}), bf16[64,48,128]{2,1,0:T(8,128)(2,1)S(1)}, u32[]{:S(2)}, u32[]{:S(2)}) async-start(bf16[64,48,128]{2,1,0:T(8,128)(2,1)} %bitcast.22), calls=%async_computation.1 | async-start | bytes 1572864 | tf_op jit(solution)/shard_map/all_to_all | solution.py:312
  70.3 9.0 %collective-permute-start.4 = (bf16[128,768]{1,0:T(8,128)(2,1)S(1)}, bf16[128,768]{1,0:T(8,128)(2,1)S(1)}, u32[]{:S(2)}, u32[]{:S(2)}) collective-permute-start(bf16[128,768]{1,0:T(8,128)(2,1)S(1)} %get-tuple-element.27), channel_id=1, source_target_pairs={{0,256},{64,832},{128,384},{192,960},{256,512},{320,64},{384,640},... | collective-permute-start | bytes 589832 | tf_op jit(solution)/shard_map/ppermute | solution.py:225
  72.2 10.7 %collective-permute-start.3 = (bf16[256,768]{1,0:T(8,128)(2,1)S(1)}, bf16[256,768]{1,0:T(8,128)(2,1)S(1)}, u32[]{:S(2)}, u32[]{:S(2)}) collective-permute-start(bf16[256,768]{1,0:T(8,128)(2,1)S(1)} %get-tuple-element.26), channel_id=1, source_target_pairs={{0,896},{64,192},{128,0},{192,320},{256,128},{320,448},{384,256},{... | collective-permute-start | bytes 1179656 | tf_op jit(solution)/shard_map/ppermute | solution.py:225
  79.3 7.2 %copy-start = (bf16[16,192]{1,0:T(8,128)(2,1)S(1)}, bf16[16,192]{1,0:T(8,128)(2,1)}, u32[]{:S(2)}) copy-start(bf16[16,192]{1,0:T(8,128)(2,1)} %get-tuple-element.15.take_ref) | copy-start | bytes 18436
  79.4 8.5 %collective-permute-start.5 = (bf16[128,768]{1,0:T(8,128)(2,1)S(1)}, bf16[128,768]{1,0:T(8,128)(2,1)S(1)}, u32[]{:S(2)}, u32[]{:S(2)}) collective-permute-start(bf16[128,768]{1,0:T(8,128)(2,1)S(1)} %shard_map.77), channel_id=1, source_target_pairs={{0,256},{64,832},{128,384},{192,960},{256,512},{320,64},{384,640},... | collective-permute-start | bytes 589832 | tf_op jit(solution)/shard_map/ppermute | solution.py:225
  83.0 13.5 %collective-permute-start.6 = (bf16[128,768]{1,0:T(8,128)(2,1)S(1)}, bf16[128,768]{1,0:T(8,128)(2,1)S(1)}, u32[]{:S(2)}, u32[]{:S(2)}) collective-permute-start(bf16[128,768]{1,0:T(8,128)(2,1)S(1)} %shard_map.78), channel_id=1, source_target_pairs={{0,768},{64,320},{128,896},{192,448},{256,0},{320,576},{384,128},{... | collective-permute-start | bytes 589832 | tf_op jit(solution)/shard_map/ppermute | solution.py:225

commit v7 on v4

--- a/solution.py
+++ b/solution.py
@@ -10,17 +10,23 @@
 BF, F32 = jnp.bfloat16, jnp.float32
 LANES = 128
 MIB = 1 << 20
+AHEAD = 3
 NT = (((1,), (1,)), ((), ()))
 
 
-def call(body, outs, ins, scratch=(), flops=0, moved=0, near=False, vmem=16):
+def call(body, outs, ins, scratch=(), flops=0, moved=0, near=False, alias=None, vmem=16):
     specs = {"h": pl.BlockSpec(), "d": pl.BlockSpec(), "v": pl.BlockSpec(memory_space=pltpu.VMEM)}
     specs |= {"s": pl.BlockSpec(memory_space=pltpu.SMEM), "u": pl.BlockSpec(memory_space=pl.ANY), "o": pl.BlockSpec(memory_space=pl.ANY)}
+    out_specs = jax.tree.map(lambda _: specs["v" if near else "h"], outs)
+    if alias:
+        ((source, place),) = alias.items()
+        out_specs[place] = specs[ins[source]]
     kernel = pl.pallas_call(
         body,
         out_shape=outs if near else jax.tree.map(lambda out: pltpu.HBM(out.shape, out.dtype), outs),
         in_specs=[specs[kind] for kind in ins],
-        out_specs=jax.tree.map(lambda _: specs["v" if near else "h"], outs),
+        out_specs=out_specs,
+        input_output_aliases=alias or {},
         scratch_shapes=list(scratch),
         compiler_params=pltpu.CompilerParams(vmem_limit_bytes=vmem * MIB),
         cost_estimate=pl.CostEstimate(flops=flops, bytes_accessed=moved, transcendentals=0),
@@ -60,8 +66,6 @@
             wide_ref[pl.ds(j * cols + c, peers, stride=rows), :] = sent[
                 j * peers : (j + 1) * peers, c * LANES : (c + 1) * LANES
             ]
-    for r in range(cap * cols, rows):
-        wide_ref[pl.ds(r, peers, stride=rows), :] = jnp.zeros((peers, LANES), F32)
     out_ref[...] = wide_ref[...].astype(BF)
     take_ref[...] = lax.dot_general(token_of, place, NT, preferred_element_type=F32).astype(BF)
 
@@ -87,7 +91,8 @@
         out_ref[n : n + LANES, apart : apart + rows] = near.T.astype(BF)
 
 
-def factors(x_ref, wg_ref, wu_ref, fg_ref, fu_ref):
+def factors(x_ref, wg_ref, wu_ref, fg_ref, fu_ref, wg_kept):
+    wg_kept[...] = wg_ref[: wg_kept.shape[0], :]
     x = x_ref[...]
     gate = jnp.dot(x, wg_ref[...], preferred_element_type=F32)
     up = jnp.dot(x, wu_ref[...], preferred_element_type=F32)
@@ -108,16 +113,19 @@
             dup_ref[at] = (piece * fu_ref[at]).astype(BF)
 
 
-def input_grads(peers, cap, steps, dgate_ref, dup_ref, wg_hbm, wu_hbm, out_ref, wide_ref, wg_ref, wu_ref, sems):
-    width = wu_ref.shape[0] // steps
+def input_grads(peers, cap, *refs):
+    dgate_ref, dup_ref, wg_kept, wg_hbm, wu_hbm, out_ref, wide_ref, wg_ref, wu_ref, sems = refs
+    width = wg_kept.shape[0]
+    steps = wg_hbm.shape[0] // width
     copies = [
         [
-            pltpu.make_async_copy(source.at[pl.ds(n * width, width)], held.at[pl.ds(n * width, width)], sems.at[i, n])
-            for i, (source, held) in enumerate(((wg_hbm, wg_ref), (wu_hbm, wu_ref)))
+            pltpu.make_async_copy(source.at[pl.ds(n * width, width)], held.at[n], sems.at[i, n])
+            for i, (source, held) in enumerate(((wu_hbm, wu_ref), (wg_hbm, wg_ref)))
+            if i == 0 or n > 0
         ]
         for n in range(steps)
     ]
-    for pair in copies:
+    for pair in copies[:AHEAD]:
         for copy in pair:
             copy.start()
     rows = wide_ref.shape[0] // peers
@@ -125,9 +133,11 @@
     for n in range(steps):
         for copy in copies[n]:
             copy.wait()
-        part = slice(n * width, (n + 1) * width)
-        back = lax.dot_general(dgate_ref[...], wg_ref[part, :], NT, preferred_element_type=F32)
-        back = back + lax.dot_general(dup_ref[...], wu_ref[part, :], NT, preferred_element_type=F32)
+        for copy in copies[n + AHEAD] if n + AHEAD < steps else ():
+            copy.start()
+        wg = wg_kept[...] if n == 0 else wg_ref[n]
+        back = lax.dot_general(dgate_ref[...], wg, NT, preferred_element_type=F32)
+        back = back + lax.dot_general(dup_ref[...], wu_ref[n], NT, preferred_element_type=F32)
         for j in range(cap):
             for c in range(cols):
                 at = pl.ds(j * (rows // cap) + n * cols + c, peers, stride=rows)
@@ -135,7 +145,8 @@
     out_ref[...] = wide_ref[...].astype(BF)
 
 
-def partials(xt_ref, own_ref, near_ref, _, *outs):
+def partials(xt_ref, own_ref, near_ref, _, *refs):
+    *outs, _ = refs
     rows, apart = own_ref.shape[0], xt_ref.shape[1] // 2
     first = 0
     for out in outs:
@@ -146,9 +157,12 @@
         first += out.shape[0]
 
 
-def sum_right(kept_ref, right_ref, most_ref, out_ref):
-    far_sum = most_ref[...].astype(F32) + right_ref[:LANES].astype(F32)
-    out_ref[...] = (kept_ref[:LANES].astype(F32) + far_sum).astype(BF)
+def sum_most(kept_ref, most_ref, out_ref):
+    out_ref[...] = kept_ref[:LANES].astype(F32) + most_ref[...].astype(F32)
+
+
+def sum_right(part_ref, right_ref, out_ref):
+    out_ref[...] = (part_ref[...] + right_ref[:LANES].astype(F32)).astype(BF)
 
 
 def sum_left(kept_ref, left_ref, out_ref):
@@ -214,16 +228,18 @@
     lent = call(partner_columns, sds((slot_rows, half), BF), "sh", moved=4 * slot_rows * half)(spot, x)
     borrowed = swap(lent)
     parts = hidden // 256
-    f_gate, f_up = pl.pallas_call(
+    keep = width // 8
+    f_gate, f_up, gate_kept = pl.pallas_call(
         factors,
         grid=(parts,),
-        out_shape=(sds((slot_rows, hidden), F32),) * 2,
+        out_shape=(sds((slot_rows, hidden), F32),) * 2 + (sds((keep, hidden), BF),),
         in_specs=[
             pl.BlockSpec((slot_rows, width), lambda i: (0, 0)),
             pl.BlockSpec((width, 256), lambda i: (0, i)),
             pl.BlockSpec((width, 256), lambda i: (0, i)),
         ],
-        out_specs=(pl.BlockSpec((slot_rows, 256), lambda i: (0, i)),) * 2,
+        out_specs=(pl.BlockSpec((slot_rows, 256), lambda i: (0, i)),) * 2
+        + (pl.BlockSpec((keep, 256), lambda i: (0, i)),),
         compiler_params=pltpu.CompilerParams(vmem_limit_bytes=24 * MIB),
         cost_estimate=pl.CostEstimate(
             flops=4 * slot_rows * width * hidden, bytes_accessed=8 * width * hidden, transcendentals=slot_rows * hidden
@@ -249,34 +265,42 @@
     dgate_near = swap(dgate)
 
     out_rows = cap * width // LANES
-    steps = 8
     back = call(
-        functools.partial(input_grads, peers, cap, steps),
+        functools.partial(input_grads, peers, cap),
         sds((peers * out_rows, LANES), BF),
-        "vvuu",
+        "vvvuu",
         [
             pltpu.VMEM((peers * out_rows, LANES), F32),
-            pltpu.VMEM((width, hidden), BF),
-            pltpu.VMEM((width, hidden), BF),
-            pltpu.SemaphoreType.DMA((2, steps)),
+            pltpu.VMEM((width // keep, keep, hidden), BF),
+            pltpu.VMEM((width // keep, keep, hidden), BF),
+            pltpu.SemaphoreType.DMA((2, width // keep)),
         ],
         flops=1,
         moved=1,
-    )(dgate, dup, w_gate, w_up)
+    )(dgate, dup, gate_kept, w_gate, w_up)
+    blocks = [sds((n * LANES, hidden), BF) for n in (1, 2, 2, 3)]
+    most, right, left, kept, back = call(
+        partials,
+        blocks + [pltpu.HBM(back.shape, BF)],
+        "vvvu",
+        flops=1,
+        moved=1,
+        near=True,
+        alias={3: len(blocks)},
+    )(x_roles, dgate, dgate_near, back)
     returned = lax.all_to_all(back.reshape(peers, out_rows, LANES), "expert", 0, 0, tiled=True)
 
-    blocks = [sds((n * LANES, hidden), BF) for n in (1, 2, 2, 3)]
-    most, right, left, kept = call(
-        partials, blocks, "vvvu", flops=20_000_000_000, moved=16 * LANES * hidden, near=True
-    )(x_roles, dgate, dgate_near, back)
+    most_in = along_z(most, 2)
+    right_in = along_z(right, 1)
     left_in = along_z(left, -1)
-    right_in = along_z(right, 1)
-    most_in = along_z(most, 2)
 
     moved = 10 * LANES * hidden
     block = sds((LANES, hidden), BF)
-    right_sum = along_z(call(sum_right, block, "vvv", flops=moved, moved=moved, near=True)(kept, right_in, most_in), 2)
-    left_sum = along_z(call(sum_left, block, "vv", flops=moved, moved=moved, near=True)(kept, left_in), -2)
+    part = call(sum_most, sds((LANES, hidden), F32), "vv", flops=5_000_000_000, moved=moved, near=True)(kept, most_in)
+    right_sum = call(sum_right, block, "vv", flops=10_500_000_000, moved=moved, near=True)(part, right_in)
+    left_sum = call(sum_left, block, "vv", flops=1, moved=moved, near=True)(kept, left_in)
+    right_sum = along_z(right_sum, 2)
+    left_sum = along_z(left_sum, -2)
     grad_tokens = call(
         functools.partial(combine, peers, cap),
         sds((tokens, width), BF),

time: 99.9 us -> 94.5 us (0.946); the launches traced: 99.3 us -> 92.7 us
  waiting for transfers between devices: 15.9 us -> 11.5 us
  starting transfers between devices: 61.6 us -> 59.5 us
    ppermute x5, waiting for transfers between devices: 15.9 us -> 11.5 us  [along_z(): return lax.ppermute(value, 'dp', pairs)]
    all_to_all x1, starting transfers between devices: 8.26 us -> 5.68 us  [on_device(): lax.all_to_all(back.reshape(peers, out_rows, LANES), 'expert', 0, 0, tile...]
    pallas_call x10 -> x11, Pallas kernels: 16.3 us -> 16.1 us  [call(): kernel(*(far(v) if kind in 'hu' else v for kind, v in zip(ins, given)))]
  transfers between devices with their start and end apart: 9 -> 9, of which waited for: 3 -> 2; matrix products, arithmetic and copies ran while one was open for 0% -> 0% of each run, Pallas kernels for 18% -> 18%
where the time goes in v7:
time: 94.5 us; the launch traced here: 92.7 us
  starting transfers between devices  59.5 us (63%)
  Pallas kernels  20.8 us (22%)
  waiting for transfers between devices  11.5 us (12%)
    ppermute x5, starting transfers between devices, along_z(): return lax.ppermute(value, 'dp', pairs)  27 us
    pallas_call x11, Pallas kernels, call(): kernel(*(far(v) if kind in 'hu' else v for kind, v in zip(ins, given)))  16.1 us
    all_to_all x1, starting transfers between devices, on_device(): lax.all_to_all(outgoing.reshape(peers, in_rows, LANES), 'expert', 0, 0, t...  14 us
    ppermute x5, waiting for transfers between devices, along_z(): return lax.ppermute(value, 'dp', pairs)  11.5 us
    ppermute x1, starting transfers between devices, on_device(): borrowed = swap(lent)  6.64 us
    ppermute x1, starting transfers between devices, on_device(): dgate_near = swap(dgate)  6.07 us
    all_to_all x1, starting transfers between devices, on_device(): lax.all_to_all(back.reshape(peers, out_rows, LANES), 'expert', 0, 0, tile...  5.68 us
    pallas_call x1, Pallas kernels, on_device(): pl.pallas_call(factors, grid=(parts,), out_shape=(sds((slot_rows, hidden)...  4.73 us
  transfers between devices with their start and end apart: 9, of which 2 were waited for; matrix products, arithmetic and copies ran while one was open for 0% of the time, Pallas kernels for 18%

profile of v7, /device:TPU:1, one launch (start us, length us, event | category | flops | bytes accessed | tf_op | source)
XLA Modules:
  0.0 92.7 jit_solution(8877158365971430660)
XLA Ops:
  0.6 2.2 %shard_map.68 = (bf16[1536,128]{1,0:T(8,128)(2,1)}, bf16[16,192]{1,0:T(8,128)(2,1)}) custom-call(s32[8,16]{1,0:T(8,128)} %bitcast.29, bf16[128,768]{1,0:T(8,128)(2,1)} %bitcast.28), custom_call_target="tpu_custom_call" | custom-call | flops 37748736 | bytes 786432 | tf_op jit(solution)/shard_map/pallas_call | solution.py:34
  2.8 14.0 %all-to-all-start = ((bf16[64,24,128]{2,1,0:T(8,128)(2,1)}), bf16[64,24,128]{2,1,0:T(8,128)(2,1)S(1)}, u32[]{:S(2)}, u32[]{:S(2)}) async-start(bf16[64,24,128]{2,1,0:T(8,128)(2,1)} %bitcast.26), calls=%async_computation | async-start | bytes 786432 | tf_op jit(solution)/shard_map/all_to_all | solution.py:225
  16.9 0.1 pad_add_fusion.core_ref.spot_ref
  16.9 2.0 %shard_map.69 = bf16[192,1024]{1,0:T(8,128)(2,1)} custom-call(s32[2]{0:T(128)S(1)} %pad_add_fusion.core_ref.spot_ref, bf16[192,2048]{1,0:T(8,128)(2,1)} %bitcast.22), custom_call_target="tpu_custom_call" | custom-call | bytes 786432 | tf_op jit(solution)/shard_map/pallas_call | solution.py:34
  18.9 6.6 %collective-permute-start = (bf16[192,1024]{1,0:T(8,128)(2,1)}, bf16[192,1024]{1,0:T(8,128)(2,1)S(1)}, u32[]{:S(2)}, u32[]{:S(2)}) collective-permute-start(bf16[192,1024]{1,0:T(8,128)(2,1)} %shard_map.69), channel_id=1, source_target_pairs={{0,64},{64,0},{128,192},{192,128},{256,320},{320,256},{384,448},{4... | collective-permute-start | bytes 1179656 | tf_op jit(solution)/shard_map/ppermute | solution.py:229
  25.6 4.7 %shard_map.71 = (f32[192,768]{1,0:T(8,128)S(1)}, f32[192,768]{1,0:T(8,128)S(1)}, bf16[256,768]{1,0:T(8,128)(2,1)S(1)}) custom-call(bf16[192,2048]{1,0:T(8,128)(2,1)} %bitcast.23, bf16[2048,768]{1,0:T(8,128)(2,1)} %bitcast.18, bf16[2048,768]{1,0:T(8,128)(2,1)} %bitcast.20), custom_call_target="tpu_custom_call" | custom-call | flops 1207959552 | bytes 12582912 | tf_op jit(solution)/shard_map/pallas_call | solution.py:232
  30.3 0.0 collective-permute-done.partner_ref
  30.3 1.5 %shard_map.70._.xt_ref = bf16[1024,512]{1,0:T(8,128)(2,1)S(1)} custom-call(s32[2]{0:T(128)S(1)} %pad_add_fusion.core_ref.spot_ref, bf16[192,2048]{1,0:T(8,128)(2,1)} %bitcast.24, bf16[192,1024]{1,0:T(8,128)(2,1)S(1)} %collective-permute-done.partner_ref), custom_call_target="tpu_custom_call" | custom-call | bytes 1572864 | tf_op jit(solution)/shard_map/pallas_call | solution.py:34
  31.8 0.0 all-to-all-done
  31.9 0.2 shard_map.72
  32.1 6.1 %collective-permute-start.1 = (bf16[192,768]{1,0:T(8,128)(2,1)S(1)}, bf16[192,768]{1,0:T(8,128)(2,1)S(1)}, u32[]{:S(2)}, u32[]{:S(2)}) collective-permute-start(bf16[192,768]{1,0:T(8,128)(2,1)S(1)} %get-tuple-element.18.refs_0_.own_ref), channel_id=1, source_target_pairs={{0,64},{64,0},{128,192},{192,128},{256,320},{320,256},{384,448},{4... | collective-permute-start | bytes 884744 | tf_op jit(solution)/shard_map/ppermute | solution.py:265
  38.2 7.0 %shard_map.73._ = bf16[3072,128]{1,0:T(8,128)(2,1)} custom-call(bf16[192,768]{1,0:T(8,128)(2,1)S(1)} %get-tuple-element.18.refs_0_.own_ref, bf16[192,768]{1,0:T(8,128)(2,1)S(1)} %get-tuple-element.19.refs_1_, bf16[256,768]{1,0:T(8,128)(2,1)S(1)} %get-tuple-element.20.refs_2_, bf16[2048,768]{1,0:T(8,128)(2,1)} %bitcast.19, bf16[2048,768]{1,0:T(8,128)(2,1)} %bitcast.21), custom_call_target="tpu_custom_call" | custom-call | flops 1 | bytes 1 | tf_op jit(solution)/shard_map/pallas_call | solution.py:34
  45.1 0.0 collective-permute-done.1.near_ref
  45.1 1.0 %shard_map.74 = (bf16[128,768]{1,0:T(8,128)(2,1)S(1)}, bf16[256,768]{1,0:T(8,128)(2,1)S(1)}, bf16[256,768]{1,0:T(8,128)(2,1)S(1)}, bf16[384,768]{1,0:T(8,128)(2,1)S(1)}, bf16[3072,128]{1,0:T(8,128)(2,1)}) custom-call(bf16[1024,512]{1,0:T(8,128)(2,1)S(1)} %shard_map.70._.xt_ref, ...), custom_call_target="tpu_custom_call", output_to_operand_aliasing={{4}: (3, {})} | custom-call | flops 1 | bytes 1 | tf_op jit(solution)/shard_map/pallas_call | solution.py:34
  46.1 14.9 %collective-permute-start.4 = (bf16[128,768]{1,0:T(8,128)(2,1)S(1)}, bf16[128,768]{1,0:T(8,128)(2,1)S(1)}, u32[]{:S(2)}, u32[]{:S(2)}) collective-permute-start(bf16[128,768]{1,0:T(8,128)(2,1)S(1)} %get-tuple-element.25), channel_id=1, source_target_pairs={{0,256},{64,832},{128,384},{192,960},{256,512},{320,64},{384,640},... | collective-permute-start | bytes 589832 | tf_op jit(solution)/shard_map/ppermute | solution.py:212
  61.1 5.7 %all-to-all-start.1 = ((bf16[64,48,128]{2,1,0:T(8,128)(2,1)}), bf16[64,48,128]{2,1,0:T(8,128)(2,1)S(1)}, u32[]{:S(2)}, u32[]{:S(2)}) async-start(bf16[64,48,128]{2,1,0:T(8,128)(2,1)} %bitcast.25), calls=%async_computation.1 | async-start | bytes 1572864 | tf_op jit(solution)/shard_map/all_to_all | solution.py:291
  66.8 2.8 %collective-permute-start.2 = (bf16[256,768]{1,0:T(8,128)(2,1)S(1)}, bf16[256,768]{1,0:T(8,128)(2,1)S(1)}, u32[]{:S(2)}, u32[]{:S(2)}) collective-permute-start(bf16[256,768]{1,0:T(8,128)(2,1)S(1)} %get-tuple-element.23), channel_id=1, source_target_pairs={{0,128},{64,960},{128,256},{192,64},{256,384},{320,192},{384,512},... | collective-permute-start | bytes 1179656 | tf_op jit(solution)/shard_map/ppermute | solution.py:212
  69.6 3.1 %collective-permute-start.3 = (bf16[256,768]{1,0:T(8,128)(2,1)S(1)}, bf16[256,768]{1,0:T(8,128)(2,1)S(1)}, u32[]{:S(2)}, u32[]{:S(2)}) collective-permute-start(bf16[256,768]{1,0:T(8,128)(2,1)S(1)} %get-tuple-element.24), channel_id=1, source_target_pairs={{0,896},{64,192},{128,0},{192,320},{256,128},{320,448},{384,256},{... | collective-permute-start | bytes 1179656 | tf_op jit(solution)/shard_map/ppermute | solution.py:212
  72.7 0.0 collective-permute-done.4.most_ref
  72.8 0.0 copy-start
  72.8 7.6 %collective-permute-done.2.right_ref = bf16[256,768]{1,0:T(8,128)(2,1)S(1)} collective-permute-done((bf16[256,768]{1,0:T(8,128)(2,1)S(1)}, bf16[256,768]{1,0:T(8,128)(2,1)S(1)}, u32[]{:S(2)}, u32[]{:S(2)}) %collective-permute-start.2) | collective-permute-done | bytes 393248 | tf_op jit(solution)/shard_map/ppermute | solution.py:212
  80.4 1.9 %collective-permute-start.5 = (bf16[128,768]{1,0:T(8,128)(2,1)S(1)}, bf16[128,768]{1,0:T(8,128)(2,1)S(1)}, u32[]{:S(2)}, u32[]{:S(2)}) collective-permute-start(bf16[128,768]{1,0:T(8,128)(2,1)S(1)} %shard_map.77), channel_id=1, source_target_pairs={{0,256},{64,832},{128,384},{192,960},{256,512},{320,64},{384,640},... | collective-permute-start | bytes 589832 | tf_op jit(solution)/shard_map/ppermute | solution.py:212
  82.3 0.0 collective-permute-done.3.left_ref
  82.4 4.3 %collective-permute-start.6 = (bf16[128,768]{1,0:T(8,128)(2,1)S(1)}, bf16[128,768]{1,0:T(8,128)(2,1)S(1)}, u32[]{:S(2)}, u32[]{:S(2)}) collective-permute-start(bf16[128,768]{1,0:T(8,128)(2,1)S(1)} %shard_map.78), channel_id=1, source_target_pairs={{0,768},{64,320},{128,896},{192,448},{256,0},{320,576},{384,128},{... | collective-permute-start | bytes 589832 | tf_op jit(solution)/shard_map/ppermute | solution.py:212
  86.7 0.0 all-to-all-done.1
  86.7 0.0 copy-done
  86.7 1.3 %shard_map.75._ = bf16[16,2048]{1,0:T(8,128)(2,1)} custom-call(bf16[16,192]{1,0:T(8,128)(2,1)S(1)} %copy-done, bf16[3072,128]{1,0:T(8,128)(2,1)S(1)} %bitcast.16), custom_call_target="tpu_custom_call" | custom-call | flops 1 | bytes 1 | tf_op jit(solution)/shard_map/pallas_call | solution.py:34
  88.0 3.8 %collective-permute-done.5.right_sum_ref = bf16[128,768]{1,0:T(8,128)(2,1)S(1)} collective-permute-done((bf16[128,768]{1,0:T(8,128)(2,1)S(1)}, bf16[128,768]{1,0:T(8,128)(2,1)S(1)}, u32[]{:S(2)}, u32[]{:S(2)}) %collective-permute-start.5) | collective-permute-done | bytes 196640 | tf_op jit(solution)/shard_map/ppermute | solution.py:212
  91.8 0.0 collective-permute-done.6.left_sum_ref
  91.8 0.9 shard_map.79
  (3 shorter events, 0.1 us)
Async XLA Ops:
  2.8 29.0 %all-to-all-start = ((bf16[64,24,128]{2,1,0:T(8,128)(2,1)}), bf16[64,24,128]{2,1,0:T(8,128)(2,1)S(1)}, u32[]{:S(2)}, u32[]{:S(2)}) async-start(bf16[64,24,128]{2,1,0:T(8,128)(2,1)} %bitcast.26), calls=%async_computation | async-start | bytes 786432 | tf_op jit(solution)/shard_map/all_to_all | solution.py:225
  18.9 11.4 %collective-permute-start = (bf16[192,1024]{1,0:T(8,128)(2,1)}, bf16[192,1024]{1,0:T(8,128)(2,1)S(1)}, u32[]{:S(2)}, u32[]{:S(2)}) collective-permute-start(bf16[192,1024]{1,0:T(8,128)(2,1)} %shard_map.69), channel_id=1, source_target_pairs={{0,64},{64,0},{128,192},{192,128},{256,320},{320,256},{384,448},{4... | collective-permute-start | bytes 1179656 | tf_op jit(solution)/shard_map/ppermute | solution.py:229
  32.1 13.0 %collective-permute-start.1 = (bf16[192,768]{1,0:T(8,128)(2,1)S(1)}, bf16[192,768]{1,0:T(8,128)(2,1)S(1)}, u32[]{:S(2)}, u32[]{:S(2)}) collective-permute-start(bf16[192,768]{1,0:T(8,128)(2,1)S(1)} %get-tuple-element.18.refs_0_.own_ref), channel_id=1, source_target_pairs={{0,64},{64,0},{128,192},{192,128},{256,320},{320,256},{384,448},{4... | collective-permute-start | bytes 884744 | tf_op jit(solution)/shard_map/ppermute | solution.py:265
  46.1 26.6 %collective-permute-start.4 = (bf16[128,768]{1,0:T(8,128)(2,1)S(1)}, bf16[128,768]{1,0:T(8,128)(2,1)S(1)}, u32[]{:S(2)}, u32[]{:S(2)}) collective-permute-start(bf16[128,768]{1,0:T(8,128)(2,1)S(1)} %get-tuple-element.25), channel_id=1, source_target_pairs={{0,256},{64,832},{128,384},{192,960},{256,512},{320,64},{384,640},... | collective-permute-start | bytes 589832 | tf_op jit(solution)/shard_map/ppermute | solution.py:212
  61.1 25.6 %all-to-all-start.1 = ((bf16[64,48,128]{2,1,0:T(8,128)(2,1)}), bf16[64,48,128]{2,1,0:T(8,128)(2,1)S(1)}, u32[]{:S(2)}, u32[]{:S(2)}) async-start(bf16[64,48,128]{2,1,0:T(8,128)(2,1)} %bitcast.25), calls=%async_computation.1 | async-start | bytes 1572864 | tf_op jit(solution)/shard_map/all_to_all | solution.py:291
  66.8 13.6 %collective-permute-start.2 = (bf16[256,768]{1,0:T(8,128)(2,1)S(1)}, bf16[256,768]{1,0:T(8,128)(2,1)S(1)}, u32[]{:S(2)}, u32[]{:S(2)}) collective-permute-start(bf16[256,768]{1,0:T(8,128)(2,1)S(1)} %get-tuple-element.23), channel_id=1, source_target_pairs={{0,128},{64,960},{128,256},{192,64},{256,384},{320,192},{384,512},... | collective-permute-start | bytes 1179656 | tf_op jit(solution)/shard_map/ppermute | solution.py:212
  69.6 12.7 %collective-permute-start.3 = (bf16[256,768]{1,0:T(8,128)(2,1)S(1)}, bf16[256,768]{1,0:T(8,128)(2,1)S(1)}, u32[]{:S(2)}, u32[]{:S(2)}) collective-permute-start(bf16[256,768]{1,0:T(8,128)(2,1)S(1)} %get-tuple-element.24), channel_id=1, source_target_pairs={{0,896},{64,192},{128,0},{192,320},{256,128},{320,448},{384,256},{... | collective-permute-start | bytes 1179656 | tf_op jit(solution)/shard_map/ppermute | solution.py:212
  72.8 13.9 %copy-start = (bf16[16,192]{1,0:T(8,128)(2,1)S(1)}, bf16[16,192]{1,0:T(8,128)(2,1)}, u32[]{:S(2)}) copy-start(bf16[16,192]{1,0:T(8,128)(2,1)} %get-tuple-element.14.take_ref) | copy-start | bytes 18436
  80.4 11.4 %collective-permute-start.5 = (bf16[128,768]{1,0:T(8,128)(2,1)S(1)}, bf16[128,768]{1,0:T(8,128)(2,1)S(1)}, u32[]{:S(2)}, u32[]{:S(2)}) collective-permute-start(bf16[128,768]{1,0:T(8,128)(2,1)S(1)} %shard_map.77), channel_id=1, source_target_pairs={{0,256},{64,832},{128,384},{192,960},{256,512},{320,64},{384,640},... | collective-permute-start | bytes 589832 | tf_op jit(solution)/shard_map/ppermute | solution.py:212
  82.4 9.4 %collective-permute-start.6 = (bf16[128,768]{1,0:T(8,128)(2,1)S(1)}, bf16[128,768]{1,0:T(8,128)(2,1)S(1)}, u32[]{:S(2)}, u32[]{:S(2)}) collective-permute-start(bf16[128,768]{1,0:T(8,128)(2,1)S(1)} %shard_map.78), channel_id=1, source_target_pairs={{0,768},{64,320},{128,896},{192,448},{256,0},{320,576},{384,128},{... | collective-permute-start | bytes 589832 | tf_op jit(solution)/shard_map/ppermute | solution.py:212

commit v8 on v7

--- a/solution.py
+++ b/solution.py
@@ -10,7 +10,7 @@
 BF, F32 = jnp.bfloat16, jnp.float32
 LANES = 128
 MIB = 1 << 20
-AHEAD = 3
+AHEAD = 2
 NT = (((1,), (1,)), ((), ()))
 
 
@@ -91,8 +91,7 @@
         out_ref[n : n + LANES, apart : apart + rows] = near.T.astype(BF)
 
 
-def factors(x_ref, wg_ref, wu_ref, fg_ref, fu_ref, wg_kept):
-    wg_kept[...] = wg_ref[: wg_kept.shape[0], :]
+def factors(x_ref, wg_ref, wu_ref, fg_ref, fu_ref):
     x = x_ref[...]
     gate = jnp.dot(x, wg_ref[...], preferred_element_type=F32)
     up = jnp.dot(x, wu_ref[...], preferred_element_type=F32)
@@ -114,14 +113,12 @@
 
 
 def input_grads(peers, cap, *refs):
-    dgate_ref, dup_ref, wg_kept, wg_hbm, wu_hbm, out_ref, wide_ref, wg_ref, wu_ref, sems = refs
-    width = wg_kept.shape[0]
-    steps = wg_hbm.shape[0] // width
+    dgate_ref, dup_ref, wg_hbm, wu_hbm, out_ref, wide_ref, wg_ref, wu_ref, sems = refs
+    steps, width, _ = wg_ref.shape
     copies = [
         [
             pltpu.make_async_copy(source.at[pl.ds(n * width, width)], held.at[n], sems.at[i, n])
-            for i, (source, held) in enumerate(((wu_hbm, wu_ref), (wg_hbm, wg_ref)))
-            if i == 0 or n > 0
+            for i, (source, held) in enumerate(((wg_hbm, wg_ref), (wu_hbm, wu_ref)))
         ]
         for n in range(steps)
     ]
@@ -135,8 +132,7 @@
             copy.wait()
         for copy in copies[n + AHEAD] if n + AHEAD < steps else ():
             copy.start()
-        wg = wg_kept[...] if n == 0 else wg_ref[n]
-        back = lax.dot_general(dgate_ref[...], wg, NT, preferred_element_type=F32)
+        back = lax.dot_general(dgate_ref[...], wg_ref[n], NT, preferred_element_type=F32)
         back = back + lax.dot_general(dup_ref[...], wu_ref[n], NT, preferred_element_type=F32)
         for j in range(cap):
             for c in range(cols):
@@ -162,15 +158,15 @@
 
 
 def sum_right(part_ref, right_ref, out_ref):
-    out_ref[...] = (part_ref[...] + right_ref[:LANES].astype(F32)).astype(BF)
+    out_ref[...] = (part_ref[...] + right_ref[...].astype(F32)).astype(BF)
 
 
 def sum_left(kept_ref, left_ref, out_ref):
-    out_ref[...] = (kept_ref[LANES : 2 * LANES].astype(F32) + left_ref[:LANES].astype(F32)).astype(BF)
+    out_ref[...] = (kept_ref[LANES : 2 * LANES].astype(F32) + left_ref[...].astype(F32)).astype(BF)
 
 
 def sum_own(kept_ref, right_ref, left_ref, right_sum_ref, left_sum_ref, _, out_ref):
-    near_sum = right_ref[LANES:].astype(F32) + left_ref[LANES:].astype(F32)
+    near_sum = right_ref[...].astype(F32) + left_ref[...].astype(F32)
     far_sum = right_sum_ref[...].astype(F32) + left_sum_ref[...].astype(F32)
     out_ref[...] = kept_ref[2 * LANES :].astype(F32) + near_sum + far_sum
 
@@ -186,7 +182,7 @@
         out_ref[:, c * LANES : (c + 1) * LANES] = total.astype(BF)
 
 
-ROLES = (4, 3, 1, -3, -1, 2, -2, 0)
+ROLES = (4, 3, -3, 1, -1, 2, -2, 0)
 
 
 def on_device(expert_ids, grad_hidden, stored_inputs, gate_weight, up_weight):
@@ -228,18 +224,16 @@
     lent = call(partner_columns, sds((slot_rows, half), BF), "sh", moved=4 * slot_rows * half)(spot, x)
     borrowed = swap(lent)
     parts = hidden // 256
-    keep = width // 8
-    f_gate, f_up, gate_kept = pl.pallas_call(
+    f_gate, f_up = pl.pallas_call(
         factors,
         grid=(parts,),
-        out_shape=(sds((slot_rows, hidden), F32),) * 2 + (sds((keep, hidden), BF),),
+        out_shape=(sds((slot_rows, hidden), F32),) * 2,
         in_specs=[
             pl.BlockSpec((slot_rows, width), lambda i: (0, 0)),
             pl.BlockSpec((width, 256), lambda i: (0, i)),
             pl.BlockSpec((width, 256), lambda i: (0, i)),
         ],
-        out_specs=(pl.BlockSpec((slot_rows, 256), lambda i: (0, i)),) * 2
-        + (pl.BlockSpec((keep, 256), lambda i: (0, i)),),
+        out_specs=(pl.BlockSpec((slot_rows, 256), lambda i: (0, i)),) * 2,
         compiler_params=pltpu.CompilerParams(vmem_limit_bytes=24 * MIB),
         cost_estimate=pl.CostEstimate(
             flops=4 * slot_rows * width * hidden, bytes_accessed=8 * width * hidden, transcendentals=slot_rows * hidden
@@ -264,22 +258,22 @@
     )(arrived.reshape(peers * in_rows, LANES), f_gate, f_up, x_roles)
     dgate_near = swap(dgate)
 
-    out_rows = cap * width // LANES
+    out_rows, steps = cap * width // LANES, 4
     back = call(
         functools.partial(input_grads, peers, cap),
         sds((peers * out_rows, LANES), BF),
-        "vvvuu",
+        "vvuu",
         [
             pltpu.VMEM((peers * out_rows, LANES), F32),
-            pltpu.VMEM((width // keep, keep, hidden), BF),
-            pltpu.VMEM((width // keep, keep, hidden), BF),
-            pltpu.SemaphoreType.DMA((2, width // keep)),
+            pltpu.VMEM((steps, width // steps, hidden), BF),
+            pltpu.VMEM((steps, width // steps, hidden), BF),
+            pltpu.SemaphoreType.DMA((2, steps)),
         ],
         flops=1,
         moved=1,
-    )(dgate, dup, gate_kept, w_gate, w_up)
-    blocks = [sds((n * LANES, hidden), BF) for n in (1, 2, 2, 3)]
-    most, right, left, kept, back = call(
+    )(dgate, dup, w_gate, w_up)
+    blocks = [sds((n * LANES, hidden), BF) for n in (1, 1, 1, 1, 1, 3)]
+    most, right, left, right_own, left_own, kept, back = call(
         partials,
         blocks + [pltpu.HBM(back.shape, BF)],
         "vvvu",
@@ -293,6 +287,8 @@
     most_in = along_z(most, 2)
     right_in = along_z(right, 1)
     left_in = along_z(left, -1)
+    right_own_in = along_z(right_own, 1)
+    left_own_in = along_z(left_own, -1)
 
     moved = 10 * LANES * hidden
     block = sds((LANES, hidden), BF)
@@ -310,7 +306,7 @@
         moved=1,
     )(take, returned.reshape(peers * out_rows, LANES))
     grad_gate = call(sum_own, sds((LANES, hidden), F32), "vvvvvu", moved=2 * moved)(
-        kept, right_in, left_in, right_sum, left_sum, grad_tokens
+        kept, right_own_in, left_own_in, right_sum, left_sum, grad_tokens
     )
     return (grad_tokens, grad_gate[None])
 

time: 94.5 us -> 96 us (1.016)
  starting transfers between devices: 59.5 us -> 64.4 us
  Pallas kernels: 20.8 us -> 19.2 us
    ppermute x5 -> x7, starting transfers between devices: 27 us -> 31.9 us  [along_z(): return lax.ppermute(value, 'dp', pairs)]
    pallas_call x11, Pallas kernels: 16.1 us -> 14.5 us  [call(): kernel(*(far(v) if kind in 'hu' else v for kind, v in zip(ins, given)))]
    ppermute x5 -> x7, waiting for transfers between devices: 11.5 us -> 10.5 us  [along_z(): return lax.ppermute(value, 'dp', pairs)]
  transfers between devices with their start and end apart: 9 -> 11, of which waited for: 2 -> 4; matrix products, arithmetic and copies ran while one was open for 0% -> 0% of each run, Pallas kernels for 18% -> 16%
where the time goes in v8:
time: 96 us; the launch traced here: 95 us
  starting transfers between devices  64.4 us (67%)
  Pallas kernels  19.2 us (20%)
  waiting for transfers between devices  10.6 us (11%)
    ppermute x7, starting transfers between devices, along_z(): return lax.ppermute(value, 'dp', pairs)  31.9 us
    pallas_call x11, Pallas kernels, call(): kernel(*(far(v) if kind in 'hu' else v for kind, v in zip(ins, given)))  14.5 us
    all_to_all x1, starting transfers between devices, on_device(): lax.all_to_all(outgoing.reshape(peers, in_rows, LANES), 'expert', 0, 0, t...  14 us
    ppermute x7, waiting for transfers between devices, along_z(): return lax.ppermute(value, 'dp', pairs)  10.5 us
    ppermute x1, starting transfers between devices, on_device(): borrowed = swap(lent)  6.64 us
    ppermute x1, starting transfers between devices, on_device(): dgate_near = swap(dgate)  6.09 us
    all_to_all x1, starting transfers between devices, on_device(): lax.all_to_all(back.reshape(peers, out_rows, LANES), 'expert', 0, 0, tile...  5.66 us
    pallas_call x1, Pallas kernels, on_device(): pl.pallas_call(factors, grid=(parts,), out_shape=(sds((slot_rows, hidden)...  4.71 us
  transfers between devices with their start and end apart: 11, of which 4 were waited for; matrix products, arithmetic and copies ran while one was open for 0% of the time, Pallas kernels for 16%

profile of v8, /device:TPU:1, one launch (start us, length us, event | category | flops | bytes accessed | tf_op | source)
XLA Modules:
  0.0 95.0 jit_solution(15197354431975585199)
XLA Ops:
  0.6 2.2 %shard_map.68 = (bf16[1536,128]{1,0:T(8,128)(2,1)}, bf16[16,192]{1,0:T(8,128)(2,1)}) custom-call(s32[8,16]{1,0:T(8,128)} %bitcast.29, bf16[128,768]{1,0:T(8,128)(2,1)} %bitcast.28), custom_call_target="tpu_custom_call" | custom-call | flops 37748736 | bytes 786432 | tf_op jit(solution)/shard_map/pallas_call | solution.py:34
  2.8 14.0 %all-to-all-start = ((bf16[64,24,128]{2,1,0:T(8,128)(2,1)}), bf16[64,24,128]{2,1,0:T(8,128)(2,1)S(1)}, u32[]{:S(2)}, u32[]{:S(2)}) async-start(bf16[64,24,128]{2,1,0:T(8,128)(2,1)} %bitcast.27), calls=%async_computation | async-start | bytes 786432 | tf_op jit(solution)/shard_map/all_to_all | solution.py:221
  16.9 0.1 pad_add_fusion.core_ref.spot_ref
  16.9 2.0 %shard_map.69 = bf16[192,1024]{1,0:T(8,128)(2,1)} custom-call(s32[2]{0:T(128)S(1)} %pad_add_fusion.core_ref.spot_ref, bf16[192,2048]{1,0:T(8,128)(2,1)} %bitcast.22), custom_call_target="tpu_custom_call" | custom-call | bytes 786432 | tf_op jit(solution)/shard_map/pallas_call | solution.py:34
  18.9 6.6 %collective-permute-start = (bf16[192,1024]{1,0:T(8,128)(2,1)}, bf16[192,1024]{1,0:T(8,128)(2,1)S(1)}, u32[]{:S(2)}, u32[]{:S(2)}) collective-permute-start(bf16[192,1024]{1,0:T(8,128)(2,1)} %shard_map.69), channel_id=1, source_target_pairs={{0,64},{64,0},{128,192},{192,128},{256,320},{320,256},{384,448},{4... | collective-permute-start | bytes 1179656 | tf_op jit(solution)/shard_map/ppermute | solution.py:225
  25.6 4.7 %shard_map.71 = (f32[192,768]{1,0:T(8,128)S(1)}, f32[192,768]{1,0:T(8,128)S(1)}) custom-call(bf16[192,2048]{1,0:T(8,128)(2,1)} %bitcast.23, bf16[2048,768]{1,0:T(8,128)(2,1)} %bitcast.18, bf16[2048,768]{1,0:T(8,128)(2,1)} %bitcast.20), custom_call_target="tpu_custom_call" | custom-call | flops 1207959552 | bytes 12582912 | tf_op jit(solution)/shard_map/pallas_call | solution.py:227
  30.3 0.0 collective-permute-done.partner_ref
  30.3 1.5 %shard_map.70._.xt_ref = bf16[1024,512]{1,0:T(8,128)(2,1)S(1)} custom-call(s32[2]{0:T(128)S(1)} %pad_add_fusion.core_ref.spot_ref, bf16[192,2048]{1,0:T(8,128)(2,1)} %bitcast.24, bf16[192,1024]{1,0:T(8,128)(2,1)S(1)} %collective-permute-done.partner_ref), custom_call_target="tpu_custom_call" | custom-call | bytes 1572864 | tf_op jit(solution)/shard_map/pallas_call | solution.py:34
  31.8 0.0 all-to-all-done
  31.8 0.2 shard_map.72
  32.1 6.1 %collective-permute-start.1 = (bf16[192,768]{1,0:T(8,128)(2,1)S(1)}, bf16[192,768]{1,0:T(8,128)(2,1)S(1)}, u32[]{:S(2)}, u32[]{:S(2)}) collective-permute-start(bf16[192,768]{1,0:T(8,128)(2,1)S(1)} %get-tuple-element.19.refs_0_.own_ref), channel_id=1, source_target_pairs={{0,64},{64,0},{128,192},{192,128},{256,320},{320,256},{384,448},{4... | collective-permute-start | bytes 884744 | tf_op jit(solution)/shard_map/ppermute | solution.py:259
  38.2 5.3 %shard_map.73._ = bf16[3072,128]{1,0:T(8,128)(2,1)} custom-call(bf16[192,768]{1,0:T(8,128)(2,1)S(1)} %get-tuple-element.19.refs_0_.own_ref, bf16[192,768]{1,0:T(8,128)(2,1)S(1)} %get-tuple-element.20.refs_1_, bf16[2048,768]{1,0:T(8,128)(2,1)} %bitcast.19, bf16[2048,768]{1,0:T(8,128)(2,1)} %bitcast.21), custom_call_target="tpu_custom_call" | custom-call | flops 1 | bytes 1 | tf_op jit(solution)/shard_map/pallas_call | solution.py:34
  43.5 0.0 collective-permute-done.1.near_ref
  43.5 1.0 %shard_map.74 = (bf16[128,768]{1,0:T(8,128)(2,1)S(1)}, bf16[128,768]{1,0:T(8,128)(2,1)S(1)}, bf16[128,768]{1,0:T(8,128)(2,1)S(1)}, bf16[128,768]{1,0:T(8,128)(2,...) custom-call(bf16[1024,512]{1,0:T(8,128)(2,1)S(1)} %shard_map.70._.xt, ...), custom_call_target="tpu_custom_call", output_to_operand_aliasing={{6}: (3, {})} | custom-call | flops 1 | bytes 1 | tf_op jit(solution)/shard_map/pallas_call | solution.py:34
  44.5 14.9 %collective-permute-start.4 = (bf16[128,768]{1,0:T(8,128)(2,1)S(1)}, bf16[128,768]{1,0:T(8,128)(2,1)S(1)}, u32[]{:S(2)}, u32[]{:S(2)}) collective-permute-start(bf16[128,768]{1,0:T(8,128)(2,1)S(1)} %get-tuple-element.25), channel_id=1, source_target_pairs={{0,256},{64,832},{128,384},{192,960},{256,512},{320,64},{384,640},... | collective-permute-start | bytes 589832 | tf_op jit(solution)/shard_map/ppermute | solution.py:208
  59.4 5.7 %all-to-all-start.1 = ((bf16[64,48,128]{2,1,0:T(8,128)(2,1)}), bf16[64,48,128]{2,1,0:T(8,128)(2,1)S(1)}, u32[]{:S(2)}, u32[]{:S(2)}) async-start(bf16[64,48,128]{2,1,0:T(8,128)(2,1)} %bitcast.25), calls=%async_computation.1 | async-start | bytes 1572864 | tf_op jit(solution)/shard_map/all_to_all | solution.py:285
  65.1 2.8 %collective-permute-start.2 = (bf16[128,768]{1,0:T(8,128)(2,1)S(1)}, bf16[128,768]{1,0:T(8,128)(2,1)S(1)}, u32[]{:S(2)}, u32[]{:S(2)}) collective-permute-start(bf16[128,768]{1,0:T(8,128)(2,1)S(1)} %get-tuple-element.23), channel_id=1, source_target_pairs={{0,128},{64,960},{128,256},{192,64},{256,384},{320,192},{384,512},... | collective-permute-start | bytes 589832 | tf_op jit(solution)/shard_map/ppermute | solution.py:208
  67.9 3.1 %collective-permute-start.3 = (bf16[128,768]{1,0:T(8,128)(2,1)S(1)}, bf16[128,768]{1,0:T(8,128)(2,1)S(1)}, u32[]{:S(2)}, u32[]{:S(2)}) collective-permute-start(bf16[128,768]{1,0:T(8,128)(2,1)S(1)} %get-tuple-element.24), channel_id=1, source_target_pairs={{0,896},{64,192},{128,0},{192,320},{256,128},{320,448},{384,256},{... | collective-permute-start | bytes 589832 | tf_op jit(solution)/shard_map/ppermute | solution.py:208
  71.0 3.4 %collective-permute-start.5 = (bf16[128,768]{1,0:T(8,128)(2,1)S(1)}, bf16[128,768]{1,0:T(8,128)(2,1)S(1)}, u32[]{:S(2)}, u32[]{:S(2)}) collective-permute-start(bf16[128,768]{1,0:T(8,128)(2,1)S(1)} %get-tuple-element.26), channel_id=1, source_target_pairs={{0,128},{64,960},{128,256},{192,64},{256,384},{320,192},{384,512},... | collective-permute-start | bytes 589832 | tf_op jit(solution)/shard_map/ppermute | solution.py:208
  74.5 1.9 %collective-permute-start.7 = (bf16[128,768]{1,0:T(8,128)(2,1)S(1)}, bf16[128,768]{1,0:T(8,128)(2,1)S(1)}, u32[]{:S(2)}, u32[]{:S(2)}) collective-permute-start(bf16[128,768]{1,0:T(8,128)(2,1)S(1)} %get-tuple-element.27), channel_id=1, source_target_pairs={{0,896},{64,192},{128,0},{192,320},{256,128},{320,448},{384,256},{... | collective-permute-start | bytes 589832 | tf_op jit(solution)/shard_map/ppermute | solution.py:208
  76.4 0.0 collective-permute-done.4.most_ref
  76.4 0.0 copy-start
  76.5 1.3 %collective-permute-done.5.right_ref = bf16[128,768]{1,0:T(8,128)(2,1)S(1)} collective-permute-done((bf16[128,768]{1,0:T(8,128)(2,1)S(1)}, bf16[128,768]{1,0:T(8,128)(2,1)S(1)}, u32[]{:S(2)}, u32[]{:S(2)}) %collective-permute-start.5) | collective-permute-done | bytes 196640 | tf_op jit(solution)/shard_map/ppermute | solution.py:208
  77.8 3.6 %collective-permute-start.6 = (bf16[128,768]{1,0:T(8,128)(2,1)S(1)}, bf16[128,768]{1,0:T(8,128)(2,1)S(1)}, u32[]{:S(2)}, u32[]{:S(2)}) collective-permute-start(bf16[128,768]{1,0:T(8,128)(2,1)S(1)} %shard_map.77), channel_id=1, source_target_pairs={{0,256},{64,832},{128,384},{192,960},{256,512},{320,64},{384,640},... | collective-permute-start | bytes 589832 | tf_op jit(solution)/shard_map/ppermute | solution.py:208
  81.4 0.7 collective-permute-done.7.left_ref
  82.1 2.1 %collective-permute-start.8 = (bf16[128,768]{1,0:T(8,128)(2,1)S(1)}, bf16[128,768]{1,0:T(8,128)(2,1)S(1)}, u32[]{:S(2)}, u32[]{:S(2)}) collective-permute-start(bf16[128,768]{1,0:T(8,128)(2,1)S(1)} %shard_map.78), channel_id=1, source_target_pairs={{0,768},{64,320},{128,896},{192,448},{256,0},{320,576},{384,128},{... | collective-permute-start | bytes 589832 | tf_op jit(solution)/shard_map/ppermute | solution.py:208
  84.3 0.0 all-to-all-done.1
  84.3 0.0 copy-done
  84.3 1.3 %shard_map.75._ = bf16[16,2048]{1,0:T(8,128)(2,1)} custom-call(bf16[16,192]{1,0:T(8,128)(2,1)S(1)} %copy-done, bf16[3072,128]{1,0:T(8,128)(2,1)S(1)} %bitcast.16), custom_call_target="tpu_custom_call" | custom-call | flops 1 | bytes 1 | tf_op jit(solution)/shard_map/pallas_call | solution.py:34
  85.6 0.0 collective-permute-done.2.right_ref
  85.6 0.0 collective-permute-done.3.left_ref
  85.6 0.7 collective-permute-done.6.right_sum_ref
  86.2 7.9 %collective-permute-done.8.left_sum_ref = bf16[128,768]{1,0:T(8,128)(2,1)S(1)} collective-permute-done((bf16[128,768]{1,0:T(8,128)(2,1)S(1)}, bf16[128,768]{1,0:T(8,128)(2,1)S(1)}, u32[]{:S(2)}, u32[]{:S(2)}) %collective-permute-start.8) | collective-permute-done | bytes 196640 | tf_op jit(solution)/shard_map/ppermute | solution.py:208
  94.1 0.9 shard_map.79
  (3 shorter events, 0.1 us)
Async XLA Ops:
  2.8 29.0 %all-to-all-start = ((bf16[64,24,128]{2,1,0:T(8,128)(2,1)}), bf16[64,24,128]{2,1,0:T(8,128)(2,1)S(1)}, u32[]{:S(2)}, u32[]{:S(2)}) async-start(bf16[64,24,128]{2,1,0:T(8,128)(2,1)} %bitcast.27), calls=%async_computation | async-start | bytes 786432 | tf_op jit(solution)/shard_map/all_to_all | solution.py:221
  18.9 11.4 %collective-permute-start = (bf16[192,1024]{1,0:T(8,128)(2,1)}, bf16[192,1024]{1,0:T(8,128)(2,1)S(1)}, u32[]{:S(2)}, u32[]{:S(2)}) collective-permute-start(bf16[192,1024]{1,0:T(8,128)(2,1)} %shard_map.69), channel_id=1, source_target_pairs={{0,64},{64,0},{128,192},{192,128},{256,320},{320,256},{384,448},{4... | collective-permute-start | bytes 1179656 | tf_op jit(solution)/shard_map/ppermute | solution.py:225
  32.1 11.4 %collective-permute-start.1 = (bf16[192,768]{1,0:T(8,128)(2,1)S(1)}, bf16[192,768]{1,0:T(8,128)(2,1)S(1)}, u32[]{:S(2)}, u32[]{:S(2)}) collective-permute-start(bf16[192,768]{1,0:T(8,128)(2,1)S(1)} %get-tuple-element.19.refs_0_.own_ref), channel_id=1, source_target_pairs={{0,64},{64,0},{128,192},{192,128},{256,320},{320,256},{384,448},{4... | collective-permute-start | bytes 884744 | tf_op jit(solution)/shard_map/ppermute | solution.py:259
  44.5 31.9 %collective-permute-start.4 = (bf16[128,768]{1,0:T(8,128)(2,1)S(1)}, bf16[128,768]{1,0:T(8,128)(2,1)S(1)}, u32[]{:S(2)}, u32[]{:S(2)}) collective-permute-start(bf16[128,768]{1,0:T(8,128)(2,1)S(1)} %get-tuple-element.25), channel_id=1, source_target_pairs={{0,256},{64,832},{128,384},{192,960},{256,512},{320,64},{384,640},... | collective-permute-start | bytes 589832 | tf_op jit(solution)/shard_map/ppermute | solution.py:208
  59.4 24.9 %all-to-all-start.1 = ((bf16[64,48,128]{2,1,0:T(8,128)(2,1)}), bf16[64,48,128]{2,1,0:T(8,128)(2,1)S(1)}, u32[]{:S(2)}, u32[]{:S(2)}) async-start(bf16[64,48,128]{2,1,0:T(8,128)(2,1)} %bitcast.25), calls=%async_computation.1 | async-start | bytes 1572864 | tf_op jit(solution)/shard_map/all_to_all | solution.py:285
  65.1 20.5 %collective-permute-start.2 = (bf16[128,768]{1,0:T(8,128)(2,1)S(1)}, bf16[128,768]{1,0:T(8,128)(2,1)S(1)}, u32[]{:S(2)}, u32[]{:S(2)}) collective-permute-start(bf16[128,768]{1,0:T(8,128)(2,1)S(1)} %get-tuple-element.23), channel_id=1, source_target_pairs={{0,128},{64,960},{128,256},{192,64},{256,384},{320,192},{384,512},... | collective-permute-start | bytes 589832 | tf_op jit(solution)/shard_map/ppermute | solution.py:208
  67.9 17.6 %collective-permute-start.3 = (bf16[128,768]{1,0:T(8,128)(2,1)S(1)}, bf16[128,768]{1,0:T(8,128)(2,1)S(1)}, u32[]{:S(2)}, u32[]{:S(2)}) collective-permute-start(bf16[128,768]{1,0:T(8,128)(2,1)S(1)} %get-tuple-element.24), channel_id=1, source_target_pairs={{0,896},{64,192},{128,0},{192,320},{256,128},{320,448},{384,256},{... | collective-permute-start | bytes 589832 | tf_op jit(solution)/shard_map/ppermute | solution.py:208
  71.0 6.7 %collective-permute-start.5 = (bf16[128,768]{1,0:T(8,128)(2,1)S(1)}, bf16[128,768]{1,0:T(8,128)(2,1)S(1)}, u32[]{:S(2)}, u32[]{:S(2)}) collective-permute-start(bf16[128,768]{1,0:T(8,128)(2,1)S(1)} %get-tuple-element.26), channel_id=1, source_target_pairs={{0,128},{64,960},{128,256},{192,64},{256,384},{320,192},{384,512},... | collective-permute-start | bytes 589832 | tf_op jit(solution)/shard_map/ppermute | solution.py:208
  74.5 7.6 %collective-permute-start.7 = (bf16[128,768]{1,0:T(8,128)(2,1)S(1)}, bf16[128,768]{1,0:T(8,128)(2,1)S(1)}, u32[]{:S(2)}, u32[]{:S(2)}) collective-permute-start(bf16[128,768]{1,0:T(8,128)(2,1)S(1)} %get-tuple-element.27), channel_id=1, source_target_pairs={{0,896},{64,192},{128,0},{192,320},{256,128},{320,448},{384,256},{... | collective-permute-start | bytes 589832 | tf_op jit(solution)/shard_map/ppermute | solution.py:208
  76.4 7.8 %copy-start = (bf16[16,192]{1,0:T(8,128)(2,1)S(1)}, bf16[16,192]{1,0:T(8,128)(2,1)}, u32[]{:S(2)}) copy-start(bf16[16,192]{1,0:T(8,128)(2,1)} %get-tuple-element.15.take_ref) | copy-start | bytes 18436
  77.8 8.4 %collective-permute-start.6 = (bf16[128,768]{1,0:T(8,128)(2,1)S(1)}, bf16[128,768]{1,0:T(8,128)(2,1)S(1)}, u32[]{:S(2)}, u32[]{:S(2)}) collective-permute-start(bf16[128,768]{1,0:T(8,128)(2,1)S(1)} %shard_map.77), channel_id=1, source_target_pairs={{0,256},{64,832},{128,384},{192,960},{256,512},{320,64},{384,640},... | collective-permute-start | bytes 589832 | tf_op jit(solution)/shard_map/ppermute | solution.py:208
  82.1 12.0 %collective-permute-start.8 = (bf16[128,768]{1,0:T(8,128)(2,1)S(1)}, bf16[128,768]{1,0:T(8,128)(2,1)S(1)}, u32[]{:S(2)}, u32[]{:S(2)}) collective-permute-start(bf16[128,768]{1,0:T(8,128)(2,1)S(1)} %shard_map.78), channel_id=1, source_target_pairs={{0,768},{64,320},{128,896},{192,448},{256,0},{320,576},{384,128},{... | collective-permute-start | bytes 589832 | tf_op jit(solution)/shard_map/ppermute | solution.py:208

commit v9 on v8

--- a/solution.py
+++ b/solution.py
@@ -158,15 +158,15 @@
 
 
 def sum_right(part_ref, right_ref, out_ref):
-    out_ref[...] = (part_ref[...] + right_ref[...].astype(F32)).astype(BF)
+    out_ref[...] = (part_ref[...] + right_ref[:LANES].astype(F32)).astype(BF)
 
 
 def sum_left(kept_ref, left_ref, out_ref):
-    out_ref[...] = (kept_ref[LANES : 2 * LANES].astype(F32) + left_ref[...].astype(F32)).astype(BF)
+    out_ref[...] = (kept_ref[LANES : 2 * LANES].astype(F32) + left_ref[:LANES].astype(F32)).astype(BF)
 
 
 def sum_own(kept_ref, right_ref, left_ref, right_sum_ref, left_sum_ref, _, out_ref):
-    near_sum = right_ref[...].astype(F32) + left_ref[...].astype(F32)
+    near_sum = right_ref[LANES:].astype(F32) + left_ref[LANES:].astype(F32)
     far_sum = right_sum_ref[...].astype(F32) + left_sum_ref[...].astype(F32)
     out_ref[...] = kept_ref[2 * LANES :].astype(F32) + near_sum + far_sum
 
@@ -182,7 +182,7 @@
         out_ref[:, c * LANES : (c + 1) * LANES] = total.astype(BF)
 
 
-ROLES = (4, 3, -3, 1, -1, 2, -2, 0)
+ROLES = (4, 3, 1, -3, -1, 2, -2, 0)
 
 
 def on_device(expert_ids, grad_hidden, stored_inputs, gate_weight, up_weight):
@@ -272,8 +272,8 @@
         flops=1,
         moved=1,
     )(dgate, dup, w_gate, w_up)
-    blocks = [sds((n * LANES, hidden), BF) for n in (1, 1, 1, 1, 1, 3)]
-    most, right, left, right_own, left_own, kept, back = call(
+    blocks = [sds((n * LANES, hidden), BF) for n in (1, 2, 2, 3)]
+    most, right, left, kept, back = call(
         partials,
         blocks + [pltpu.HBM(back.shape, BF)],
         "vvvu",
@@ -287,8 +287,6 @@
     most_in = along_z(most, 2)
     right_in = along_z(right, 1)
     left_in = along_z(left, -1)
-    right_own_in = along_z(right_own, 1)
-    left_own_in = along_z(left_own, -1)
 
     moved = 10 * LANES * hidden
     block = sds((LANES, hidden), BF)
@@ -306,7 +304,7 @@
         moved=1,
     )(take, returned.reshape(peers * out_rows, LANES))
     grad_gate = call(sum_own, sds((LANES, hidden), F32), "vvvvvu", moved=2 * moved)(
-        kept, right_own_in, left_own_in, right_sum, left_sum, grad_tokens
+        kept, right_in, left_in, right_sum, left_sum, grad_tokens
     )
     return (grad_tokens, grad_gate[None])
 

time: 96 us -> 92.9 us (0.968)
  starting transfers between devices: 64.4 us -> 59.5 us
    ppermute x7 -> x5, starting transfers between devices: 31.9 us -> 27 us  [along_z(): return lax.ppermute(value, 'dp', pairs)]
    ppermute x7 -> x5, waiting for transfers between devices: 10.5 us -> 11.5 us  [along_z(): return lax.ppermute(value, 'dp', pairs)]
  transfers between devices with their start and end apart: 11 -> 9, of which waited for: 4 -> 2; matrix products, arithmetic and copies ran while one was open for 0% -> 0% of each run, Pallas kernels for 16% -> 16%
where the time goes in v9:
time: 92.9 us; the launch traced here: 91 us
  starting transfers between devices  59.5 us (64%)
  Pallas kernels  19.2 us (21%)
  waiting for transfers between devices  11.5 us (12%)
    ppermute x5, starting transfers between devices, along_z(): return lax.ppermute(value, 'dp', pairs)  27 us
    pallas_call x11, Pallas kernels, call(): kernel(*(far(v) if kind in 'hu' else v for kind, v in zip(ins, given)))  14.5 us
    all_to_all x1, starting transfers between devices, on_device(): lax.all_to_all(outgoing.reshape(peers, in_rows, LANES), 'expert', 0, 0, t...  14 us
    ppermute x5, waiting for transfers between devices, along_z(): return lax.ppermute(value, 'dp', pairs)  11.5 us
    ppermute x1, starting transfers between devices, on_device(): borrowed = swap(lent)  6.64 us
    ppermute x1, starting transfers between devices, on_device(): dgate_near = swap(dgate)  6.09 us
    all_to_all x1, starting transfers between devices, on_device(): lax.all_to_all(back.reshape(peers, out_rows, LANES), 'expert', 0, 0, tile...  5.66 us
    pallas_call x1, Pallas kernels, on_device(): pl.pallas_call(factors, grid=(parts,), out_shape=(sds((slot_rows, hidden)...  4.71 us
  transfers between devices with their start and end apart: 9, of which 2 were waited for; matrix products, arithmetic and copies ran while one was open for 0% of the time, Pallas kernels for 16%

profile of v9, /device:TPU:1, one launch (start us, length us, event | category | flops | bytes accessed | tf_op | source)
XLA Modules:
  0.0 91.0 jit_solution(10677268383771854944)
XLA Ops:
  0.6 2.2 %shard_map.68 = (bf16[1536,128]{1,0:T(8,128)(2,1)}, bf16[16,192]{1,0:T(8,128)(2,1)}) custom-call(s32[8,16]{1,0:T(8,128)} %bitcast.29, bf16[128,768]{1,0:T(8,128)(2,1)} %bitcast.28), custom_call_target="tpu_custom_call" | custom-call | flops 37748736 | bytes 786432 | tf_op jit(solution)/shard_map/pallas_call | solution.py:34
  2.8 14.0 %all-to-all-start = ((bf16[64,24,128]{2,1,0:T(8,128)(2,1)}), bf16[64,24,128]{2,1,0:T(8,128)(2,1)S(1)}, u32[]{:S(2)}, u32[]{:S(2)}) async-start(bf16[64,24,128]{2,1,0:T(8,128)(2,1)} %bitcast.26), calls=%async_computation | async-start | bytes 786432 | tf_op jit(solution)/shard_map/all_to_all | solution.py:221
  16.9 0.1 pad_add_fusion.core_ref.spot_ref
  16.9 2.0 %shard_map.69 = bf16[192,1024]{1,0:T(8,128)(2,1)} custom-call(s32[2]{0:T(128)S(1)} %pad_add_fusion.core_ref.spot_ref, bf16[192,2048]{1,0:T(8,128)(2,1)} %bitcast.22), custom_call_target="tpu_custom_call" | custom-call | bytes 786432 | tf_op jit(solution)/shard_map/pallas_call | solution.py:34
  18.9 6.6 %collective-permute-start = (bf16[192,1024]{1,0:T(8,128)(2,1)}, bf16[192,1024]{1,0:T(8,128)(2,1)S(1)}, u32[]{:S(2)}, u32[]{:S(2)}) collective-permute-start(bf16[192,1024]{1,0:T(8,128)(2,1)} %shard_map.69), channel_id=1, source_target_pairs={{0,64},{64,0},{128,192},{192,128},{256,320},{320,256},{384,448},{4... | collective-permute-start | bytes 1179656 | tf_op jit(solution)/shard_map/ppermute | solution.py:225
  25.6 4.7 %shard_map.71 = (f32[192,768]{1,0:T(8,128)S(1)}, f32[192,768]{1,0:T(8,128)S(1)}) custom-call(bf16[192,2048]{1,0:T(8,128)(2,1)} %bitcast.23, bf16[2048,768]{1,0:T(8,128)(2,1)} %bitcast.18, bf16[2048,768]{1,0:T(8,128)(2,1)} %bitcast.20), custom_call_target="tpu_custom_call" | custom-call | flops 1207959552 | bytes 12582912 | tf_op jit(solution)/shard_map/pallas_call | solution.py:227
  30.3 0.0 collective-permute-done.partner_ref
  30.3 1.5 %shard_map.70._.xt_ref = bf16[1024,512]{1,0:T(8,128)(2,1)S(1)} custom-call(s32[2]{0:T(128)S(1)} %pad_add_fusion.core_ref.spot_ref, bf16[192,2048]{1,0:T(8,128)(2,1)} %bitcast.24, bf16[192,1024]{1,0:T(8,128)(2,1)S(1)} %collective-permute-done.partner_ref), custom_call_target="tpu_custom_call" | custom-call | bytes 1572864 | tf_op jit(solution)/shard_map/pallas_call | solution.py:34
  31.8 0.0 all-to-all-done
  31.8 0.3 shard_map.72
  32.1 6.1 %collective-permute-start.1 = (bf16[192,768]{1,0:T(8,128)(2,1)S(1)}, bf16[192,768]{1,0:T(8,128)(2,1)S(1)}, u32[]{:S(2)}, u32[]{:S(2)}) collective-permute-start(bf16[192,768]{1,0:T(8,128)(2,1)S(1)} %get-tuple-element.17.refs_0_.own_ref), channel_id=1, source_target_pairs={{0,64},{64,0},{128,192},{192,128},{256,320},{320,256},{384,448},{4... | collective-permute-start | bytes 884744 | tf_op jit(solution)/shard_map/ppermute | solution.py:259
  38.2 5.3 %shard_map.73._ = bf16[3072,128]{1,0:T(8,128)(2,1)} custom-call(bf16[192,768]{1,0:T(8,128)(2,1)S(1)} %get-tuple-element.17.refs_0_.own_ref, bf16[192,768]{1,0:T(8,128)(2,1)S(1)} %get-tuple-element.18.refs_1_, bf16[2048,768]{1,0:T(8,128)(2,1)} %bitcast.19, bf16[2048,768]{1,0:T(8,128)(2,1)} %bitcast.21), custom_call_target="tpu_custom_call" | custom-call | flops 1 | bytes 1 | tf_op jit(solution)/shard_map/pallas_call | solution.py:34
  43.5 0.0 collective-permute-done.1.near_ref
  43.5 1.0 %shard_map.74 = (bf16[128,768]{1,0:T(8,128)(2,1)S(1)}, bf16[256,768]{1,0:T(8,128)(2,1)S(1)}, bf16[256,768]{1,0:T(8,128)(2,1)S(1)}, bf16[384,768]{1,0:T(8,128)(2,1)S(1)}, bf16[3072,128]{1,0:T(8,128)(2,1)}) custom-call(bf16[1024,512]{1,0:T(8,128)(2,1)S(1)} %shard_map.70._.xt_ref, ...), custom_call_target="tpu_custom_call", output_to_operand_aliasing={{4}: (3, {})} | custom-call | flops 1 | bytes 1 | tf_op jit(solution)/shard_map/pallas_call | solution.py:34
  44.5 14.9 %collective-permute-start.4 = (bf16[128,768]{1,0:T(8,128)(2,1)S(1)}, bf16[128,768]{1,0:T(8,128)(2,1)S(1)}, u32[]{:S(2)}, u32[]{:S(2)}) collective-permute-start(bf16[128,768]{1,0:T(8,128)(2,1)S(1)} %get-tuple-element.23), channel_id=1, source_target_pairs={{0,256},{64,832},{128,384},{192,960},{256,512},{320,64},{384,640},... | collective-permute-start | bytes 589832 | tf_op jit(solution)/shard_map/ppermute | solution.py:208
  59.5 5.7 %all-to-all-start.1 = ((bf16[64,48,128]{2,1,0:T(8,128)(2,1)}), bf16[64,48,128]{2,1,0:T(8,128)(2,1)S(1)}, u32[]{:S(2)}, u32[]{:S(2)}) async-start(bf16[64,48,128]{2,1,0:T(8,128)(2,1)} %bitcast.25), calls=%async_computation.1 | async-start | bytes 1572864 | tf_op jit(solution)/shard_map/all_to_all | solution.py:285
  65.1 2.8 %collective-permute-start.2 = (bf16[256,768]{1,0:T(8,128)(2,1)S(1)}, bf16[256,768]{1,0:T(8,128)(2,1)S(1)}, u32[]{:S(2)}, u32[]{:S(2)}) collective-permute-start(bf16[256,768]{1,0:T(8,128)(2,1)S(1)} %get-tuple-element.21), channel_id=1, source_target_pairs={{0,128},{64,960},{128,256},{192,64},{256,384},{320,192},{384,512},... | collective-permute-start | bytes 1179656 | tf_op jit(solution)/shard_map/ppermute | solution.py:208
  68.0 3.1 %collective-permute-start.3 = (bf16[256,768]{1,0:T(8,128)(2,1)S(1)}, bf16[256,768]{1,0:T(8,128)(2,1)S(1)}, u32[]{:S(2)}, u32[]{:S(2)}) collective-permute-start(bf16[256,768]{1,0:T(8,128)(2,1)S(1)} %get-tuple-element.22), channel_id=1, source_target_pairs={{0,896},{64,192},{128,0},{192,320},{256,128},{320,448},{384,256},{... | collective-permute-start | bytes 1179656 | tf_op jit(solution)/shard_map/ppermute | solution.py:208
  71.1 0.0 collective-permute-done.4.most_ref
  71.1 0.0 copy-start
  71.2 7.6 %collective-permute-done.2.right_ref = bf16[256,768]{1,0:T(8,128)(2,1)S(1)} collective-permute-done((bf16[256,768]{1,0:T(8,128)(2,1)S(1)}, bf16[256,768]{1,0:T(8,128)(2,1)S(1)}, u32[]{:S(2)}, u32[]{:S(2)}) %collective-permute-start.2) | collective-permute-done | bytes 393248 | tf_op jit(solution)/shard_map/ppermute | solution.py:208
  78.8 1.9 %collective-permute-start.5 = (bf16[128,768]{1,0:T(8,128)(2,1)S(1)}, bf16[128,768]{1,0:T(8,128)(2,1)S(1)}, u32[]{:S(2)}, u32[]{:S(2)}) collective-permute-start(bf16[128,768]{1,0:T(8,128)(2,1)S(1)} %shard_map.77), channel_id=1, source_target_pairs={{0,256},{64,832},{128,384},{192,960},{256,512},{320,64},{384,640},... | collective-permute-start | bytes 589832 | tf_op jit(solution)/shard_map/ppermute | solution.py:208
  80.7 0.0 collective-permute-done.3.left_ref
  80.8 4.3 %collective-permute-start.6 = (bf16[128,768]{1,0:T(8,128)(2,1)S(1)}, bf16[128,768]{1,0:T(8,128)(2,1)S(1)}, u32[]{:S(2)}, u32[]{:S(2)}) collective-permute-start(bf16[128,768]{1,0:T(8,128)(2,1)S(1)} %shard_map.78), channel_id=1, source_target_pairs={{0,768},{64,320},{128,896},{192,448},{256,0},{320,576},{384,128},{... | collective-permute-start | bytes 589832 | tf_op jit(solution)/shard_map/ppermute | solution.py:208
  85.1 0.0 all-to-all-done.1
  85.1 0.0 copy-done
  85.1 1.3 %shard_map.75._ = bf16[16,2048]{1,0:T(8,128)(2,1)} custom-call(bf16[16,192]{1,0:T(8,128)(2,1)S(1)} %copy-done, bf16[3072,128]{1,0:T(8,128)(2,1)S(1)} %bitcast.16), custom_call_target="tpu_custom_call" | custom-call | flops 1 | bytes 1 | tf_op jit(solution)/shard_map/pallas_call | solution.py:34
  86.3 3.8 %collective-permute-done.5.right_sum_ref = bf16[128,768]{1,0:T(8,128)(2,1)S(1)} collective-permute-done((bf16[128,768]{1,0:T(8,128)(2,1)S(1)}, bf16[128,768]{1,0:T(8,128)(2,1)S(1)}, u32[]{:S(2)}, u32[]{:S(2)}) %collective-permute-start.5) | collective-permute-done | bytes 196640 | tf_op jit(solution)/shard_map/ppermute | solution.py:208
  90.2 0.0 collective-permute-done.6.left_sum_ref
  90.2 0.9 shard_map.79
  (3 shorter events, 0.1 us)
Async XLA Ops:
  2.8 29.0 %all-to-all-start = ((bf16[64,24,128]{2,1,0:T(8,128)(2,1)}), bf16[64,24,128]{2,1,0:T(8,128)(2,1)S(1)}, u32[]{:S(2)}, u32[]{:S(2)}) async-start(bf16[64,24,128]{2,1,0:T(8,128)(2,1)} %bitcast.26), calls=%async_computation | async-start | bytes 786432 | tf_op jit(solution)/shard_map/all_to_all | solution.py:221
  18.9 11.4 %collective-permute-start = (bf16[192,1024]{1,0:T(8,128)(2,1)}, bf16[192,1024]{1,0:T(8,128)(2,1)S(1)}, u32[]{:S(2)}, u32[]{:S(2)}) collective-permute-start(bf16[192,1024]{1,0:T(8,128)(2,1)} %shard_map.69), channel_id=1, source_target_pairs={{0,64},{64,0},{128,192},{192,128},{256,320},{320,256},{384,448},{4... | collective-permute-start | bytes 1179656 | tf_op jit(solution)/shard_map/ppermute | solution.py:225
  32.1 11.4 %collective-permute-start.1 = (bf16[192,768]{1,0:T(8,128)(2,1)S(1)}, bf16[192,768]{1,0:T(8,128)(2,1)S(1)}, u32[]{:S(2)}, u32[]{:S(2)}) collective-permute-start(bf16[192,768]{1,0:T(8,128)(2,1)S(1)} %get-tuple-element.17.refs_0_.own_ref), channel_id=1, source_target_pairs={{0,64},{64,0},{128,192},{192,128},{256,320},{320,256},{384,448},{4... | collective-permute-start | bytes 884744 | tf_op jit(solution)/shard_map/ppermute | solution.py:259
  44.5 26.5 %collective-permute-start.4 = (bf16[128,768]{1,0:T(8,128)(2,1)S(1)}, bf16[128,768]{1,0:T(8,128)(2,1)S(1)}, u32[]{:S(2)}, u32[]{:S(2)}) collective-permute-start(bf16[128,768]{1,0:T(8,128)(2,1)S(1)} %get-tuple-element.23), channel_id=1, source_target_pairs={{0,256},{64,832},{128,384},{192,960},{256,512},{320,64},{384,640},... | collective-permute-start | bytes 589832 | tf_op jit(solution)/shard_map/ppermute | solution.py:208
  59.5 25.6 %all-to-all-start.1 = ((bf16[64,48,128]{2,1,0:T(8,128)(2,1)}), bf16[64,48,128]{2,1,0:T(8,128)(2,1)S(1)}, u32[]{:S(2)}, u32[]{:S(2)}) async-start(bf16[64,48,128]{2,1,0:T(8,128)(2,1)} %bitcast.25), calls=%async_computation.1 | async-start | bytes 1572864 | tf_op jit(solution)/shard_map/all_to_all | solution.py:285
  65.1 13.6 %collective-permute-start.2 = (bf16[256,768]{1,0:T(8,128)(2,1)S(1)}, bf16[256,768]{1,0:T(8,128)(2,1)S(1)}, u32[]{:S(2)}, u32[]{:S(2)}) collective-permute-start(bf16[256,768]{1,0:T(8,128)(2,1)S(1)} %get-tuple-element.21), channel_id=1, source_target_pairs={{0,128},{64,960},{128,256},{192,64},{256,384},{320,192},{384,512},... | collective-permute-start | bytes 1179656 | tf_op jit(solution)/shard_map/ppermute | solution.py:208
  68.0 12.7 %collective-permute-start.3 = (bf16[256,768]{1,0:T(8,128)(2,1)S(1)}, bf16[256,768]{1,0:T(8,128)(2,1)S(1)}, u32[]{:S(2)}, u32[]{:S(2)}) collective-permute-start(bf16[256,768]{1,0:T(8,128)(2,1)S(1)} %get-tuple-element.22), channel_id=1, source_target_pairs={{0,896},{64,192},{128,0},{192,320},{256,128},{320,448},{384,256},{... | collective-permute-start | bytes 1179656 | tf_op jit(solution)/shard_map/ppermute | solution.py:208
  71.1 13.9 %copy-start = (bf16[16,192]{1,0:T(8,128)(2,1)S(1)}, bf16[16,192]{1,0:T(8,128)(2,1)}, u32[]{:S(2)}) copy-start(bf16[16,192]{1,0:T(8,128)(2,1)} %get-tuple-element.13.take_ref) | copy-start | bytes 18436
  78.8 11.4 %collective-permute-start.5 = (bf16[128,768]{1,0:T(8,128)(2,1)S(1)}, bf16[128,768]{1,0:T(8,128)(2,1)S(1)}, u32[]{:S(2)}, u32[]{:S(2)}) collective-permute-start(bf16[128,768]{1,0:T(8,128)(2,1)S(1)} %shard_map.77), channel_id=1, source_target_pairs={{0,256},{64,832},{128,384},{192,960},{256,512},{320,64},{384,640},... | collective-permute-start | bytes 589832 | tf_op jit(solution)/shard_map/ppermute | solution.py:208
  80.8 9.4 %collective-permute-start.6 = (bf16[128,768]{1,0:T(8,128)(2,1)S(1)}, bf16[128,768]{1,0:T(8,128)(2,1)S(1)}, u32[]{:S(2)}, u32[]{:S(2)}) collective-permute-start(bf16[128,768]{1,0:T(8,128)(2,1)S(1)} %shard_map.78), channel_id=1, source_target_pairs={{0,768},{64,320},{128,896},{192,448},{256,0},{320,576},{384,128},{... | collective-permute-start | bytes 589832 | tf_op jit(solution)/shard_map/ppermute | solution.py:208

commit v10 on v9

--- a/solution.py
+++ b/solution.py
@@ -158,7 +158,7 @@
 
 
 def sum_right(part_ref, right_ref, out_ref):
-    out_ref[...] = (part_ref[...] + right_ref[:LANES].astype(F32)).astype(BF)
+    out_ref[...] = (part_ref[...] + right_ref[...].astype(F32)).astype(BF)
 
 
 def sum_left(kept_ref, left_ref, out_ref):
@@ -166,7 +166,7 @@
 
 
 def sum_own(kept_ref, right_ref, left_ref, right_sum_ref, left_sum_ref, _, out_ref):
-    near_sum = right_ref[LANES:].astype(F32) + left_ref[LANES:].astype(F32)
+    near_sum = right_ref[...].astype(F32) + left_ref[LANES:].astype(F32)
     far_sum = right_sum_ref[...].astype(F32) + left_sum_ref[...].astype(F32)
     out_ref[...] = kept_ref[2 * LANES :].astype(F32) + near_sum + far_sum
 
@@ -182,7 +182,7 @@
         out_ref[:, c * LANES : (c + 1) * LANES] = total.astype(BF)
 
 
-ROLES = (4, 3, 1, -3, -1, 2, -2, 0)
+ROLES = (4, 3, -3, -1, 1, 2, -2, 0)
 
 
 def on_device(expert_ids, grad_hidden, stored_inputs, gate_weight, up_weight):
@@ -272,8 +272,8 @@
         flops=1,
         moved=1,
     )(dgate, dup, w_gate, w_up)
-    blocks = [sds((n * LANES, hidden), BF) for n in (1, 2, 2, 3)]
-    most, right, left, kept, back = call(
+    blocks = [sds((n * LANES, hidden), BF) for n in (1, 1, 2, 1, 3)]
+    most, right, left, right_own, kept, back = call(
         partials,
         blocks + [pltpu.HBM(back.shape, BF)],
         "vvvu",
@@ -287,6 +287,7 @@
     most_in = along_z(most, 2)
     right_in = along_z(right, 1)
     left_in = along_z(left, -1)
+    right_own_in = along_z(right_own, 1)
 
     moved = 10 * LANES * hidden
     block = sds((LANES, hidden), BF)
@@ -304,7 +305,7 @@
         moved=1,
     )(take, returned.reshape(peers * out_rows, LANES))
     grad_gate = call(sum_own, sds((LANES, hidden), F32), "vvvvvu", moved=2 * moved)(
-        kept, right_in, left_in, right_sum, left_sum, grad_tokens
+        kept, right_own_in, left_in, right_sum, left_sum, grad_tokens
     )
     return (grad_tokens, grad_gate[None])
 

time: 92.9 us -> 95 us (1.023)
  starting transfers between devices: 59.5 us -> 60.7 us
    ppermute x5 -> x6, starting transfers between devices: 27 us -> 28.3 us  [along_z(): return lax.ppermute(value, 'dp', pairs)]
    ppermute x5 -> x6, waiting for transfers between devices: 11.5 us -> 12.3 us  [along_z(): return lax.ppermute(value, 'dp', pairs)]
  transfers between devices with their start and end apart: 9 -> 10, of which waited for: 2 -> 4; matrix products, arithmetic and copies ran while one was open for 0% -> 0% of each run, Pallas kernels for 16% -> 16%
where the time goes in v10:
time: 95 us; the launch traced here: 93.2 us
  starting transfers between devices  60.7 us (64%)
  Pallas kernels  19.2 us (20%)
  waiting for transfers between devices  12.4 us (13%)
    ppermute x6, starting transfers between devices, along_z(): return lax.ppermute(value, 'dp', pairs)  28.3 us
    pallas_call x11, Pallas kernels, call(): kernel(*(far(v) if kind in 'hu' else v for kind, v in zip(ins, given)))  14.5 us
    all_to_all x1, starting transfers between devices, on_device(): lax.all_to_all(outgoing.reshape(peers, in_rows, LANES), 'expert', 0, 0, t...  14 us
    ppermute x6, waiting for transfers between devices, along_z(): return lax.ppermute(value, 'dp', pairs)  12.3 us
    ppermute x1, starting transfers between devices, on_device(): borrowed = swap(lent)  6.64 us
    ppermute x1, starting transfers between devices, on_device(): dgate_near = swap(dgate)  6.08 us
    all_to_all x1, starting transfers between devices, on_device(): lax.all_to_all(back.reshape(peers, out_rows, LANES), 'expert', 0, 0, tile...  5.67 us
    pallas_call x1, Pallas kernels, on_device(): pl.pallas_call(factors, grid=(parts,), out_shape=(sds((slot_rows, hidden)...  4.71 us
  transfers between devices with their start and end apart: 10, of which 4 were waited for; matrix products, arithmetic and copies ran while one was open for 0% of the time, Pallas kernels for 16%

profile of v10, /device:TPU:1, one launch (start us, length us, event | category | flops | bytes accessed | tf_op | source)
XLA Modules:
  0.0 93.2 jit_solution(3778887482079233)
XLA Ops:
  0.6 2.2 %shard_map.68 = (bf16[1536,128]{1,0:T(8,128)(2,1)}, bf16[16,192]{1,0:T(8,128)(2,1)}) custom-call(s32[8,16]{1,0:T(8,128)} %bitcast.29, bf16[128,768]{1,0:T(8,128)(2,1)} %bitcast.28), custom_call_target="tpu_custom_call" | custom-call | flops 37748736 | bytes 786432 | tf_op jit(solution)/shard_map/pallas_call | solution.py:34
  2.8 14.0 %all-to-all-start = ((bf16[64,24,128]{2,1,0:T(8,128)(2,1)}), bf16[64,24,128]{2,1,0:T(8,128)(2,1)S(1)}, u32[]{:S(2)}, u32[]{:S(2)}) async-start(bf16[64,24,128]{2,1,0:T(8,128)(2,1)} %bitcast.26), calls=%async_computation | async-start | bytes 786432 | tf_op jit(solution)/shard_map/all_to_all | solution.py:221
  16.9 0.1 pad_add_fusion.core_ref.spot_ref
  16.9 2.0 %shard_map.69 = bf16[192,1024]{1,0:T(8,128)(2,1)} custom-call(s32[2]{0:T(128)S(1)} %pad_add_fusion.core_ref.spot_ref, bf16[192,2048]{1,0:T(8,128)(2,1)} %bitcast.22), custom_call_target="tpu_custom_call" | custom-call | bytes 786432 | tf_op jit(solution)/shard_map/pallas_call | solution.py:34
  19.0 6.6 %collective-permute-start = (bf16[192,1024]{1,0:T(8,128)(2,1)}, bf16[192,1024]{1,0:T(8,128)(2,1)S(1)}, u32[]{:S(2)}, u32[]{:S(2)}) collective-permute-start(bf16[192,1024]{1,0:T(8,128)(2,1)} %shard_map.69), channel_id=1, source_target_pairs={{0,64},{64,0},{128,192},{192,128},{256,320},{320,256},{384,448},{4... | collective-permute-start | bytes 1179656 | tf_op jit(solution)/shard_map/ppermute | solution.py:225
  25.6 4.7 %shard_map.71 = (f32[192,768]{1,0:T(8,128)S(1)}, f32[192,768]{1,0:T(8,128)S(1)}) custom-call(bf16[192,2048]{1,0:T(8,128)(2,1)} %bitcast.23, bf16[2048,768]{1,0:T(8,128)(2,1)} %bitcast.18, bf16[2048,768]{1,0:T(8,128)(2,1)} %bitcast.20), custom_call_target="tpu_custom_call" | custom-call | flops 1207959552 | bytes 12582912 | tf_op jit(solution)/shard_map/pallas_call | solution.py:227
  30.3 0.0 collective-permute-done.partner_ref
  30.3 1.5 %shard_map.70._.xt_ref = bf16[1024,512]{1,0:T(8,128)(2,1)S(1)} custom-call(s32[2]{0:T(128)S(1)} %pad_add_fusion.core_ref.spot_ref, bf16[192,2048]{1,0:T(8,128)(2,1)} %bitcast.24, bf16[192,1024]{1,0:T(8,128)(2,1)S(1)} %collective-permute-done.partner_ref), custom_call_target="tpu_custom_call" | custom-call | bytes 1572864 | tf_op jit(solution)/shard_map/pallas_call | solution.py:34
  31.8 0.0 all-to-all-done
  31.8 0.3 shard_map.72
  32.1 6.1 %collective-permute-start.1 = (bf16[192,768]{1,0:T(8,128)(2,1)S(1)}, bf16[192,768]{1,0:T(8,128)(2,1)S(1)}, u32[]{:S(2)}, u32[]{:S(2)}) collective-permute-start(bf16[192,768]{1,0:T(8,128)(2,1)S(1)} %get-tuple-element.18.refs_0_.own_ref), channel_id=1, source_target_pairs={{0,64},{64,0},{128,192},{192,128},{256,320},{320,256},{384,448},{4... | collective-permute-start | bytes 884744 | tf_op jit(solution)/shard_map/ppermute | solution.py:259
  38.2 5.3 %shard_map.73._ = bf16[3072,128]{1,0:T(8,128)(2,1)} custom-call(bf16[192,768]{1,0:T(8,128)(2,1)S(1)} %get-tuple-element.18.refs_0_.own_ref, bf16[192,768]{1,0:T(8,128)(2,1)S(1)} %get-tuple-element.19.refs_1_, bf16[2048,768]{1,0:T(8,128)(2,1)} %bitcast.19, bf16[2048,768]{1,0:T(8,128)(2,1)} %bitcast.21), custom_call_target="tpu_custom_call" | custom-call | flops 1 | bytes 1 | tf_op jit(solution)/shard_map/pallas_call | solution.py:34
  43.5 0.0 collective-permute-done.1.near_ref
  43.5 1.0 %shard_map.74 = (bf16[128,768]{1,0:T(8,128)(2,1)S(1)}, bf16[128,768]{1,0:T(8,128)(2,1)S(1)}, bf16[256,768]{1,0:T(8,128)(2,1)S(1)}, bf16[128,768]{1,0:T(8,128)(2,...) custom-call(bf16[1024,512]{1,0:T(8,128)(2,1)S(1)} %shard_map.70._.xt_ref, ...), custom_call_target="tpu_custom_call", output_to_operand_aliasing={{5}: (3, {})} | custom-call | flops 1 | bytes 1 | tf_op jit(solution)/shard_map/pallas_call | solution.py:34
  44.5 14.9 %collective-permute-start.4 = (bf16[128,768]{1,0:T(8,128)(2,1)S(1)}, bf16[128,768]{1,0:T(8,128)(2,1)S(1)}, u32[]{:S(2)}, u32[]{:S(2)}) collective-permute-start(bf16[128,768]{1,0:T(8,128)(2,1)S(1)} %get-tuple-element.24), channel_id=1, source_target_pairs={{0,256},{64,832},{128,384},{192,960},{256,512},{320,64},{384,640},... | collective-permute-start | bytes 589832 | tf_op jit(solution)/shard_map/ppermute | solution.py:208
  59.5 5.7 %all-to-all-start.1 = ((bf16[64,48,128]{2,1,0:T(8,128)(2,1)}), bf16[64,48,128]{2,1,0:T(8,128)(2,1)S(1)}, u32[]{:S(2)}, u32[]{:S(2)}) async-start(bf16[64,48,128]{2,1,0:T(8,128)(2,1)} %bitcast.25), calls=%async_computation.1 | async-start | bytes 1572864 | tf_op jit(solution)/shard_map/all_to_all | solution.py:285
  65.1 2.8 %collective-permute-start.2 = (bf16[128,768]{1,0:T(8,128)(2,1)S(1)}, bf16[128,768]{1,0:T(8,128)(2,1)S(1)}, u32[]{:S(2)}, u32[]{:S(2)}) collective-permute-start(bf16[128,768]{1,0:T(8,128)(2,1)S(1)} %get-tuple-element.22), channel_id=1, source_target_pairs={{0,128},{64,960},{128,256},{192,64},{256,384},{320,192},{384,512},... | collective-permute-start | bytes 589832 | tf_op jit(solution)/shard_map/ppermute | solution.py:208
  68.0 1.9 %collective-permute-start.5 = (bf16[128,768]{1,0:T(8,128)(2,1)S(1)}, bf16[128,768]{1,0:T(8,128)(2,1)S(1)}, u32[]{:S(2)}, u32[]{:S(2)}) collective-permute-start(bf16[128,768]{1,0:T(8,128)(2,1)S(1)} %get-tuple-element.25), channel_id=1, source_target_pairs={{0,128},{64,960},{128,256},{192,64},{256,384},{320,192},{384,512},... | collective-permute-start | bytes 589832 | tf_op jit(solution)/shard_map/ppermute | solution.py:208
  69.9 3.4 %collective-permute-start.3 = (bf16[256,768]{1,0:T(8,128)(2,1)S(1)}, bf16[256,768]{1,0:T(8,128)(2,1)S(1)}, u32[]{:S(2)}, u32[]{:S(2)}) collective-permute-start(bf16[256,768]{1,0:T(8,128)(2,1)S(1)} %get-tuple-element.23), channel_id=1, source_target_pairs={{0,896},{64,192},{128,0},{192,320},{256,128},{320,448},{384,256},{... | collective-permute-start | bytes 1179656 | tf_op jit(solution)/shard_map/ppermute | solution.py:208
  73.3 0.0 collective-permute-done.4.most_ref
  73.3 0.0 copy-start
  73.4 1.3 %collective-permute-done.5.right_ref = bf16[128,768]{1,0:T(8,128)(2,1)S(1)} collective-permute-done((bf16[128,768]{1,0:T(8,128)(2,1)S(1)}, bf16[128,768]{1,0:T(8,128)(2,1)S(1)}, u32[]{:S(2)}, u32[]{:S(2)}) %collective-permute-start.5) | collective-permute-done | bytes 196640 | tf_op jit(solution)/shard_map/ppermute | solution.py:208
  74.7 1.9 %collective-permute-start.6 = (bf16[128,768]{1,0:T(8,128)(2,1)S(1)}, bf16[128,768]{1,0:T(8,128)(2,1)S(1)}, u32[]{:S(2)}, u32[]{:S(2)}) collective-permute-start(bf16[128,768]{1,0:T(8,128)(2,1)S(1)} %shard_map.77), channel_id=1, source_target_pairs={{0,256},{64,832},{128,384},{192,960},{256,512},{320,64},{384,640},... | collective-permute-start | bytes 589832 | tf_op jit(solution)/shard_map/ppermute | solution.py:208
  76.7 3.0 %collective-permute-done.3.left_ref = bf16[256,768]{1,0:T(8,128)(2,1)S(1)} collective-permute-done((bf16[256,768]{1,0:T(8,128)(2,1)S(1)}, bf16[256,768]{1,0:T(8,128)(2,1)S(1)}, u32[]{:S(2)}, u32[]{:S(2)}) %collective-permute-start.3) | collective-permute-done | bytes 393248 | tf_op jit(solution)/shard_map/ppermute | solution.py:208
  79.7 3.3 %collective-permute-start.7 = (bf16[128,768]{1,0:T(8,128)(2,1)S(1)}, bf16[128,768]{1,0:T(8,128)(2,1)S(1)}, u32[]{:S(2)}, u32[]{:S(2)}) collective-permute-start(bf16[128,768]{1,0:T(8,128)(2,1)S(1)} %shard_map.78), channel_id=1, source_target_pairs={{0,768},{64,320},{128,896},{192,448},{256,0},{320,576},{384,128},{... | collective-permute-start | bytes 589832 | tf_op jit(solution)/shard_map/ppermute | solution.py:208
  83.0 0.0 all-to-all-done.1
  83.1 0.0 copy-done
  83.1 1.3 %shard_map.75._ = bf16[16,2048]{1,0:T(8,128)(2,1)} custom-call(bf16[16,192]{1,0:T(8,128)(2,1)S(1)} %copy-done, bf16[3072,128]{1,0:T(8,128)(2,1)S(1)} %bitcast.16), custom_call_target="tpu_custom_call" | custom-call | flops 1 | bytes 1 | tf_op jit(solution)/shard_map/pallas_call | solution.py:34
  84.3 0.0 collective-permute-done.2.right_ref
  84.3 0.1 collective-permute-done.6.right_sum_ref
  84.4 7.9 %collective-permute-done.7.left_sum_ref = bf16[128,768]{1,0:T(8,128)(2,1)S(1)} collective-permute-done((bf16[128,768]{1,0:T(8,128)(2,1)S(1)}, bf16[128,768]{1,0:T(8,128)(2,1)S(1)}, u32[]{:S(2)}, u32[]{:S(2)}) %collective-permute-start.7) | collective-permute-done | bytes 196640 | tf_op jit(solution)/shard_map/ppermute | solution.py:208
  92.4 0.9 shard_map.79
  (3 shorter events, 0.1 us)
Async XLA Ops:
  2.8 29.0 %all-to-all-start = ((bf16[64,24,128]{2,1,0:T(8,128)(2,1)}), bf16[64,24,128]{2,1,0:T(8,128)(2,1)S(1)}, u32[]{:S(2)}, u32[]{:S(2)}) async-start(bf16[64,24,128]{2,1,0:T(8,128)(2,1)} %bitcast.26), calls=%async_computation | async-start | bytes 786432 | tf_op jit(solution)/shard_map/all_to_all | solution.py:221
  19.0 11.4 %collective-permute-start = (bf16[192,1024]{1,0:T(8,128)(2,1)}, bf16[192,1024]{1,0:T(8,128)(2,1)S(1)}, u32[]{:S(2)}, u32[]{:S(2)}) collective-permute-start(bf16[192,1024]{1,0:T(8,128)(2,1)} %shard_map.69), channel_id=1, source_target_pairs={{0,64},{64,0},{128,192},{192,128},{256,320},{320,256},{384,448},{4... | collective-permute-start | bytes 1179656 | tf_op jit(solution)/shard_map/ppermute | solution.py:225
  32.1 11.4 %collective-permute-start.1 = (bf16[192,768]{1,0:T(8,128)(2,1)S(1)}, bf16[192,768]{1,0:T(8,128)(2,1)S(1)}, u32[]{:S(2)}, u32[]{:S(2)}) collective-permute-start(bf16[192,768]{1,0:T(8,128)(2,1)S(1)} %get-tuple-element.18.refs_0_.own_ref), channel_id=1, source_target_pairs={{0,64},{64,0},{128,192},{192,128},{256,320},{320,256},{384,448},{4... | collective-permute-start | bytes 884744 | tf_op jit(solution)/shard_map/ppermute | solution.py:259
  44.5 28.8 %collective-permute-start.4 = (bf16[128,768]{1,0:T(8,128)(2,1)S(1)}, bf16[128,768]{1,0:T(8,128)(2,1)S(1)}, u32[]{:S(2)}, u32[]{:S(2)}) collective-permute-start(bf16[128,768]{1,0:T(8,128)(2,1)S(1)} %get-tuple-element.24), channel_id=1, source_target_pairs={{0,256},{64,832},{128,384},{192,960},{256,512},{320,64},{384,640},... | collective-permute-start | bytes 589832 | tf_op jit(solution)/shard_map/ppermute | solution.py:208
  59.5 23.6 %all-to-all-start.1 = ((bf16[64,48,128]{2,1,0:T(8,128)(2,1)}), bf16[64,48,128]{2,1,0:T(8,128)(2,1)S(1)}, u32[]{:S(2)}, u32[]{:S(2)}) async-start(bf16[64,48,128]{2,1,0:T(8,128)(2,1)} %bitcast.25), calls=%async_computation.1 | async-start | bytes 1572864 | tf_op jit(solution)/shard_map/all_to_all | solution.py:285
  65.1 19.2 %collective-permute-start.2 = (bf16[128,768]{1,0:T(8,128)(2,1)S(1)}, bf16[128,768]{1,0:T(8,128)(2,1)S(1)}, u32[]{:S(2)}, u32[]{:S(2)}) collective-permute-start(bf16[128,768]{1,0:T(8,128)(2,1)S(1)} %get-tuple-element.22), channel_id=1, source_target_pairs={{0,128},{64,960},{128,256},{192,64},{256,384},{320,192},{384,512},... | collective-permute-start | bytes 589832 | tf_op jit(solution)/shard_map/ppermute | solution.py:208
  68.0 6.7 %collective-permute-start.5 = (bf16[128,768]{1,0:T(8,128)(2,1)S(1)}, bf16[128,768]{1,0:T(8,128)(2,1)S(1)}, u32[]{:S(2)}, u32[]{:S(2)}) collective-permute-start(bf16[128,768]{1,0:T(8,128)(2,1)S(1)} %get-tuple-element.25), channel_id=1, source_target_pairs={{0,128},{64,960},{128,256},{192,64},{256,384},{320,192},{384,512},... | collective-permute-start | bytes 589832 | tf_op jit(solution)/shard_map/ppermute | solution.py:208
  69.9 9.7 %collective-permute-start.3 = (bf16[256,768]{1,0:T(8,128)(2,1)S(1)}, bf16[256,768]{1,0:T(8,128)(2,1)S(1)}, u32[]{:S(2)}, u32[]{:S(2)}) collective-permute-start(bf16[256,768]{1,0:T(8,128)(2,1)S(1)} %get-tuple-element.23), channel_id=1, source_target_pairs={{0,896},{64,192},{128,0},{192,320},{256,128},{320,448},{384,256},{... | collective-permute-start | bytes 1179656 | tf_op jit(solution)/shard_map/ppermute | solution.py:208
  73.3 9.7 %copy-start = (bf16[16,192]{1,0:T(8,128)(2,1)S(1)}, bf16[16,192]{1,0:T(8,128)(2,1)}, u32[]{:S(2)}) copy-start(bf16[16,192]{1,0:T(8,128)(2,1)} %get-tuple-element.14.take_ref) | copy-start | bytes 18436
  74.7 9.7 %collective-permute-start.6 = (bf16[128,768]{1,0:T(8,128)(2,1)S(1)}, bf16[128,768]{1,0:T(8,128)(2,1)S(1)}, u32[]{:S(2)}, u32[]{:S(2)}) collective-permute-start(bf16[128,768]{1,0:T(8,128)(2,1)S(1)} %shard_map.77), channel_id=1, source_target_pairs={{0,256},{64,832},{128,384},{192,960},{256,512},{320,64},{384,640},... | collective-permute-start | bytes 589832 | tf_op jit(solution)/shard_map/ppermute | solution.py:208
  79.7 12.7 %collective-permute-start.7 = (bf16[128,768]{1,0:T(8,128)(2,1)S(1)}, bf16[128,768]{1,0:T(8,128)(2,1)S(1)}, u32[]{:S(2)}, u32[]{:S(2)}) collective-permute-start(bf16[128,768]{1,0:T(8,128)(2,1)S(1)} %shard_map.78), channel_id=1, source_target_pairs={{0,768},{64,320},{128,896},{192,448},{256,0},{320,576},{384,128},{... | collective-permute-start | bytes 589832 | tf_op jit(solution)/shard_map/ppermute | solution.py:208
